TPU v7x, 512 devices: a whole 4x4x16 slice. The times are simulated.
512 devices in a mesh: outer: 16 (over x, z_hi, core), inner: 32 (over y, z_lo).
Axes of the slice: x: 4, y: 4, z: 16 (z_hi: 2, z_lo: 8; z = z_hi * 8 + z_lo), core: 2. Of those that a mesh axis runs over, the one named last changes fastest.
Arguments:
- queries: bfloat16 [65536, 1024], P(('outer', 'inner')), may hold values from -24 to 24
- keys: bfloat16 [65536, 128], P(('outer', 'inner')), may hold values from -4 to 4
- values: bfloat16 [65536, 128], P(('outer', 'inner')), may hold values from -6 to 6
- grad_out: bfloat16 [65536, 1024], P(('outer', 'inner')), may hold values from -24 to 24
- doc_ids: int32 [512], replicated, may hold values from 0 to 23, never falling along the last dimension, each value on 1 to 32 neighbouring positions
- block_order: int32 [512], replicated, may hold values from 0 to 511, as said below
Outputs:
- grad_queries: bfloat16 [65536, 1024], P(('outer', 'inner'))
- grad_keys: bfloat16 [65536, 128], P(('outer', 'inner'))
- grad_values: bfloat16 [65536, 128], P(('outer', 'inner'))
Inputs may be any that keep to these rules, and one draw needn't show every extreme that they name: `doc_ids`: never falling along the sequence; each document spans 1 to 32 blocks and one spans exactly 32. Stored block s holds sequence block block_order[s]; the stored blocks of each aligned run of 32 (those of one index of outer) hold a permutation of the same run of sequence blocks.
All inputs are finite; a program needn't handle non-finite values.
Results may differ from a plain program's by a relative error of at most 0.022.
Values may be sent and summed in bfloat16 or wider, within the bound.
No kernel may reach another device: no remote copies, remote signals or barrier semaphores. Data moves between devices by JAX's collectives and lax.ppermute only.
A program may use at most 64 MiB of HBM per device.

v0:
```python
import jax
import jax.numpy as jnp
from jax import lax
from jax.sharding import PartitionSpec as P

BLOCK = 128
TILE_BLOCKS = 4


NEG = -1e30


def from_behind(array, axis, by):
    count = lax.axis_size(axis)
    pairs = [(i, i + by) for i in range(count) if 0 <= i + by < count]
    return lax.ppermute(array, axis, pairs)


def block_visibility(tile_docs, my_doc, start_block, own_block):
    count = tile_docs.shape[0]
    blocks = start_block + jnp.arange(count, dtype=jnp.int32)
    matches = tile_docs == my_doc
    query_offset = jnp.arange(BLOCK, dtype=jnp.int32)[:, None, None]
    key_offset = jnp.arange(BLOCK, dtype=jnp.int32)[None, None, :]
    earlier = (blocks < own_block)[None, :, None]
    diagonal = (blocks == own_block)[None, :, None] & (key_offset <= query_offset)
    allowed = matches[None, :, None] & (earlier | diagonal)
    return allowed.reshape(BLOCK, count * BLOCK)


def to_sequence(stored, order):
    count = order.shape[0]
    inverse = jnp.zeros((count,), jnp.int32).at[order].set(jnp.arange(count, dtype=jnp.int32))
    width = stored.shape[1]
    return stored.reshape(count, BLOCK, width)[inverse].reshape(count * BLOCK, width)


def to_storage(ordered, order):
    count = order.shape[0]
    width = ordered.shape[1]
    return ordered.reshape(count, BLOCK, width)[order].reshape(count * BLOCK, width)


def shards(queries, keys, values, grad_out, doc_ids, block_order):
    inner_count = lax.axis_size("inner")
    outer_index = lax.axis_index("outer")
    inner_index = lax.axis_index("inner")
    head_dim = keys.shape[1]
    head_count = queries.shape[1] // head_dim
    per_device = queries.shape[0] // BLOCK
    group_blocks = inner_count * per_device
    tile_count = group_blocks // TILE_BLOCKS
    tile_rows = TILE_BLOCKS * BLOCK
    scale = head_dim ** (-0.5)
    group_start = outer_index * group_blocks
    before_start = jnp.maximum(outer_index - 1, 0) * group_blocks
    order_own = lax.dynamic_slice_in_dim(block_order, group_start, group_blocks) - group_start
    order_before = lax.dynamic_slice_in_dim(block_order, before_start, group_blocks) - before_start
    docs_own = lax.dynamic_slice_in_dim(doc_ids, group_start, group_blocks)
    docs_before = jnp.where(
        outer_index > 0, lax.dynamic_slice_in_dim(doc_ids, before_start, group_blocks), -1
    )
    window_docs = jnp.concatenate([docs_before, docs_own])
    own_keys, own_values = (
        lax.all_gather(keys, "inner", axis=0, tiled=True),
        lax.all_gather(values, "inner", axis=0, tiled=True),
    )
    prior_keys, prior_values = from_behind((own_keys, own_values), "outer", 1)
    all_keys = jnp.concatenate(
        [to_sequence(prior_keys, order_before), to_sequence(own_keys, order_own)], axis=0
    )
    all_values = jnp.concatenate(
        [to_sequence(prior_values, order_before), to_sequence(own_values, order_own)], axis=0
    )
    partial_value = jnp.zeros((2 * group_blocks * BLOCK, 2 * head_dim), jnp.float32)
    position = order_own[inner_index * per_device + 0]
    my_doc = docs_own[position]
    first = position + 1
    own_block = position + group_blocks
    query_block = queries.reshape(BLOCK, head_count, head_dim)
    grad_block = grad_out.reshape(BLOCK, head_count, head_dim)

    def tile_inputs(tile_index, first=first, my_doc=my_doc, own_block=own_block):
        start_block = first + tile_index * TILE_BLOCKS
        key_tile = lax.dynamic_slice_in_dim(all_keys, start_block * BLOCK, tile_rows, 0)
        value_tile = lax.dynamic_slice_in_dim(all_values, start_block * BLOCK, tile_rows, 0)
        tile_docs = lax.dynamic_slice_in_dim(window_docs, start_block, TILE_BLOCKS, 0)
        visible = block_visibility(tile_docs, my_doc, start_block, own_block)
        return (start_block, key_tile, value_tile, visible, jnp.any(tile_docs == my_doc))

    def forward_tile(tile_index, carry, query_block=query_block, tile_inputs=tile_inputs):
        start_block, key_tile, value_tile, visible, live = tile_inputs(tile_index)

        def forward_update(state):
            running_max, running_sum, running_out = state
            scores = (
                jnp.einsum("bhd,kd->hbk", query_block, key_tile, preferred_element_type=jnp.float32)
                * scale
            )
            scores = jnp.where(visible[None], scores, NEG)
            new_max = jnp.maximum(running_max, jnp.max(scores, axis=-1))
            factor = jnp.exp(running_max - new_max)
            weights = jnp.where(visible[None], jnp.exp(scores - new_max[..., None]), 0.0)
            new_sum = running_sum * factor + jnp.sum(weights, axis=-1)
            product = jnp.einsum(
                "hbk,kd->hbd",
                weights.astype(jnp.bfloat16),
                value_tile,
                preferred_element_type=jnp.float32,
            )
            return (new_max, new_sum, running_out * factor[..., None] + product)

        return lax.cond(live, forward_update, lambda state: state, carry)

    start_state = (
        jnp.full((head_count, BLOCK), NEG, jnp.float32),
        jnp.zeros((head_count, BLOCK), jnp.float32),
        jnp.zeros((head_count, BLOCK, head_dim), jnp.float32),
    )
    running_max, running_sum, running_out = lax.fori_loop(0, tile_count, forward_tile, start_state)
    log_total = running_max + jnp.log(running_sum)
    attended = running_out / running_sum[..., None]
    delta = jnp.einsum("hbd,bhd->hb", attended, grad_block.astype(jnp.float32))

    def backward_tile(
        tile_index,
        carry,
        query_block=query_block,
        grad_block=grad_block,
        log_total=log_total,
        delta=delta,
        tile_inputs=tile_inputs,
    ):
        start_block, key_tile, value_tile, visible, live = tile_inputs(tile_index)

        def backward_update(state):
            grad_query, accumulated = state
            scores = (
                jnp.einsum("bhd,kd->hbk", query_block, key_tile, preferred_element_type=jnp.float32)
                * scale
            )
            probs = jnp.where(visible[None], jnp.exp(scores - log_total[..., None]), 0.0)
            probs_low = probs.astype(jnp.bfloat16)
            value_grad = jnp.einsum(
                "hbk,bhd->kd", probs_low, grad_block, preferred_element_type=jnp.float32
            )
            prob_grad = jnp.einsum(
                "bhd,kd->hbk", grad_block, value_tile, preferred_element_type=jnp.float32
            )
            score_low = (probs * (prob_grad - delta[..., None])).astype(jnp.bfloat16)
            grad_query = grad_query + jnp.einsum(
                "hbk,kd->hbd", score_low, key_tile, preferred_element_type=jnp.float32
            )
            key_grad = (
                jnp.einsum(
                    "hbk,bhd->kd", score_low, query_block, preferred_element_type=jnp.float32
                )
                * scale
            )
            rows_at = start_block * BLOCK
            current = lax.dynamic_slice_in_dim(accumulated, rows_at, tile_rows, 0)
            joined = jnp.concatenate([key_grad, value_grad], axis=1)
            accumulated = lax.dynamic_update_slice_in_dim(accumulated, current + joined, rows_at, 0)
            return (grad_query, accumulated)

        return lax.cond(live, backward_update, lambda state: state, carry)

    grad_query, partial_value = lax.fori_loop(
        0,
        tile_count,
        backward_tile,
        (jnp.zeros((head_count, BLOCK, head_dim), jnp.float32), partial_value),
    )
    grad_blocks = (
        (grad_query * scale)
        .transpose(1, 0, 2)
        .reshape(BLOCK, head_count * head_dim)
        .astype(jnp.bfloat16)
    )
    rounded = partial_value.astype(jnp.bfloat16)
    stored_before = to_storage(rounded[: group_blocks * BLOCK], order_before)
    stored_own = to_storage(rounded[group_blocks * BLOCK :], order_own)
    returned = from_behind(stored_before, "outer", -1)
    own_sum, back_sum = (
        lax.psum_scatter(
            stored_own.astype(jnp.float32).astype(jnp.bfloat16),
            "inner",
            scatter_dimension=0,
            tiled=True,
        ).astype(jnp.float32),
        lax.psum_scatter(
            returned.astype(jnp.float32).astype(jnp.bfloat16),
            "inner",
            scatter_dimension=0,
            tiled=True,
        ).astype(jnp.float32),
    )
    totals = own_sum + back_sum
    grad_keys = totals[:, :head_dim].astype(jnp.bfloat16)
    grad_values = totals[:, head_dim:].astype(jnp.bfloat16)
    return (grad_blocks, grad_keys, grad_values)


def solution(mesh):
    in_specs = (
        P(("outer", "inner"), None),
        P(("outer", "inner"), None),
        P(("outer", "inner"), None),
        P(("outer", "inner"), None),
        P(),
        P(),
    )
    out_specs = (
        P(("outer", "inner"), None),
        P(("outer", "inner"), None),
        P(("outer", "inner"), None),
    )
    return jax.shard_map(shards, mesh=mesh, in_specs=in_specs, out_specs=out_specs, check_vma=False)
```

profile of v0, /device:TPU:6, one launch (start us, length us, event | category | flops | bytes accessed | tf_op | source)
XLA Modules:
  0.0 1178.9 jit_solution(3200356129722083603)
XLA Ops:
  8.7 228.0 %all-gather.3.cloned.1.call-done = bf16[4096,128]{1,0:T(8,128)(2,1)} async-done(((bf16[128,128]{1,0:T(8,128)(2,1)}), bf16[4096,128]{1,0:T(8,128)(2,1)}) %all-gather.3.cloned.1.call-update) | async-done | bytes 1048592 | tf_op jit(solution)/shard_map/all_gather | solution.py:65
  236.7 2.0 collective-permute-start
  238.8 252.5 %all-gather.5.cloned.1.call-done = bf16[4096,128]{1,0:T(8,128)(2,1)} async-done(((bf16[128,128]{1,0:T(8,128)(2,1)}), bf16[4096,128]{1,0:T(8,128)(2,1)}) %all-gather.5.cloned.1.call-update) | async-done | bytes 1048592 | tf_op jit(solution)/shard_map/all_gather | solution.py:66
  491.3 2.0 collective-permute-start.1
  502.6 1.7 gather_fusion.1
  504.3 1.6 gather_fusion.3
  505.9 2.9 gather_fusion
  508.8 20.8 %collective-permute-done.1 = bf16[4096,128]{1,0:T(8,128)(2,1)} collective-permute-done((bf16[4096,128]{1,0:T(8,128)(2,1)}, bf16[4096,128]{1,0:T(8,128)(2,1)}, u32[]{:S(2)}, u32[]{:S(2)}) %collective-permute-start.1) | collective-permute-done | bytes 1048608 | tf_op jit(solution)/shard_map/ppermute | solution.py:16
  529.7 2.9 gather_fusion.2
  532.6 1.8 pad_maximum_fusion
  534.7 1.5 pad_maximum_fusion.1
  536.3 42.2 %while.32 = (s32[]{:T(128)}, f32[8,128]{1,0:T(8,128)S(1)}, f32[8,128]{1,0:T(8,128)S(1)}, f32[8,128,128]{2,1,0:T(8,128)S(1)}, s32[]{:T(128)}, /*index=5*/s32[64]{...) while((s32[]{:T(128)}, f32[8,128]{1,0:T(8,128)S(1)}, ...), condition=%wide.region_8.0_spmd, body=%wide.region_2.8_spmd.sunk | while | flops 275728384 | bytes 8490491 | solution.py:120
  538.3 3.3 conditional.4
  539.8 1.7 convolution_add_fusion
  543.6 3.3 conditional.4
  545.1 1.7 convolution_add_fusion
  548.8 3.3 conditional.4
  550.3 1.7 convolution_add_fusion
  554.1 3.3 conditional.4
  555.6 1.7 convolution_add_fusion
  559.4 3.3 conditional.4
  560.9 1.7 convolution_add_fusion
  564.7 3.3 conditional.4
  566.2 1.7 convolution_add_fusion
  569.9 3.3 conditional.4
  571.4 1.7 convolution_add_fusion
  575.2 3.3 conditional.4
  576.7 1.7 convolution_add_fusion
  580.9 4.2 broadcast_in_dim.114
  585.1 63.1 %while.33 = (s32[]{:T(128)}, f32[8,128,128]{2,1,0:T(8,128)S(1)}, f32[8192,256]{0,1:T(8,128)}, s32[]{:T(128)}, s32[64]{0:T(128)S(1)}, /*index=5*/s32[]{:T(128)}, ...) while((s32[]{:T(128)}, f32[8,128,128]{2,1,0:T(8,128)S(1)}, ...), condition=%wide.region_13.14_spmd, body=%wide.region_9.13_spmd.sunk | while | flops 675430400 | bytes 14462483 | solution.py:168
  585.1 1.4 fusion.58
  587.1 5.8 conditional.5
  591.0 1.9 fusion.26
  592.9 1.4 fusion.58
  595.0 5.8 conditional.5
  598.9 1.9 fusion.26
  600.8 1.4 fusion.58
  602.9 5.8 conditional.5
  606.8 1.9 fusion.26
  608.7 1.4 fusion.58
  610.7 5.8 conditional.5
  614.6 1.9 fusion.26
  616.6 1.4 fusion.58
  618.6 5.8 conditional.5
  622.5 2.0 fusion.26
  624.5 1.4 fusion.58
  626.5 5.9 conditional.5
  630.4 2.0 fusion.26
  632.4 1.4 fusion.58
  634.4 5.8 conditional.5
  638.3 1.9 fusion.26
  640.2 1.4 fusion.58
  642.3 5.9 conditional.5
  646.2 2.0 fusion.26
  648.1 3.9 convert_element_type.63
  652.1 2.2 fusion.45
  654.3 3.3 copy.29
  657.6 2.0 gather_fusion.4
  659.7 3.3 copy.30
  663.0 2.0 gather_fusion.5
  665.0 1.9 collective-permute-start.2
  666.9 51.9 %collective-permute-done.2 = bf16[4096,256]{1,0:T(8,128)(2,1)S(1)} collective-permute-done((bf16[4096,256]{1,0:T(8,128)(2,1)}, bf16[4096,256]{1,0:T(8,128)(2,1)S(1)}, u32[]{:S(2)}, u32[]{:S(2)}) %collective-permute-start.2) | collective-permute-done | bytes 2097184 | tf_op jit(solution)/shard_map/ppermute | solution.py:16
  720.8 197.8 %reduce-scatter.3.cloned.1.call-done = bf16[128,256]{1,0:T(8,128)(2,1)} async-done(((bf16[4096,256]{1,0:T(8,128)(2,1)}), bf16[128,256]{1,0:T(8,128)(2,1)}) %reduce-scatter.3.cloned.1.call-update) | async-done | bytes 65552 | tf_op jit(solution)/shard_map/reduce_scatter | solution.py:185
  918.6 252.2 %reduce-scatter.5.cloned.1.call-done = bf16[128,256]{1,0:T(8,128)(2,1)} async-done(((bf16[4096,256]{1,0:T(8,128)(2,1)}), bf16[128,256]{1,0:T(8,128)(2,1)}) %reduce-scatter.5.cloned.1.call-update) | async-done | bytes 65552 | tf_op jit(solution)/shard_map/reduce_scatter | solution.py:191
  (263 shorter events, 67.4 us)
Async XLA Ops:
  7.2 229.6 %all-gather.3.cloned.1.call-start = ((), (), s32[]{:S(2)}) async-start(), calls=%async_computation.2 | async-start | bytes 1081344 | tf_op jit(solution)/shard_map/all_gather | solution.py:65
  7.9 483.4 %all-gather.5.cloned.1.call-start = ((), (), s32[]{:S(2)}) async-start(), calls=%async_computation.3 | async-start | bytes 1081344 | tf_op jit(solution)/shard_map/all_gather | solution.py:66
  8.6 910.0 %reduce-scatter.3.cloned.1.call-start = ((), (), s32[]{:S(2)}) async-start(), calls=%async_computation.4 | async-start | bytes 2162688 | tf_op jit(solution)/shard_map/reduce_scatter | solution.py:185
  236.7 265.9 %copy-start.3 = (bf16[4096,128]{1,0:T(8,128)(2,1)S(1)}, bf16[4096,128]{1,0:T(8,128)(2,1)}, u32[]{:S(2)}) copy-start(bf16[4096,128]{1,0:T(8,128)(2,1)} %all-gather.3.cloned.1.call-done) | copy-start | bytes 3145732
  236.7 269.2 %collective-permute-start = (bf16[4096,128]{1,0:T(8,128)(2,1)}, bf16[4096,128]{1,0:T(8,128)(2,1)}, u32[]{:S(2)}, u32[]{:S(2)}) collective-permute-start(bf16[4096,128]{1,0:T(8,128)(2,1)} %all-gather.3.cloned.1.call-done), channel_id=1, source_target_pairs={{0,32},{32,64},{64,96},{96,128},{128,160},{160,192},{192,224},{224... | collective-permute-start | bytes 3145736 | tf_op jit(solution)/shard_map/ppermute | solution.py:16
  491.3 13.0 %copy-start.4 = (bf16[4096,128]{1,0:T(8,128)(2,1)S(1)}, bf16[4096,128]{1,0:T(8,128)(2,1)}, u32[]{:S(2)}) copy-start(bf16[4096,128]{1,0:T(8,128)(2,1)} %all-gather.5.cloned.1.call-done) | copy-start | bytes 3145732
  491.3 38.4 %collective-permute-start.1 = (bf16[4096,128]{1,0:T(8,128)(2,1)}, bf16[4096,128]{1,0:T(8,128)(2,1)}, u32[]{:S(2)}, u32[]{:S(2)}) collective-permute-start(bf16[4096,128]{1,0:T(8,128)(2,1)} %all-gather.5.cloned.1.call-done), channel_id=1, source_target_pairs={{0,32},{32,64},{64,96},{96,128},{128,160},{160,192},{192,224},{224... | collective-permute-start | bytes 3145736 | tf_op jit(solution)/shard_map/ppermute | solution.py:16
  532.6 1.9 copy-start
  532.6 2.2 copy-start.1
  659.6 511.2 %reduce-scatter.5.cloned.1.call-start = ((), (), s32[]{:S(2)}) async-start(), calls=%async_computation.5 | async-start | bytes 2162688 | tf_op jit(solution)/shard_map/reduce_scatter | solution.py:191
  665.0 53.8 %collective-permute-start.2 = (bf16[4096,256]{1,0:T(8,128)(2,1)}, bf16[4096,256]{1,0:T(8,128)(2,1)S(1)}, u32[]{:S(2)}, u32[]{:S(2)}) collective-permute-start(bf16[4096,256]{1,0:T(8,128)(2,1)} %bitcast.124), channel_id=1, source_target_pairs={{32,0},{64,32},{96,64},{128,96},{160,128},{192,160},{224,192},{256... | collective-permute-start | bytes 6291464 | tf_op jit(solution)/shard_map/ppermute | solution.py:16
  718.7 1.3 copy-start.2
Sparse Core Ops, SparseCore 0:
  10.1 226.6 all-gather.2
  238.8 252.4 all-gather.4
  659.8 258.8 reduce-scatter.2
  921.5 249.2 reduce-scatter.4
where the time goes:
time: 1180 us
  waiting for transfers between devices  1000 us (85%)
  other arithmetic  57.3 us (5%)
  matrix products  44.4 us (4%)
  local copies, waits for them, and re-layouts  38 us (3%)
  between operations  16.6 us (1%)
  loops' own time  11.8 us (1%)
    all_gather x1, waiting for transfers between devices, shards(): lax.all_gather(values, 'inner', axis=0, tiled=True)  253 us
    reduce_scatter x1, waiting for transfers between devices, shards(): lax.psum_scatter(returned.astype(jnp.float32).astype(jnp.bfloat16), 'inne...  252 us
    all_gather x1, waiting for transfers between devices, shards(): lax.all_gather(keys, 'inner', axis=0, tiled=True)  228 us
    reduce_scatter x1, waiting for transfers between devices, shards(): lax.psum_scatter(stored_own.astype(jnp.float32).astype(jnp.bfloat16), 'in...  198 us
    ppermute x3, waiting for transfers between devices, from_behind(): return lax.ppermute(array, axis, pairs)  72.7 us
  transfers between devices with their start and end apart: 7, of which 6 were waited for; matrix products, arithmetic and copies ran while one was open for 2% of the time, Pallas kernels for 0%

commit v1 on v0

v1 whole, which is shorter than its diff:
```python
import functools

import jax
import jax.numpy as jnp
from jax import lax
from jax.experimental import pallas as pl
from jax.experimental.pallas import tpu as pltpu
from jax.sharding import PartitionSpec as P

BLOCK = 128
HD = 128
HEADS = 8
ROWS = HEADS * BLOCK
GROUP = 32
NY = 4
NZ = 8
CHUNK = 256
NEG = -1e30
SCALE = HD**-0.5
SCALE2 = SCALE * 1.4426950408889634
VMEM_LIMIT = 40 * 1024 * 1024


def dot_nt(a, b):
    return lax.dot_general(a, b, (((1,), (1,)), ((), ())), preferred_element_type=jnp.float32)


def dot_nn(a, b):
    return lax.dot_general(a, b, (((1,), (0,)), ((), ())), preferred_element_type=jnp.float32)


def dot_tn(a, b):
    return lax.dot_general(a, b, (((0,), (0,)), ((), ())), preferred_element_type=jnp.float32)


def stack_heads(refs, target):
    for r, ref in enumerate(refs):
        for h in range(HEADS):
            target[r * ROWS + h * BLOCK : r * ROWS + (h + 1) * BLOCK, :] = ref[
                :, h * HD : (h + 1) * HD
            ]


def place(low, high, target):
    half = low.shape[0]
    target[0:half, :] = low[...]
    target[half : 2 * half, :] = high[...]


def pair_visible(ids, docs, order, prior, r, s):
    outer, inner = ids[0], ids[1]
    flip = ((s & 1) << 2) | (s & 2) | ((s >> 2) & 1)
    q_pos = order[outer * GROUP + (inner ^ (r * NZ))]
    if prior:
        k_pos = order[jnp.maximum(outer - 1, 0) * GROUP + (inner ^ flip)]
        return (outer > 0) & (docs[q_pos] == docs[k_pos])
    k_pos = order[outer * GROUP + (inner ^ flip)]
    return (docs[q_pos] == docs[k_pos]) & (k_pos < q_pos)


def diagonal_mask():
    k_at = lax.broadcasted_iota(jnp.int32, (BLOCK, CHUNK), 0)
    q_at = lax.broadcasted_iota(jnp.int32, (BLOCK, CHUNK), 1) % BLOCK
    return k_at <= q_at


def for_pairs(ids, docs, order, prior, pair):
    if not prior:
        pair(0, 0, True)

    @pl.loop(0 if prior else 1, NY * NZ)
    def _(step):
        r = step // NZ
        s = step % NZ

        @pl.when(pair_visible(ids, docs, order, prior, r, s))
        def _():
            pair(r, s, False)


def stats_kernel(prior, *refs):
    ids, docs, order = refs[:3]
    q_refs, g_refs = refs[3:7], refs[7:11]
    low, high = refs[11:13]
    rest = refs[13:]
    if prior:
        before, rest = rest[0], rest[1:]
    stats, qs, gs, kv = rest
    stack_heads(q_refs, qs)
    stack_heads(g_refs, gs)
    place(low, high, kv)
    if prior:
        stats[...] = before[...]
    else:
        stats[0:NY, :] = jnp.full((NY, ROWS), NEG, jnp.float32)
        stats[NY : 3 * NY, :] = jnp.zeros((2 * NY, ROWS), jnp.float32)

    def pair(r, s, diagonal):
        key = kv[pl.ds(s * 2 * BLOCK, BLOCK), :]
        value = kv[pl.ds(s * 2 * BLOCK + BLOCK, BLOCK), :]
        for c in range(ROWS // CHUNK):
            rows = pl.ds(r * ROWS + c * CHUNK, CHUNK)
            cols = pl.ds(c * CHUNK, CHUNK)
            scores = dot_nt(key, qs[rows, :]) * SCALE2
            dprob = dot_nt(value, gs[rows, :])
            if diagonal:
                scores = jnp.where(diagonal_mask(), scores, NEG)
            top = stats[pl.ds(r, 1), cols]
            new_top = jnp.maximum(top, jnp.max(scores, axis=0, keepdims=True))
            factor = jnp.exp2(top - new_top)
            weights = jnp.exp2(scores - new_top)
            stats[pl.ds(r, 1), cols] = new_top
            stats[pl.ds(NY + r, 1), cols] = stats[pl.ds(NY + r, 1), cols] * factor + jnp.sum(
                weights, axis=0, keepdims=True
            )
            stats[pl.ds(2 * NY + r, 1), cols] = stats[
                pl.ds(2 * NY + r, 1), cols
            ] * factor + jnp.sum(weights * dprob, axis=0, keepdims=True)

    for_pairs(ids, docs, order, prior, pair)


def grads_kernel(prior, *refs):
    ids, docs, order = refs[:3]
    q_refs, g_refs = refs[3:7], refs[7:11]
    low, high = refs[11:13]
    stat_refs = refs[13:17]
    rest = refs[17:]
    if prior:
        outs, scratch = rest[:5], rest[5:]
    else:
        dq_before, rest = rest[0], rest[1:]
        outs, scratch = rest[:8], rest[8:]
    out_high, out_mid, out_one, out_zero = outs[:4]
    qs, gs, kv, lse, delta, w_low, d_low, dkv = scratch[:8]
    dq = outs[4] if prior else scratch[8]
    stack_heads(q_refs, qs)
    stack_heads(g_refs, gs)
    place(low, high, kv)
    dkv[...] = jnp.zeros_like(dkv)
    if prior:
        dq[...] = jnp.zeros_like(dq)
    else:
        dq[...] = dq_before[...]
    for r in range(NY):
        tops = [stat_refs[k][(r ^ k) : (r ^ k) + 1, :] for k in range(NY)]
        top = functools.reduce(jnp.maximum, tops)
        total = jnp.zeros_like(top)
        product = jnp.zeros_like(top)
        for k in range(NY):
            factor = jnp.exp2(tops[k] - top)
            at = r ^ k
            total = total + stat_refs[k][NY + at : NY + at + 1, :] * factor
            product = product + stat_refs[k][2 * NY + at : 2 * NY + at + 1, :] * factor
        lse[r : r + 1, :] = top + jnp.log2(total)
        delta[r : r + 1, :] = product / total

    def pair(r, s, diagonal):
        key = kv[pl.ds(s * 2 * BLOCK, BLOCK), :]
        value = kv[pl.ds(s * 2 * BLOCK + BLOCK, BLOCK), :]
        for c in range(ROWS // CHUNK):
            rows = pl.ds(r * ROWS + c * CHUNK, CHUNK)
            cols = pl.ds(c * CHUNK, CHUNK)
            scores = dot_nt(key, qs[rows, :]) * SCALE2
            dprob = dot_nt(value, gs[rows, :])
            probs = jnp.exp2(scores - lse[pl.ds(r, 1), cols])
            if diagonal:
                probs = jnp.where(diagonal_mask(), probs, 0.0)
            w_low[:, cols] = probs.astype(jnp.bfloat16)
            d_low[:, cols] = (probs * (dprob - delta[pl.ds(r, 1), cols])).astype(jnp.bfloat16)
        rows = pl.ds(r * ROWS, ROWS)
        dkv[pl.ds(s * 2 * BLOCK, BLOCK), :] += dot_nn(d_low[...], qs[rows, :])
        dkv[pl.ds(s * 2 * BLOCK + BLOCK, BLOCK), :] += dot_nn(w_low[...], gs[rows, :])
        dq[pl.ds(r * HD, HD), :] += dot_tn(key, d_low[...])

    for_pairs(ids, docs, order, prior, pair)

    for slots, out in (((4, 8), out_high), ((2, 4), out_mid), ((1, 2), out_one), ((0, 1), out_zero)):
        for at, s in enumerate(range(*slots)):
            lo = s * 2 * BLOCK
            to = at * 2 * BLOCK
            out[to : to + BLOCK, :] = (dkv[lo : lo + BLOCK, :] * SCALE).astype(jnp.bfloat16)
            out[to + BLOCK : to + 2 * BLOCK, :] = dkv[lo + BLOCK : lo + 2 * BLOCK, :].astype(
                jnp.bfloat16
            )
    if not prior:
        for r in range(NY):
            for h in range(HEADS):
                part = dq[r * HD : (r + 1) * HD, h * BLOCK : (h + 1) * BLOCK] * SCALE
                outs[4 + r][:, h * HD : (h + 1) * HD] = part.astype(jnp.bfloat16).T


def smem():
    return pl.BlockSpec(memory_space=pltpu.SMEM)


def vmem():
    return pl.BlockSpec(memory_space=pltpu.VMEM)


def common_scratch():
    return [
        pltpu.VMEM((NY * ROWS, HD), jnp.bfloat16),
        pltpu.VMEM((NY * ROWS, HD), jnp.bfloat16),
        pltpu.VMEM((NZ * 2 * BLOCK, HD), jnp.bfloat16),
    ]


def cost(matmuls, pairs):
    return pl.CostEstimate(
        flops=matmuls * pairs * 2 * ROWS * BLOCK * HD,
        bytes_accessed=4 * 1024 * 1024,
        transcendentals=pairs * ROWS * BLOCK,
    )


def run_stats(prior, scalars, q_slots, g_slots, low, high, before=None):
    args = (*scalars, *q_slots, *g_slots, low, high)
    if prior:
        args = (*args, before)
    return pl.pallas_call(
        functools.partial(stats_kernel, prior),
        out_shape=jax.ShapeDtypeStruct((3 * NY, ROWS), jnp.float32),
        in_specs=[smem()] * 3 + [vmem()] * (len(args) - 3),
        out_specs=vmem(),
        scratch_shapes=common_scratch(),
        compiler_params=pltpu.CompilerParams(vmem_limit_bytes=VMEM_LIMIT),
        cost_estimate=cost(2, 16),
    )(*args)


def run_grads(prior, scalars, q_slots, g_slots, low, high, stats, dq_before=None):
    args = (*scalars, *q_slots, *g_slots, low, high, *stats)
    outs = [jax.ShapeDtypeStruct((n * 2 * BLOCK, HD), jnp.bfloat16) for n in (4, 2, 1, 1)]
    scratch = common_scratch() + [
        pltpu.VMEM((NY, ROWS), jnp.float32),
        pltpu.VMEM((NY, ROWS), jnp.float32),
        pltpu.VMEM((BLOCK, ROWS), jnp.bfloat16),
        pltpu.VMEM((BLOCK, ROWS), jnp.bfloat16),
        pltpu.VMEM((NZ * 2 * BLOCK, HD), jnp.float32),
    ]
    if prior:
        outs.append(jax.ShapeDtypeStruct((NY * HD, ROWS), jnp.float32))
    else:
        args = (*args, dq_before)
        outs += [jax.ShapeDtypeStruct((BLOCK, HEADS * HD), jnp.bfloat16)] * NY
        scratch.append(pltpu.VMEM((NY * HD, ROWS), jnp.float32))
    return pl.pallas_call(
        functools.partial(grads_kernel, prior),
        out_shape=outs,
        in_specs=[smem()] * 3 + [vmem()] * (len(args) - 3),
        out_specs=[vmem()] * len(outs),
        scratch_shapes=scratch,
        compiler_params=pltpu.CompilerParams(vmem_limit_bytes=VMEM_LIMIT),
        cost_estimate=cost(5, 16),
    )(*args)


def swap(array, flip):
    return lax.ppermute(array, "inner", [(i, i ^ flip) for i in range(GROUP)])


def across(array, by, flip):
    outer = lax.axis_size("outer")
    pairs = [
        (o * GROUP + i, (o + by) * GROUP + (i ^ flip))
        for o in range(outer)
        if 0 <= o + by < outer
        for i in range(GROUP)
    ]
    return lax.ppermute(array, ("outer", "inner"), pairs)


def add_low(*terms):
    total = terms[0].astype(jnp.float32)
    for term in terms[1:]:
        total = total + term.astype(jnp.float32)
    return total.astype(jnp.bfloat16)


def shards(queries, keys, values, grad_out, doc_ids, block_order):
    one = 2 * BLOCK
    ids = jnp.stack([lax.axis_index("outer"), lax.axis_index("inner")]).astype(jnp.int32)
    scalars = (ids, doc_ids, block_order)
    own = jnp.concatenate([keys, values], axis=0)

    before0 = across(own, 1, 0)
    before4 = across(own, 1, 4)
    own4 = swap(own, 4)
    q1, g1 = swap(queries, NZ), swap(grad_out, NZ)
    q3, g3 = swap(queries, 3 * NZ), swap(grad_out, 3 * NZ)
    own_pair = jnp.concatenate([own, own4], axis=0)
    own2 = swap(own_pair, 2)
    own_low = jnp.concatenate([own_pair, own2], axis=0)
    own_high = swap(own_low, 1)
    before_pair = jnp.concatenate([before0, before4], axis=0)
    before2 = swap(before_pair, 2)
    before_low = jnp.concatenate([before_pair, before2], axis=0)
    before_high = swap(before_low, 1)
    q2, g2 = swap(q1, 3 * NZ), swap(g3, NZ)
    q_slots = (queries, q1, q2, q3)
    g_slots = (grad_out, g1, g2, g3)

    stats = run_stats(False, scalars, q_slots, g_slots, own_low, own_high)
    stats = run_stats(True, scalars, q_slots, g_slots, before_low, before_high, stats)
    all_stats = (stats, swap(stats, NZ), swap(stats, 2 * NZ), swap(stats, 3 * NZ))

    b_high, b_mid, b_one, b_zero, dq_before = run_grads(
        True, scalars, q_slots, g_slots, before_low, before_high, all_stats
    )
    b1 = swap(b_high, 1)
    o_high, o_mid, o_one, o_zero, dq0, dq1, dq2, dq3 = run_grads(
        False, scalars, q_slots, g_slots, own_low, own_high, all_stats, dq_before
    )
    b2 = swap(add_low(b_mid, b1[2 * one :]), 2)
    o1 = swap(o_high, 1)
    back0 = across(add_low(b_zero, b1[:one], b2[:one]), -1, 0)
    back4 = across(add_low(b_one, b1[one : 2 * one], b2[one:]), -1, 4)
    o2 = swap(add_low(o_mid, o1[2 * one :]), 2)
    e2 = swap(dq2, 2 * NZ)
    e1 = swap(dq1, NZ)
    e3 = swap(dq3, 3 * NZ)
    o4 = swap(add_low(o_one, o1[one : 2 * one], o2[one:]), 4)
    grad_queries = add_low(dq0, e1, e2, e3)
    totals = add_low(o_zero, o1[:one], o2[:one], o4, back0, back4)
    return grad_queries, totals[:BLOCK], totals[BLOCK:]


def solution(mesh):
    rows = P(("outer", "inner"), None)
    return jax.shard_map(
        shards,
        mesh=mesh,
        in_specs=(rows, rows, rows, rows, P(), P()),
        out_specs=(rows, rows, rows),
        check_vma=False,
    )
```

time: 1180 us -> 166 us (0.14)
  the two profiles are of different devices: /device:TPU:6 before, /device:TPU:4 now
where the time goes in v1:
time: 166 us; the launch traced here: 165 us
  starting transfers between devices  105 us (63%)
  waiting for transfers between devices  33.4 us (20%)
  Pallas kernels  18.5 us (11%)
  local copies, waits for them, and re-layouts  5.51 us (3%)
  other arithmetic  1.96 us (1%)
    ppermute x22, starting transfers between devices, swap(): return lax.ppermute(array, 'inner', [(i, i ^ flip) for i in range(GROUP)])  86.3 us
    ppermute x22, waiting for transfers between devices, swap(): return lax.ppermute(array, 'inner', [(i, i ^ flip) for i in range(GROUP)])  28.3 us
    ppermute x4, starting transfers between devices, across(): return lax.ppermute(array, ('outer', 'inner'), pairs)  18.6 us
    pallas_call x2, Pallas kernels, run_grads(): pl.pallas_call(functools.partial(grads_kernel, prior), out_shape=outs, in...  10.6 us
    pallas_call x2, Pallas kernels, run_stats(): pl.pallas_call(functools.partial(stats_kernel, prior), out_shape=jax.Shap...  7.93 us
    ppermute x4, waiting for transfers between devices, across(): return lax.ppermute(array, ('outer', 'inner'), pairs)  5.1 us
    unnamed x12, local copies, waits for them, and re-layouts  4.07 us
  transfers between devices with their start and end apart: 26, of which 10 were waited for; matrix products, arithmetic and copies ran while one was open for 1% of the time, Pallas kernels for 3%

profile of v1, /device:TPU:4, one launch (start us, length us, event | category | flops | bytes accessed | tf_op | source)
XLA Modules:
  0.0 165.3 jit_solution(9293890555986381761)
XLA Ops:
  0.6 0.8 constant_dynamic-update-slice_fusion.1
  1.4 0.8 constant_dynamic-update-slice_fusion
  2.2 8.5 %collective-permute-start.10 = (bf16[256,128]{1,0:T(8,128)(2,1)S(1)}, bf16[256,128]{1,0:T(8,128)(2,1)S(1)}, u32[]{:S(2)}, u32[]{:S(2)}) collective-permute-start(bf16[256,128]{1,0:T(8,128)(2,1)S(1)} %get-tuple-element.33), channel_id=1, source_target_pairs={{0,36},{1,37},{2,38},{3,39},{4,32},{5,33},{6,34},{7,35},{8,44},{9,... | collective-permute-start | bytes 196616 | tf_op jit(solution)/shard_map/ppermute | solution.py:271
  10.7 6.2 %collective-permute-start.9 = (bf16[256,128]{1,0:T(8,128)(2,1)S(1)}, bf16[256,128]{1,0:T(8,128)(2,1)S(1)}, u32[]{:S(2)}, u32[]{:S(2)}) collective-permute-start(bf16[256,128]{1,0:T(8,128)(2,1)S(1)} %get-tuple-element.33), channel_id=1, source_target_pairs={{0,32},{1,33},{2,34},{3,35},{4,36},{5,37},{6,38},{7,39},{8,40},{9,... | collective-permute-start | bytes 196616 | tf_op jit(solution)/shard_map/ppermute | solution.py:271
  17.0 4.9 %collective-permute-start.2 = (bf16[128,1024]{1,0:T(8,128)(2,1)}, bf16[128,1024]{1,0:T(8,128)(2,1)S(1)}, u32[]{:S(2)}, u32[]{:S(2)}) collective-permute-start(bf16[128,1024]{1,0:T(8,128)(2,1)} %refs_3_.7), channel_id=1, source_target_pairs={{0,24},{1,25},{2,26},{3,27},{4,28},{5,29},{6,30},{7,31},{8,16},{9,... | collective-permute-start | bytes 786440 | tf_op jit(solution)/shard_map/ppermute | solution.py:260
  21.9 2.0 %collective-permute-start = (bf16[128,1024]{1,0:T(8,128)(2,1)}, bf16[128,1024]{1,0:T(8,128)(2,1)S(1)}, u32[]{:S(2)}, u32[]{:S(2)}) collective-permute-start(bf16[128,1024]{1,0:T(8,128)(2,1)} %refs_3_.7), channel_id=1, source_target_pairs={{0,8},{1,9},{2,10},{3,11},{4,12},{5,13},{6,14},{7,15},{8,0},{9,1},... | collective-permute-start | bytes 786440 | tf_op jit(solution)/shard_map/ppermute | solution.py:260
  23.9 5.5 %collective-permute-start.6 = (bf16[256,128]{1,0:T(8,128)(2,1)S(1)}, bf16[256,128]{1,0:T(8,128)(2,1)S(1)}, u32[]{:S(2)}, u32[]{:S(2)}) collective-permute-start(bf16[256,128]{1,0:T(8,128)(2,1)S(1)} %get-tuple-element.33), channel_id=1, source_target_pairs={{0,4},{1,5},{2,6},{3,7},{4,0},{5,1},{6,2},{7,3},{8,12},{9,13},{10,... | collective-permute-start | bytes 196616 | tf_op jit(solution)/shard_map/ppermute | solution.py:260
  29.4 0.0 collective-permute-done.10
  29.4 3.0 %collective-permute-start.4 = (bf16[128,1024]{1,0:T(8,128)(2,1)}, bf16[128,1024]{1,0:T(8,128)(2,1)S(1)}, u32[]{:S(2)}, u32[]{:S(2)}) collective-permute-start(bf16[128,1024]{1,0:T(8,128)(2,1)} %refs_7_.7), channel_id=1, source_target_pairs={{0,24},{1,25},{2,26},{3,27},{4,28},{5,29},{6,30},{7,31},{8,16},{9,... | collective-permute-start | bytes 786440 | tf_op jit(solution)/shard_map/ppermute | solution.py:260
  32.4 0.0 collective-permute-done.9
  32.4 3.4 %collective-permute-start.11 = (bf16[512,128]{1,0:T(8,128)(2,1)S(1)}, bf16[512,128]{1,0:T(8,128)(2,1)S(1)}, u32[]{:S(2)}, u32[]{:S(2)}) collective-permute-start(bf16[512,128]{1,0:T(8,128)(2,1)S(1)} %pad_maximum_fusion.1), channel_id=1, source_target_pairs={{0,2},{1,3},{2,0},{3,1},{4,6},{5,7},{6,4},{7,5},{8,10},{9,11},{10,... | collective-permute-start | bytes 393224 | tf_op jit(solution)/shard_map/ppermute | solution.py:260
  35.8 0.3 collective-permute-done.6
  36.1 0.8 pad_maximum_fusion
  36.9 3.1 %collective-permute-start.7 = (bf16[512,128]{1,0:T(8,128)(2,1)S(1)}, bf16[512,128]{1,0:T(8,128)(2,1)S(1)}, u32[]{:S(2)}, u32[]{:S(2)}) collective-permute-start(bf16[512,128]{1,0:T(8,128)(2,1)S(1)} %pad_maximum_fusion), channel_id=1, source_target_pairs={{0,2},{1,3},{2,0},{3,1},{4,6},{5,7},{6,4},{7,5},{8,10},{9,11},{10,... | collective-permute-start | bytes 393224 | tf_op jit(solution)/shard_map/ppermute | solution.py:260
  40.0 9.2 %collective-permute-done.7 = bf16[512,128]{1,0:T(8,128)(2,1)S(1)} collective-permute-done((bf16[512,128]{1,0:T(8,128)(2,1)S(1)}, bf16[512,128]{1,0:T(8,128)(2,1)S(1)}, u32[]{:S(2)}, u32[]{:S(2)}) %collective-permute-start.7) | collective-permute-done | bytes 131104 | tf_op jit(solution)/shard_map/ppermute | solution.py:260
  49.2 3.4 %collective-permute-start.3 = (bf16[128,1024]{1,0:T(8,128)(2,1)}, bf16[128,1024]{1,0:T(8,128)(2,1)S(1)}, u32[]{:S(2)}, u32[]{:S(2)}) collective-permute-start(bf16[128,1024]{1,0:T(8,128)(2,1)} %refs_7_.7), channel_id=1, source_target_pairs={{0,8},{1,9},{2,10},{3,11},{4,12},{5,13},{6,14},{7,15},{8,0},{9,1},... | collective-permute-start | bytes 786440 | tf_op jit(solution)/shard_map/ppermute | solution.py:260
  52.6 0.0 collective-permute-done.11
  52.6 1.9 %collective-permute-start.8 = (bf16[1024,128]{1,0:T(8,128)(2,1)S(1)}, bf16[1024,128]{1,0:T(8,128)(2,1)S(1)}, u32[]{:S(2)}, u32[]{:S(2)}) collective-permute-start(bf16[1024,128]{1,0:T(8,128)(2,1)S(1)} %constant_dynamic-update-slice_fusion.2.refs_11_), channel_id=1, source_target_pairs={{0,1},{1,0},{2,3},{3,2},{4,5},{5,4},{6,7},{7,6},{8,9},{9,8},{10,11... | collective-permute-start | bytes 786440 | tf_op jit(solution)/shard_map/ppermute | solution.py:260
  54.6 0.0 collective-permute-done.refs_4_
  54.6 3.8 %collective-permute-start.1 = (bf16[128,1024]{1,0:T(8,128)(2,1)S(1)}, bf16[128,1024]{1,0:T(8,128)(2,1)S(1)}, u32[]{:S(2)}, u32[]{:S(2)}) collective-permute-start(bf16[128,1024]{1,0:T(8,128)(2,1)S(1)} %collective-permute-done.refs_4_), channel_id=1, source_target_pairs={{0,24},{1,25},{2,26},{3,27},{4,28},{5,29},{6,30},{7,31},{8,16},{9,... | collective-permute-start | bytes 786440 | tf_op jit(solution)/shard_map/ppermute | solution.py:260
  58.4 0.0 collective-permute-done.4.refs_10_
  58.4 2.2 %collective-permute-start.5 = (bf16[128,1024]{1,0:T(8,128)(2,1)S(1)}, bf16[128,1024]{1,0:T(8,128)(2,1)S(1)}, u32[]{:S(2)}, u32[]{:S(2)}) collective-permute-start(bf16[128,1024]{1,0:T(8,128)(2,1)S(1)} %collective-permute-done.4.refs_10_), channel_id=1, source_target_pairs={{0,8},{1,9},{2,10},{3,11},{4,12},{5,13},{6,14},{7,15},{8,0},{9,1},... | collective-permute-start | bytes 786440 | tf_op jit(solution)/shard_map/ppermute | solution.py:260
  60.6 0.0 collective-permute-done.2.refs_6_
  60.6 3.9 %collective-permute-start.12 = (bf16[1024,128]{1,0:T(8,128)(2,1)S(1)}, bf16[1024,128]{1,0:T(8,128)(2,1)S(1)}, u32[]{:S(2)}, u32[]{:S(2)}) collective-permute-start(bf16[1024,128]{1,0:T(8,128)(2,1)S(1)} %constant_dynamic-update-slice_fusion.6.refs_11_), channel_id=1, source_target_pairs={{0,1},{1,0},{2,3},{3,2},{4,5},{5,4},{6,7},{7,6},{8,9},{9,8},{10,11... | collective-permute-start | bytes 786440 | tf_op jit(solution)/shard_map/ppermute | solution.py:260
  64.6 0.1 pad_add_fusion.refs_0_
  64.6 0.0 collective-permute-done.3.refs_8_
  64.6 0.0 collective-permute-done.8.refs_12_
  64.7 1.2 collective-permute-done.1.refs_5_
  65.9 2.8 %collective-permute-done.5.refs_9_ = bf16[128,1024]{1,0:T(8,128)(2,1)S(1)} collective-permute-done((bf16[128,1024]{1,0:T(8,128)(2,1)S(1)}, bf16[128,1024]{1,0:T(8,128)(2,1)S(1)}, u32[]{:S(2)}, u32[]{:S(2)}) %collective-permute-start.5) | collective-permute-done | bytes 262176 | tf_op jit(solution)/shard_map/ppermute | solution.py:260
  68.7 0.9 copy-done
  69.6 0.9 copy-done.1
  70.6 0.7 copy-done.2
  71.3 0.7 copy-done.3
  71.9 4.5 %shard_map.85.refs_13_ = f32[12,1024]{1,0:T(8,128)S(1)} custom-call(s32[2]{0:T(128)S(1)} %pad_add_fusion.refs_0_, s32[512]{0:T(512)S(1)} %copy-done.2, s32[512]{0:T(512)S(1)} %copy-done.3, bf16[128,1024]{1,0:T(8,128)(2,1)S(1)} %copy-done, bf16[128,1024]{1,0:T(8,128)(2,1)S(1)} %collective-permute-done.refs_4_, ...), custom_call_target="tpu_custom_call" | custom-call | flops 1073741824 | bytes 4194304 | tf_op jit(solution)/shard_map/pallas_call | solution.py:221
  76.4 0.0 collective-permute-done.12.refs_12_
  76.4 3.5 %shard_map.86.refs_13_ = f32[12,1024]{1,0:T(8,128)S(1)} custom-call(s32[2]{0:T(128)S(1)} %pad_add_fusion.refs_0_, s32[512]{0:T(512)S(1)} %copy-done.2, s32[512]{0:T(512)S(1)} %copy-done.3, bf16[128,1024]{1,0:T(8,128)(2,1)S(1)} %copy-done, bf16[128,1024]{1,0:T(8,128)(2,1)S(1)} %collective-permute-done.refs_4_, ...), custom_call_target="tpu_custom_call" | custom-call | flops 1073741824 | bytes 4194304 | tf_op jit(solution)/shard_map/pallas_call | solution.py:221
  79.9 8.7 %collective-permute-start.15 = (f32[12,1024]{1,0:T(8,128)S(1)}, f32[12,1024]{1,0:T(8,128)S(1)}, u32[]{:S(2)}, u32[]{:S(2)}) collective-permute-start(f32[12,1024]{1,0:T(8,128)S(1)} %shard_map.86.refs_13_), channel_id=1, source_target_pairs={{0,24},{1,25},{2,26},{3,27},{4,28},{5,29},{6,30},{7,31},{8,16},{9,... | collective-permute-start | bytes 147464 | tf_op jit(solution)/shard_map/ppermute | solution.py:260
  88.6 2.2 %collective-permute-start.14 = (f32[12,1024]{1,0:T(8,128)S(1)}, f32[12,1024]{1,0:T(8,128)S(1)}, u32[]{:S(2)}, u32[]{:S(2)}) collective-permute-start(f32[12,1024]{1,0:T(8,128)S(1)} %shard_map.86.refs_13_), channel_id=1, source_target_pairs={{0,16},{1,17},{2,18},{3,19},{4,20},{5,21},{6,22},{7,23},{8,24},{9,... | collective-permute-start | bytes 147464 | tf_op jit(solution)/shard_map/ppermute | solution.py:260
  90.8 2.5 %collective-permute-start.13 = (f32[12,1024]{1,0:T(8,128)S(1)}, f32[12,1024]{1,0:T(8,128)S(1)}, u32[]{:S(2)}, u32[]{:S(2)}) collective-permute-start(f32[12,1024]{1,0:T(8,128)S(1)} %shard_map.86.refs_13_), channel_id=1, source_target_pairs={{0,8},{1,9},{2,10},{3,11},{4,12},{5,13},{6,14},{7,15},{8,0},{9,1},... | collective-permute-start | bytes 147464 | tf_op jit(solution)/shard_map/ppermute | solution.py:260
  93.3 0.0 collective-permute-done.15.refs_16_
  93.3 3.2 %collective-permute-done.14.refs_15_ = f32[12,1024]{1,0:T(8,128)S(1)} collective-permute-done((f32[12,1024]{1,0:T(8,128)S(1)}, f32[12,1024]{1,0:T(8,128)S(1)}, u32[]{:S(2)}, u32[]{:S(2)}) %collective-permute-start.14) | collective-permute-done | bytes 49184 | tf_op jit(solution)/shard_map/ppermute | solution.py:260
  96.5 0.4 collective-permute-done.13.refs_14_
  96.9 4.4 %shard_map.87 = (bf16[1024,128]{1,0:T(8,128)(2,1)S(1)}, bf16[512,128]{1,0:T(8,128)(2,1)S(1)}, bf16[256,128]{1,0:T(8,128)(2,1)S(1)}, bf16[256,128]{1,0:T(8,128)(2,1)S(1)}, f32[512,1024]{1,0:T(8,128)S(1)}) custom-call(s32[2]{0:T(128)S(1)} %pad_add_fusion.refs_0_, s32[512]{0:T(512)S(1)} %copy-done.2, s32[512]{0:T(512)S(1)} %copy-done.3, ...), custom_call_target="tpu_custom_call" | custom-call | flops 2684354560 | bytes 4194304 | tf_op jit(solution)/shard_map/pallas_call | solution.py:248
  101.4 6.2 %shard_map.88 = (bf16[1024,128]{1,0:T(8,128)(2,1)S(1)}, bf16[512,128]{1,0:T(8,128)(2,1)S(1)}, bf16[256,128]{1,0:T(8,128)(2,1)S(1)}, bf16[256,128]{1,0:T(8,128)(2...) custom-call(s32[2]{0:T(128)S(1)} %pad_add_fusion.refs_0_, ...), custom_call_target="tpu_custom_call" | custom-call | flops 2684354560 | bytes 4194304 | tf_op jit(solution)/shard_map/pallas_call | solution.py:248
  107.6 10.6 %collective-permute-start.19 = (bf16[1024,128]{1,0:T(8,128)(2,1)S(1)}, bf16[1024,128]{1,0:T(8,128)(2,1)S(1)}, u32[]{:S(2)}, u32[]{:S(2)}) collective-permute-start(bf16[1024,128]{1,0:T(8,128)(2,1)S(1)} %get-tuple-element.22), channel_id=1, source_target_pairs={{0,1},{1,0},{2,3},{3,2},{4,5},{5,4},{6,7},{7,6},{8,9},{9,8},{10,11... | collective-permute-start | bytes 786440 | tf_op jit(solution)/shard_map/ppermute | solution.py:260
  118.2 1.9 %collective-permute-start.22 = (bf16[1024,128]{1,0:T(8,128)(2,1)S(1)}, bf16[1024,128]{1,0:T(8,128)(2,1)S(1)}, u32[]{:S(2)}, u32[]{:S(2)}) collective-permute-start(bf16[1024,128]{1,0:T(8,128)(2,1)S(1)} %get-tuple-element.26), channel_id=1, source_target_pairs={{0,1},{1,0},{2,3},{3,2},{4,5},{5,4},{6,7},{7,6},{8,9},{9,8},{10,11... | collective-permute-start | bytes 786440 | tf_op jit(solution)/shard_map/ppermute | solution.py:260
  120.1 6.4 %collective-permute-start.16 = (bf16[128,1024]{1,0:T(8,128)(2,1)S(1)}, bf16[128,1024]{1,0:T(8,128)(2,1)S(1)}, u32[]{:S(2)}, u32[]{:S(2)}) collective-permute-start(bf16[128,1024]{1,0:T(8,128)(2,1)S(1)} %get-tuple-element.18), channel_id=1, source_target_pairs={{0,8},{1,9},{2,10},{3,11},{4,12},{5,13},{6,14},{7,15},{8,0},{9,1},... | collective-permute-start | bytes 786440 | tf_op jit(solution)/shard_map/ppermute | solution.py:260
  126.5 4.9 %collective-permute-start.17 = (bf16[128,1024]{1,0:T(8,128)(2,1)S(1)}, bf16[128,1024]{1,0:T(8,128)(2,1)S(1)}, u32[]{:S(2)}, u32[]{:S(2)}) collective-permute-start(bf16[128,1024]{1,0:T(8,128)(2,1)S(1)} %get-tuple-element.19), channel_id=1, source_target_pairs={{0,16},{1,17},{2,18},{3,19},{4,20},{5,21},{6,22},{7,23},{8,24},{9,... | collective-permute-start | bytes 786440 | tf_op jit(solution)/shard_map/ppermute | solution.py:260
  131.5 1.9 %collective-permute-start.18 = (bf16[128,1024]{1,0:T(8,128)(2,1)S(1)}, bf16[128,1024]{1,0:T(8,128)(2,1)S(1)}, u32[]{:S(2)}, u32[]{:S(2)}) collective-permute-start(bf16[128,1024]{1,0:T(8,128)(2,1)S(1)} %get-tuple-element.20), channel_id=1, source_target_pairs={{0,24},{1,25},{2,26},{3,27},{4,28},{5,29},{6,30},{7,31},{8,16},{9,... | collective-permute-start | bytes 786440 | tf_op jit(solution)/shard_map/ppermute | solution.py:260
  133.5 6.2 %collective-permute-start.20 = (bf16[512,128]{1,0:T(8,128)(2,1)S(1)}, bf16[512,128]{1,0:T(8,128)(2,1)S(1)}, u32[]{:S(2)}, u32[]{:S(2)}) collective-permute-start(bf16[512,128]{1,0:T(8,128)(2,1)S(1)} %add_convert_fusion.2), channel_id=1, source_target_pairs={{0,2},{1,3},{2,0},{3,1},{4,6},{5,7},{6,4},{7,5},{8,10},{9,11},{10,... | collective-permute-start | bytes 393224 | tf_op jit(solution)/shard_map/ppermute | solution.py:260
  139.7 1.9 %collective-permute-start.23 = (bf16[512,128]{1,0:T(8,128)(2,1)S(1)}, bf16[512,128]{1,0:T(8,128)(2,1)S(1)}, u32[]{:S(2)}, u32[]{:S(2)}) collective-permute-start(bf16[512,128]{1,0:T(8,128)(2,1)S(1)} %add_convert_fusion.1), channel_id=1, source_target_pairs={{0,2},{1,3},{2,0},{3,1},{4,6},{5,7},{6,4},{7,5},{8,10},{9,11},{10,... | collective-permute-start | bytes 393224 | tf_op jit(solution)/shard_map/ppermute | solution.py:260
  141.7 5.8 %collective-permute-done.20 = bf16[512,128]{1,0:T(8,128)(2,1)S(1)} collective-permute-done((bf16[512,128]{1,0:T(8,128)(2,1)S(1)}, bf16[512,128]{1,0:T(8,128)(2,1)S(1)}, u32[]{:S(2)}, u32[]{:S(2)}) %collective-permute-start.20) | collective-permute-done | bytes 131104 | tf_op jit(solution)/shard_map/ppermute | solution.py:260
  147.5 1.9 %collective-permute-start.21 = (bf16[256,128]{1,0:T(8,128)(2,1)S(1)}, bf16[256,128]{1,0:T(8,128)(2,1)S(1)}, u32[]{:S(2)}, u32[]{:S(2)}) collective-permute-start(bf16[256,128]{1,0:T(8,128)(2,1)S(1)} %add_convert_fusion.6), channel_id=1, source_target_pairs={{0,4},{1,5},{2,6},{3,7},{4,0},{5,1},{6,2},{7,3},{8,12},{9,13},{10,... | collective-permute-start | bytes 196616 | tf_op jit(solution)/shard_map/ppermute | solution.py:260
  149.4 0.8 collective-permute-done.23
  150.3 0.1 add_convert_fusion.5
  150.4 1.9 %collective-permute-start.24 = (bf16[256,128]{1,0:T(8,128)(2,1)S(1)}, bf16[256,128]{1,0:T(8,128)(2,1)S(1)}, u32[]{:S(2)}, u32[]{:S(2)}) collective-permute-start(bf16[256,128]{1,0:T(8,128)(2,1)S(1)} %get-tuple-element.29), channel_id=1, source_target_pairs={{32,0},{33,1},{34,2},{35,3},{36,4},{37,5},{38,6},{39,7},{40,8},{41... | collective-permute-start | bytes 196616 | tf_op jit(solution)/shard_map/ppermute | solution.py:271
  152.3 1.9 %collective-permute-start.25 = (bf16[256,128]{1,0:T(8,128)(2,1)S(1)}, bf16[256,128]{1,0:T(8,128)(2,1)S(1)}, u32[]{:S(2)}, u32[]{:S(2)}) collective-permute-start(bf16[256,128]{1,0:T(8,128)(2,1)S(1)} %get-tuple-element.30), channel_id=1, source_target_pairs={{32,4},{33,5},{34,6},{35,7},{36,0},{37,1},{38,2},{39,3},{40,12},{4... | collective-permute-start | bytes 196616 | tf_op jit(solution)/shard_map/ppermute | solution.py:271
  154.2 0.0 collective-permute-done.17
  154.2 0.0 collective-permute-done.18
  154.2 0.9 add_convert_fusion
  155.1 4.4 %collective-permute-done.21 = bf16[256,128]{1,0:T(8,128)(2,1)S(1)} collective-permute-done((bf16[256,128]{1,0:T(8,128)(2,1)S(1)}, bf16[256,128]{1,0:T(8,128)(2,1)S(1)}, u32[]{:S(2)}, u32[]{:S(2)}) %collective-permute-start.21) | collective-permute-done | bytes 65568 | tf_op jit(solution)/shard_map/ppermute | solution.py:260
  159.5 5.1 %collective-permute-done.25 = bf16[256,128]{1,0:T(8,128)(2,1)S(1)} collective-permute-done((bf16[256,128]{1,0:T(8,128)(2,1)S(1)}, bf16[256,128]{1,0:T(8,128)(2,1)S(1)}, u32[]{:S(2)}, u32[]{:S(2)}) %collective-permute-start.25) | collective-permute-done | bytes 65568 | tf_op jit(solution)/shard_map/ppermute | solution.py:271
  164.6 0.1 add_convert_fusion.3
  164.7 0.6 fusion
  (17 shorter events, 0.2 us)
Async XLA Ops:
  2.2 27.2 %collective-permute-start.10 = (bf16[256,128]{1,0:T(8,128)(2,1)S(1)}, bf16[256,128]{1,0:T(8,128)(2,1)S(1)}, u32[]{:S(2)}, u32[]{:S(2)}) collective-permute-start(bf16[256,128]{1,0:T(8,128)(2,1)S(1)} %get-tuple-element.33), channel_id=1, source_target_pairs={{0,36},{1,37},{2,38},{3,39},{4,32},{5,33},{6,34},{7,35},{8,44},{9,... | collective-permute-start | bytes 196616 | tf_op jit(solution)/shard_map/ppermute | solution.py:271
  10.7 21.7 %collective-permute-start.9 = (bf16[256,128]{1,0:T(8,128)(2,1)S(1)}, bf16[256,128]{1,0:T(8,128)(2,1)S(1)}, u32[]{:S(2)}, u32[]{:S(2)}) collective-permute-start(bf16[256,128]{1,0:T(8,128)(2,1)S(1)} %get-tuple-element.33), channel_id=1, source_target_pairs={{0,32},{1,33},{2,34},{3,35},{4,36},{5,37},{6,38},{7,39},{8,40},{9,... | collective-permute-start | bytes 196616 | tf_op jit(solution)/shard_map/ppermute | solution.py:271
  17.0 43.7 %collective-permute-start.2 = (bf16[128,1024]{1,0:T(8,128)(2,1)}, bf16[128,1024]{1,0:T(8,128)(2,1)S(1)}, u32[]{:S(2)}, u32[]{:S(2)}) collective-permute-start(bf16[128,1024]{1,0:T(8,128)(2,1)} %refs_3_.7), channel_id=1, source_target_pairs={{0,24},{1,25},{2,26},{3,27},{4,28},{5,29},{6,30},{7,31},{8,16},{9,... | collective-permute-start | bytes 786440 | tf_op jit(solution)/shard_map/ppermute | solution.py:260
  21.9 32.7 %collective-permute-start = (bf16[128,1024]{1,0:T(8,128)(2,1)}, bf16[128,1024]{1,0:T(8,128)(2,1)S(1)}, u32[]{:S(2)}, u32[]{:S(2)}) collective-permute-start(bf16[128,1024]{1,0:T(8,128)(2,1)} %refs_3_.7), channel_id=1, source_target_pairs={{0,8},{1,9},{2,10},{3,11},{4,12},{5,13},{6,14},{7,15},{8,0},{9,1},... | collective-permute-start | bytes 786440 | tf_op jit(solution)/shard_map/ppermute | solution.py:260
  23.9 12.2 %collective-permute-start.6 = (bf16[256,128]{1,0:T(8,128)(2,1)S(1)}, bf16[256,128]{1,0:T(8,128)(2,1)S(1)}, u32[]{:S(2)}, u32[]{:S(2)}) collective-permute-start(bf16[256,128]{1,0:T(8,128)(2,1)S(1)} %get-tuple-element.33), channel_id=1, source_target_pairs={{0,4},{1,5},{2,6},{3,7},{4,0},{5,1},{6,2},{7,3},{8,12},{9,13},{10,... | collective-permute-start | bytes 196616 | tf_op jit(solution)/shard_map/ppermute | solution.py:260
  29.4 29.0 %collective-permute-start.4 = (bf16[128,1024]{1,0:T(8,128)(2,1)}, bf16[128,1024]{1,0:T(8,128)(2,1)S(1)}, u32[]{:S(2)}, u32[]{:S(2)}) collective-permute-start(bf16[128,1024]{1,0:T(8,128)(2,1)} %refs_7_.7), channel_id=1, source_target_pairs={{0,24},{1,25},{2,26},{3,27},{4,28},{5,29},{6,30},{7,31},{8,16},{9,... | collective-permute-start | bytes 786440 | tf_op jit(solution)/shard_map/ppermute | solution.py:260
  32.4 20.2 %collective-permute-start.11 = (bf16[512,128]{1,0:T(8,128)(2,1)S(1)}, bf16[512,128]{1,0:T(8,128)(2,1)S(1)}, u32[]{:S(2)}, u32[]{:S(2)}) collective-permute-start(bf16[512,128]{1,0:T(8,128)(2,1)S(1)} %pad_maximum_fusion.1), channel_id=1, source_target_pairs={{0,2},{1,3},{2,0},{3,1},{4,6},{5,7},{6,4},{7,5},{8,10},{9,11},{10,... | collective-permute-start | bytes 393224 | tf_op jit(solution)/shard_map/ppermute | solution.py:260
  36.9 12.3 %collective-permute-start.7 = (bf16[512,128]{1,0:T(8,128)(2,1)S(1)}, bf16[512,128]{1,0:T(8,128)(2,1)S(1)}, u32[]{:S(2)}, u32[]{:S(2)}) collective-permute-start(bf16[512,128]{1,0:T(8,128)(2,1)S(1)} %pad_maximum_fusion), channel_id=1, source_target_pairs={{0,2},{1,3},{2,0},{3,1},{4,6},{5,7},{6,4},{7,5},{8,10},{9,11},{10,... | collective-permute-start | bytes 393224 | tf_op jit(solution)/shard_map/ppermute | solution.py:260
  49.2 15.4 %collective-permute-start.3 = (bf16[128,1024]{1,0:T(8,128)(2,1)}, bf16[128,1024]{1,0:T(8,128)(2,1)S(1)}, u32[]{:S(2)}, u32[]{:S(2)}) collective-permute-start(bf16[128,1024]{1,0:T(8,128)(2,1)} %refs_7_.7), channel_id=1, source_target_pairs={{0,8},{1,9},{2,10},{3,11},{4,12},{5,13},{6,14},{7,15},{8,0},{9,1},... | collective-permute-start | bytes 786440 | tf_op jit(solution)/shard_map/ppermute | solution.py:260
  52.6 12.0 %collective-permute-start.8 = (bf16[1024,128]{1,0:T(8,128)(2,1)S(1)}, bf16[1024,128]{1,0:T(8,128)(2,1)S(1)}, u32[]{:S(2)}, u32[]{:S(2)}) collective-permute-start(bf16[1024,128]{1,0:T(8,128)(2,1)S(1)} %constant_dynamic-update-slice_fusion.2.refs_11_), channel_id=1, source_target_pairs={{0,1},{1,0},{2,3},{3,2},{4,5},{5,4},{6,7},{7,6},{8,9},{9,8},{10,11... | collective-permute-start | bytes 786440 | tf_op jit(solution)/shard_map/ppermute | solution.py:260
  54.6 11.3 %collective-permute-start.1 = (bf16[128,1024]{1,0:T(8,128)(2,1)S(1)}, bf16[128,1024]{1,0:T(8,128)(2,1)S(1)}, u32[]{:S(2)}, u32[]{:S(2)}) collective-permute-start(bf16[128,1024]{1,0:T(8,128)(2,1)S(1)} %collective-permute-done.refs_4_), channel_id=1, source_target_pairs={{0,24},{1,25},{2,26},{3,27},{4,28},{5,29},{6,30},{7,31},{8,16},{9,... | collective-permute-start | bytes 786440 | tf_op jit(solution)/shard_map/ppermute | solution.py:260
  58.4 10.3 %collective-permute-start.5 = (bf16[128,1024]{1,0:T(8,128)(2,1)S(1)}, bf16[128,1024]{1,0:T(8,128)(2,1)S(1)}, u32[]{:S(2)}, u32[]{:S(2)}) collective-permute-start(bf16[128,1024]{1,0:T(8,128)(2,1)S(1)} %collective-permute-done.4.refs_10_), channel_id=1, source_target_pairs={{0,8},{1,9},{2,10},{3,11},{4,12},{5,13},{6,14},{7,15},{8,0},{9,1},... | collective-permute-start | bytes 786440 | tf_op jit(solution)/shard_map/ppermute | solution.py:260
  60.6 15.8 %collective-permute-start.12 = (bf16[1024,128]{1,0:T(8,128)(2,1)S(1)}, bf16[1024,128]{1,0:T(8,128)(2,1)S(1)}, u32[]{:S(2)}, u32[]{:S(2)}) collective-permute-start(bf16[1024,128]{1,0:T(8,128)(2,1)S(1)} %constant_dynamic-update-slice_fusion.6.refs_11_), channel_id=1, source_target_pairs={{0,1},{1,0},{2,3},{3,2},{4,5},{5,4},{6,7},{7,6},{8,9},{9,8},{10,11... | collective-permute-start | bytes 786440 | tf_op jit(solution)/shard_map/ppermute | solution.py:260
  68.7 1.0 copy-start
  69.6 0.9 copy-start.1
  70.6 0.7 copy-start.2
  71.3 0.7 copy-start.3
  79.9 13.4 %collective-permute-start.15 = (f32[12,1024]{1,0:T(8,128)S(1)}, f32[12,1024]{1,0:T(8,128)S(1)}, u32[]{:S(2)}, u32[]{:S(2)}) collective-permute-start(f32[12,1024]{1,0:T(8,128)S(1)} %shard_map.86.refs_13_), channel_id=1, source_target_pairs={{0,24},{1,25},{2,26},{3,27},{4,28},{5,29},{6,30},{7,31},{8,16},{9,... | collective-permute-start | bytes 147464 | tf_op jit(solution)/shard_map/ppermute | solution.py:260
  88.6 7.9 %collective-permute-start.14 = (f32[12,1024]{1,0:T(8,128)S(1)}, f32[12,1024]{1,0:T(8,128)S(1)}, u32[]{:S(2)}, u32[]{:S(2)}) collective-permute-start(f32[12,1024]{1,0:T(8,128)S(1)} %shard_map.86.refs_13_), channel_id=1, source_target_pairs={{0,16},{1,17},{2,18},{3,19},{4,20},{5,21},{6,22},{7,23},{8,24},{9,... | collective-permute-start | bytes 147464 | tf_op jit(solution)/shard_map/ppermute | solution.py:260
  90.8 6.2 %collective-permute-start.13 = (f32[12,1024]{1,0:T(8,128)S(1)}, f32[12,1024]{1,0:T(8,128)S(1)}, u32[]{:S(2)}, u32[]{:S(2)}) collective-permute-start(f32[12,1024]{1,0:T(8,128)S(1)} %shard_map.86.refs_13_), channel_id=1, source_target_pairs={{0,8},{1,9},{2,10},{3,11},{4,12},{5,13},{6,14},{7,15},{8,0},{9,1},... | collective-permute-start | bytes 147464 | tf_op jit(solution)/shard_map/ppermute | solution.py:260
  107.6 25.9 %collective-permute-start.19 = (bf16[1024,128]{1,0:T(8,128)(2,1)S(1)}, bf16[1024,128]{1,0:T(8,128)(2,1)S(1)}, u32[]{:S(2)}, u32[]{:S(2)}) collective-permute-start(bf16[1024,128]{1,0:T(8,128)(2,1)S(1)} %get-tuple-element.22), channel_id=1, source_target_pairs={{0,1},{1,0},{2,3},{3,2},{4,5},{5,4},{6,7},{7,6},{8,9},{9,8},{10,11... | collective-permute-start | bytes 786440 | tf_op jit(solution)/shard_map/ppermute | solution.py:260
  118.2 21.5 %collective-permute-start.22 = (bf16[1024,128]{1,0:T(8,128)(2,1)S(1)}, bf16[1024,128]{1,0:T(8,128)(2,1)S(1)}, u32[]{:S(2)}, u32[]{:S(2)}) collective-permute-start(bf16[1024,128]{1,0:T(8,128)(2,1)S(1)} %get-tuple-element.26), channel_id=1, source_target_pairs={{0,1},{1,0},{2,3},{3,2},{4,5},{5,4},{6,7},{7,6},{8,9},{9,8},{10,11... | collective-permute-start | bytes 786440 | tf_op jit(solution)/shard_map/ppermute | solution.py:260
  120.1 32.2 %collective-permute-start.16 = (bf16[128,1024]{1,0:T(8,128)(2,1)S(1)}, bf16[128,1024]{1,0:T(8,128)(2,1)S(1)}, u32[]{:S(2)}, u32[]{:S(2)}) collective-permute-start(bf16[128,1024]{1,0:T(8,128)(2,1)S(1)} %get-tuple-element.18), channel_id=1, source_target_pairs={{0,8},{1,9},{2,10},{3,11},{4,12},{5,13},{6,14},{7,15},{8,0},{9,1},... | collective-permute-start | bytes 786440 | tf_op jit(solution)/shard_map/ppermute | solution.py:260
  126.5 27.7 %collective-permute-start.17 = (bf16[128,1024]{1,0:T(8,128)(2,1)S(1)}, bf16[128,1024]{1,0:T(8,128)(2,1)S(1)}, u32[]{:S(2)}, u32[]{:S(2)}) collective-permute-start(bf16[128,1024]{1,0:T(8,128)(2,1)S(1)} %get-tuple-element.19), channel_id=1, source_target_pairs={{0,16},{1,17},{2,18},{3,19},{4,20},{5,21},{6,22},{7,23},{8,24},{9,... | collective-permute-start | bytes 786440 | tf_op jit(solution)/shard_map/ppermute | solution.py:260
  131.5 22.7 %collective-permute-start.18 = (bf16[128,1024]{1,0:T(8,128)(2,1)S(1)}, bf16[128,1024]{1,0:T(8,128)(2,1)S(1)}, u32[]{:S(2)}, u32[]{:S(2)}) collective-permute-start(bf16[128,1024]{1,0:T(8,128)(2,1)S(1)} %get-tuple-element.20), channel_id=1, source_target_pairs={{0,24},{1,25},{2,26},{3,27},{4,28},{5,29},{6,30},{7,31},{8,16},{9,... | collective-permute-start | bytes 786440 | tf_op jit(solution)/shard_map/ppermute | solution.py:260
  133.5 14.0 %collective-permute-start.20 = (bf16[512,128]{1,0:T(8,128)(2,1)S(1)}, bf16[512,128]{1,0:T(8,128)(2,1)S(1)}, u32[]{:S(2)}, u32[]{:S(2)}) collective-permute-start(bf16[512,128]{1,0:T(8,128)(2,1)S(1)} %add_convert_fusion.2), channel_id=1, source_target_pairs={{0,2},{1,3},{2,0},{3,1},{4,6},{5,7},{6,4},{7,5},{8,10},{9,11},{10,... | collective-permute-start | bytes 393224 | tf_op jit(solution)/shard_map/ppermute | solution.py:260
  139.7 10.5 %collective-permute-start.23 = (bf16[512,128]{1,0:T(8,128)(2,1)S(1)}, bf16[512,128]{1,0:T(8,128)(2,1)S(1)}, u32[]{:S(2)}, u32[]{:S(2)}) collective-permute-start(bf16[512,128]{1,0:T(8,128)(2,1)S(1)} %add_convert_fusion.1), channel_id=1, source_target_pairs={{0,2},{1,3},{2,0},{3,1},{4,6},{5,7},{6,4},{7,5},{8,10},{9,11},{10,... | collective-permute-start | bytes 393224 | tf_op jit(solution)/shard_map/ppermute | solution.py:260
  147.5 12.0 %collective-permute-start.21 = (bf16[256,128]{1,0:T(8,128)(2,1)S(1)}, bf16[256,128]{1,0:T(8,128)(2,1)S(1)}, u32[]{:S(2)}, u32[]{:S(2)}) collective-permute-start(bf16[256,128]{1,0:T(8,128)(2,1)S(1)} %add_convert_fusion.6), channel_id=1, source_target_pairs={{0,4},{1,5},{2,6},{3,7},{4,0},{5,1},{6,2},{7,3},{8,12},{9,13},{10,... | collective-permute-start | bytes 196616 | tf_op jit(solution)/shard_map/ppermute | solution.py:260
  150.4 9.2 %collective-permute-start.24 = (bf16[256,128]{1,0:T(8,128)(2,1)S(1)}, bf16[256,128]{1,0:T(8,128)(2,1)S(1)}, u32[]{:S(2)}, u32[]{:S(2)}) collective-permute-start(bf16[256,128]{1,0:T(8,128)(2,1)S(1)} %get-tuple-element.29), channel_id=1, source_target_pairs={{32,0},{33,1},{34,2},{35,3},{36,4},{37,5},{38,6},{39,7},{40,8},{41... | collective-permute-start | bytes 196616 | tf_op jit(solution)/shard_map/ppermute | solution.py:271
  152.3 12.3 %collective-permute-start.25 = (bf16[256,128]{1,0:T(8,128)(2,1)S(1)}, bf16[256,128]{1,0:T(8,128)(2,1)S(1)}, u32[]{:S(2)}, u32[]{:S(2)}) collective-permute-start(bf16[256,128]{1,0:T(8,128)(2,1)S(1)} %get-tuple-element.30), channel_id=1, source_target_pairs={{32,4},{33,5},{34,6},{35,7},{36,0},{37,1},{38,2},{39,3},{40,12},{4... | collective-permute-start | bytes 196616 | tf_op jit(solution)/shard_map/ppermute | solution.py:271

commit v2 on v1

v2 whole, which is shorter than its diff:
```python
import functools

import jax
import jax.numpy as jnp
from jax import lax
from jax.experimental import pallas as pl
from jax.experimental.pallas import tpu as pltpu
from jax.sharding import PartitionSpec as P

BLOCK = 128
HD = 128
HEADS = 8
ROWS = HEADS * BLOCK
GROUP = 32
BLOCKS = 512
FIRST = 4
SECOND = 3
NY = 4
NZ = 8
CHUNK = 256
NEG = -1e30
SCALE = HD**-0.5
SCALE2 = SCALE * 1.4426950408889634
VMEM_LIMIT = 40 * 1024 * 1024


def dot_nt(a, b):
    return lax.dot_general(a, b, (((1,), (1,)), ((), ())), preferred_element_type=jnp.float32)


def dot_nn(a, b):
    return lax.dot_general(a, b, (((1,), (0,)), ((), ())), preferred_element_type=jnp.float32)


def dot_tn(a, b):
    return lax.dot_general(a, b, (((0,), (0,)), ((), ())), preferred_element_type=jnp.float32)


def stack_heads(refs, qs, gs):
    for r, ref in enumerate(refs):
        for h in range(HEADS):
            to = r * ROWS + h * BLOCK
            qs[to : to + BLOCK, :] = ref[0:BLOCK, h * HD : (h + 1) * HD]
            gs[to : to + BLOCK, :] = ref[BLOCK : 2 * BLOCK, h * HD : (h + 1) * HD]


def place(low, high, target):
    pair = 4 * BLOCK
    for half, ref in enumerate((low, high)):
        for quarter in range(2):
            for before in range(2):
                lo = (2 * quarter + before) * pair
                to = (4 * before + 2 * half + quarter) * pair
                target[to : to + pair, :] = ref[lo : lo + pair, :]


def pair_visible(meta, before, r, s):
    outer, inner = meta[2 * BLOCKS], meta[2 * BLOCKS + 1]
    tail = (s & 2) | ((s >> 2) & 1)
    q_pos = meta[BLOCKS + outer * GROUP + (inner ^ (r * NZ))]
    if before:
        flip = jnp.where((s & 1) == 0, FIRST, SECOND) ^ tail
        k_pos = meta[BLOCKS + jnp.maximum(outer - 1, 0) * GROUP + (inner ^ flip)]
        return (outer > 0) & (meta[q_pos] == meta[k_pos])
    flip = ((s & 1) << 2) | tail
    k_pos = meta[BLOCKS + outer * GROUP + (inner ^ flip)]
    return (meta[q_pos] == meta[k_pos]) & (k_pos < q_pos)


def diagonal_mask():
    k_at = lax.broadcasted_iota(jnp.int32, (BLOCK, CHUNK), 0)
    q_at = lax.broadcasted_iota(jnp.int32, (BLOCK, CHUNK), 1) % BLOCK
    return k_at <= q_at


def for_pairs(meta, pair):
    pair(0, 0, True)

    @pl.loop(1, NY * NZ)
    def _(step):
        r = step // NZ
        s = step % NZ

        @pl.when(pair_visible(meta, False, r, s))
        def _():
            pair(r, s, False)

    @pl.loop(0, NY * NZ)
    def _(step):
        r = step // NZ
        s = step % NZ

        @pl.when(pair_visible(meta, True, r, s))
        def _():
            pair(r, s + NZ, False)


def stats_kernel(meta, qg0, qg1, qg2, qg3, low, high, stats, qs, gs, kv):
    stack_heads((qg0, qg1, qg2, qg3), qs, gs)
    place(low, high, kv)
    stats[0:NY, :] = jnp.full((NY, ROWS), NEG, jnp.float32)
    stats[NY : 3 * NY, :] = jnp.zeros((2 * NY, ROWS), jnp.float32)

    def pair(r, s, diagonal):
        key = kv[pl.ds(s * 2 * BLOCK, BLOCK), :]
        value = kv[pl.ds(s * 2 * BLOCK + BLOCK, BLOCK), :]
        for c in range(ROWS // CHUNK):
            rows = pl.ds(r * ROWS + c * CHUNK, CHUNK)
            cols = pl.ds(c * CHUNK, CHUNK)
            scores = dot_nt(key, qs[rows, :]) * SCALE2
            dprob = dot_nt(value, gs[rows, :])
            if diagonal:
                scores = jnp.where(diagonal_mask(), scores, NEG)
            top = stats[pl.ds(r, 1), cols]
            new_top = jnp.maximum(top, jnp.max(scores, axis=0, keepdims=True))
            factor = jnp.exp2(top - new_top)
            weights = jnp.exp2(scores - new_top)
            stats[pl.ds(r, 1), cols] = new_top
            stats[pl.ds(NY + r, 1), cols] = stats[pl.ds(NY + r, 1), cols] * factor + jnp.sum(
                weights, axis=0, keepdims=True
            )
            stats[pl.ds(2 * NY + r, 1), cols] = stats[
                pl.ds(2 * NY + r, 1), cols
            ] * factor + jnp.sum(weights * dprob, axis=0, keepdims=True)

    for_pairs(meta, pair)


def grads_kernel(meta, qg0, qg1, qg2, qg3, low, high, st0, st1, st2, st3, *rest):
    out_high, out_mid, own_one, own_zero, before_one, before_zero = rest[:6]
    dq_outs = rest[6:10]
    qs, gs, kv, lse, delta, w_low, d_low, dkv, dq = rest[10:]
    stat_refs = (st0, st1, st2, st3)
    stack_heads((qg0, qg1, qg2, qg3), qs, gs)
    place(low, high, kv)
    dkv[...] = jnp.zeros_like(dkv)
    dq[...] = jnp.zeros_like(dq)
    for r in range(NY):
        tops = [stat_refs[k][(r ^ k) : (r ^ k) + 1, :] for k in range(NY)]
        top = functools.reduce(jnp.maximum, tops)
        total = jnp.zeros_like(top)
        product = jnp.zeros_like(top)
        for k in range(NY):
            factor = jnp.exp2(tops[k] - top)
            at = r ^ k
            total = total + stat_refs[k][NY + at : NY + at + 1, :] * factor
            product = product + stat_refs[k][2 * NY + at : 2 * NY + at + 1, :] * factor
        lse[r : r + 1, :] = top + jnp.log2(total)
        delta[r : r + 1, :] = product / total

    def pair(r, s, diagonal):
        key = kv[pl.ds(s * 2 * BLOCK, BLOCK), :]
        value = kv[pl.ds(s * 2 * BLOCK + BLOCK, BLOCK), :]
        for c in range(ROWS // CHUNK):
            rows = pl.ds(r * ROWS + c * CHUNK, CHUNK)
            cols = pl.ds(c * CHUNK, CHUNK)
            scores = dot_nt(key, qs[rows, :]) * SCALE2
            dprob = dot_nt(value, gs[rows, :])
            probs = jnp.exp2(scores - lse[pl.ds(r, 1), cols])
            if diagonal:
                probs = jnp.where(diagonal_mask(), probs, 0.0)
            w_low[:, cols] = probs.astype(jnp.bfloat16)
            d_low[:, cols] = (probs * (dprob - delta[pl.ds(r, 1), cols])).astype(jnp.bfloat16)
        rows = pl.ds(r * ROWS, ROWS)
        dkv[pl.ds(s * 2 * BLOCK, BLOCK), :] += dot_nn(d_low[...], qs[rows, :])
        dkv[pl.ds(s * 2 * BLOCK + BLOCK, BLOCK), :] += dot_nn(w_low[...], gs[rows, :])
        dq[pl.ds(r * HD, HD), :] += dot_tn(key, d_low[...])

    for_pairs(meta, pair)

    def write(slots, out, at):
        for s in slots:
            lo = s * 2 * BLOCK
            out[at : at + BLOCK, :] = (dkv[lo : lo + BLOCK, :] * SCALE).astype(jnp.bfloat16)
            out[at + BLOCK : at + 2 * BLOCK, :] = dkv[lo + BLOCK : lo + 2 * BLOCK, :].astype(
                jnp.bfloat16
            )
            at += 2 * BLOCK

    write((4, 5, NZ + 4, NZ + 5, 6, 7, NZ + 6, NZ + 7), out_high, 0)
    write((2, 3, NZ + 2, NZ + 3), out_mid, 0)
    write((1,), own_one, 0)
    write((0,), own_zero, 0)
    write((NZ + 1,), before_one, 0)
    write((NZ,), before_zero, 0)
    for r in range(NY):
        for h in range(HEADS):
            part = dq[r * HD : (r + 1) * HD, h * BLOCK : (h + 1) * BLOCK] * SCALE
            dq_outs[r][:, h * HD : (h + 1) * HD] = part.astype(jnp.bfloat16).T


def smem():
    return pl.BlockSpec(memory_space=pltpu.SMEM)


def vmem():
    return pl.BlockSpec(memory_space=pltpu.VMEM)


def common_scratch():
    return [
        pltpu.VMEM((NY * ROWS, HD), jnp.bfloat16),
        pltpu.VMEM((NY * ROWS, HD), jnp.bfloat16),
        pltpu.VMEM((2 * NZ * 2 * BLOCK, HD), jnp.bfloat16),
    ]


def cost(matmuls, pairs):
    return pl.CostEstimate(
        flops=matmuls * pairs * 2 * ROWS * BLOCK * HD,
        bytes_accessed=4 * 1024 * 1024,
        transcendentals=pairs * ROWS * BLOCK,
    )


def run_stats(*args):
    return pl.pallas_call(
        stats_kernel,
        out_shape=jax.ShapeDtypeStruct((3 * NY, ROWS), jnp.float32),
        in_specs=[smem()] + [vmem()] * (len(args) - 1),
        out_specs=vmem(),
        scratch_shapes=common_scratch(),
        compiler_params=pltpu.CompilerParams(vmem_limit_bytes=VMEM_LIMIT),
        cost_estimate=cost(2, 20),
    )(*args)


def run_grads(*args):
    outs = [jax.ShapeDtypeStruct((n * 2 * BLOCK, HD), jnp.bfloat16) for n in (8, 4, 1, 1, 1, 1)]
    outs += [jax.ShapeDtypeStruct((BLOCK, HEADS * HD), jnp.bfloat16)] * NY
    return pl.pallas_call(
        grads_kernel,
        out_shape=outs,
        in_specs=[smem()] + [vmem()] * (len(args) - 1),
        out_specs=[vmem()] * len(outs),
        scratch_shapes=common_scratch()
        + [
            pltpu.VMEM((NY, ROWS), jnp.float32),
            pltpu.VMEM((NY, ROWS), jnp.float32),
            pltpu.VMEM((BLOCK, ROWS), jnp.bfloat16),
            pltpu.VMEM((BLOCK, ROWS), jnp.bfloat16),
            pltpu.VMEM((2 * NZ * 2 * BLOCK, HD), jnp.float32),
            pltpu.VMEM((NY * HD, ROWS), jnp.float32),
        ],
        compiler_params=pltpu.CompilerParams(vmem_limit_bytes=VMEM_LIMIT),
        cost_estimate=cost(5, 20),
    )(*args)


def swap(array, flip):
    return lax.ppermute(array, "inner", [(i, i ^ flip) for i in range(GROUP)])


def across(array, by, flip):
    outer = lax.axis_size("outer")
    pairs = [
        (o * GROUP + i, (o + by) * GROUP + (i ^ flip))
        for o in range(outer)
        if 0 <= o + by < outer
        for i in range(GROUP)
    ]
    return lax.ppermute(array, ("outer", "inner"), pairs)


def add_low(*terms):
    total = terms[0].astype(jnp.float32)
    for term in terms[1:]:
        total = total + term.astype(jnp.float32)
    return total.astype(jnp.bfloat16)


def shards(queries, keys, values, grad_out, doc_ids, block_order):
    one = 2 * BLOCK
    ids = jnp.stack([lax.axis_index("outer"), lax.axis_index("inner")]).astype(jnp.int32)
    meta = jnp.concatenate([doc_ids, block_order, ids])
    own = jnp.concatenate([keys, values], axis=0)
    qg0 = jnp.concatenate([queries, grad_out], axis=0)

    before_a = across(own, 1, FIRST)
    before_b = across(own, 1, SECOND)
    own4 = swap(own, 4)
    qg2 = swap(qg0, 2 * NZ)
    qg1 = swap(qg0, NZ)
    qg3 = swap(qg0, 3 * NZ)
    quad = jnp.concatenate([own, own4, before_a, before_b], axis=0)
    low = jnp.concatenate([quad, swap(quad, 2)], axis=0)
    high = swap(low, 1)
    inputs = (meta, qg0, qg1, qg2, qg3, low, high)

    stats = run_stats(*inputs)
    all_stats = (stats, swap(stats, NZ), swap(stats, 2 * NZ), swap(stats, 3 * NZ))
    d_high, d_mid, own_one, own_zero, before_one, before_zero, dq0, dq1, dq2, dq3 = run_grads(
        *inputs, *all_stats
    )

    near = swap(d_high, 1)
    e2 = swap(dq2, 2 * NZ)
    e1 = swap(dq1, NZ)
    e3 = swap(dq3, 3 * NZ)
    far = swap(add_low(d_mid, near[4 * one :]), 2)
    back_a = across(add_low(before_zero, near[2 * one : 3 * one], far[2 * one : 3 * one]), -1, FIRST)
    back_b = across(add_low(before_one, near[3 * one : 4 * one], far[3 * one :]), -1, SECOND)
    own_far = swap(add_low(own_one, near[one : 2 * one], far[one : 2 * one]), 4)
    grad_queries = add_low(dq0, e1, e2, e3)
    totals = add_low(own_zero, near[:one], far[:one], own_far, back_a, back_b)
    return grad_queries, totals[:BLOCK], totals[BLOCK:]


def solution(mesh):
    rows = P(("outer", "inner"), None)
    return jax.shard_map(
        shards,
        mesh=mesh,
        in_specs=(rows, rows, rows, rows, P(), P()),
        out_specs=(rows, rows, rows),
        check_vma=False,
    )
```

time: 166 us -> 162 us (0.976)
  the two profiles are of different devices: /device:TPU:4 before, /device:TPU:67 now
where the time goes in v2:
time: 162 us; the launch traced here: 161 us
  starting transfers between devices  81.5 us (50%)
  waiting for transfers between devices  51.8 us (32%)
  Pallas kernels  23.3 us (14%)
  local copies, waits for them, and re-layouts  2.36 us (1%)
    ppermute x15, starting transfers between devices, swap(): return lax.ppermute(array, 'inner', [(i, i ^ flip) for i in range(GROUP)])  66.5 us
    ppermute x15, waiting for transfers between devices, swap(): return lax.ppermute(array, 'inner', [(i, i ^ flip) for i in range(GROUP)])  32.6 us
    ppermute x4, waiting for transfers between devices, across(): return lax.ppermute(array, ('outer', 'inner'), pairs)  19.2 us
    ppermute x4, starting transfers between devices, across(): return lax.ppermute(array, ('outer', 'inner'), pairs)  15 us
    pallas_call x1, Pallas kernels, run_grads(): pl.pallas_call(grads_kernel, out_shape=outs, in_specs=[smem()] + [vmem()]...  13.5 us
    pallas_call x1, Pallas kernels, run_stats(): pl.pallas_call(stats_kernel, out_shape=jax.ShapeDtypeStruct((3 * NY, ROWS...  9.77 us
  transfers between devices with their start and end apart: 19, of which 7 were waited for; matrix products, arithmetic and copies ran while one was open for 1% of the time, Pallas kernels for 0%

profile of v2, /device:TPU:67, one launch (start us, length us, event | category | flops | bytes accessed | tf_op | source)
XLA Modules:
  0.0 161.0 jit_solution(9449399995254734595)
XLA Ops:
  0.6 0.0 copy-start.2
  0.6 0.8 constant_dynamic-update-slice_fusion.8
  1.4 0.0 copy-done.2
  1.5 8.8 %collective-permute-start.3 = (bf16[256,128]{1,0:T(8,128)(2,1)S(1)}, bf16[256,128]{1,0:T(8,128)(2,1)S(1)}, u32[]{:S(2)}, u32[]{:S(2)}) collective-permute-start(bf16[256,128]{1,0:T(8,128)(2,1)S(1)} %get-tuple-element.35), channel_id=1, source_target_pairs={{0,4},{1,5},{2,6},{3,7},{4,0},{5,1},{6,2},{7,3},{8,12},{9,13},{10,... | collective-permute-start | bytes 196616 | tf_op jit(solution)/shard_map/ppermute | solution.py:251
  10.3 9.2 %collective-permute-start.5 = (bf16[256,128]{1,0:T(8,128)(2,1)S(1)}, bf16[256,128]{1,0:T(8,128)(2,1)S(1)}, u32[]{:S(2)}, u32[]{:S(2)}) collective-permute-start(bf16[256,128]{1,0:T(8,128)(2,1)S(1)} %get-tuple-element.35), channel_id=1, source_target_pairs={{0,35},{1,34},{2,33},{3,32},{4,39},{5,38},{6,37},{7,36},{8,43},{9,... | collective-permute-start | bytes 196616 | tf_op jit(solution)/shard_map/ppermute | solution.py:262
  19.5 1.9 %collective-permute-start.4 = (bf16[256,128]{1,0:T(8,128)(2,1)S(1)}, bf16[256,128]{1,0:T(8,128)(2,1)S(1)}, u32[]{:S(2)}, u32[]{:S(2)}) collective-permute-start(bf16[256,128]{1,0:T(8,128)(2,1)S(1)} %get-tuple-element.35), channel_id=1, source_target_pairs={{0,36},{1,37},{2,38},{3,39},{4,32},{5,33},{6,34},{7,35},{8,44},{9,... | collective-permute-start | bytes 196616 | tf_op jit(solution)/shard_map/ppermute | solution.py:262
  21.4 0.0 collective-permute-done.3
  21.5 0.0 copy-start
  21.5 8.6 %collective-permute-done.4 = bf16[256,128]{1,0:T(8,128)(2,1)S(1)} collective-permute-done((bf16[256,128]{1,0:T(8,128)(2,1)S(1)}, bf16[256,128]{1,0:T(8,128)(2,1)S(1)}, u32[]{:S(2)}, u32[]{:S(2)}) %collective-permute-start.4) | collective-permute-done | bytes 65568 | tf_op jit(solution)/shard_map/ppermute | solution.py:262
  30.1 0.0 collective-permute-done.5
  30.2 0.0 copy-start.1
  30.2 2.1 %collective-permute-start.6 = (bf16[1024,128]{1,0:T(8,128)(2,1)S(1)}, bf16[1024,128]{1,0:T(8,128)(2,1)S(1)}, u32[]{:S(2)}, u32[]{:S(2)}) collective-permute-start(bf16[1024,128]{1,0:T(8,128)(2,1)S(1)} %get-tuple-element.28), channel_id=1, source_target_pairs={{0,2},{1,3},{2,0},{3,1},{4,6},{5,7},{6,4},{7,5},{8,10},{9,11},{10,... | collective-permute-start | bytes 786440 | tf_op jit(solution)/shard_map/ppermute | solution.py:251
  32.3 0.0 copy-done
  32.3 0.0 copy-done.1
  32.3 4.6 %collective-permute-start.2 = (bf16[256,1024]{1,0:T(8,128)(2,1)S(1)}, bf16[256,1024]{1,0:T(8,128)(2,1)S(1)}, u32[]{:S(2)}, u32[]{:S(2)}) collective-permute-start(bf16[256,1024]{1,0:T(8,128)(2,1)S(1)} %constant_dynamic-update-slice_fusion.qg0), channel_id=1, source_target_pairs={{0,24},{1,25},{2,26},{3,27},{4,28},{5,29},{6,30},{7,31},{8,16},{9,... | collective-permute-start | bytes 1572872 | tf_op jit(solution)/shard_map/ppermute | solution.py:251
  37.0 2.3 %collective-permute-start.1 = (bf16[256,1024]{1,0:T(8,128)(2,1)S(1)}, bf16[256,1024]{1,0:T(8,128)(2,1)S(1)}, u32[]{:S(2)}, u32[]{:S(2)}) collective-permute-start(bf16[256,1024]{1,0:T(8,128)(2,1)S(1)} %constant_dynamic-update-slice_fusion.qg0), channel_id=1, source_target_pairs={{0,16},{1,17},{2,18},{3,19},{4,20},{5,21},{6,22},{7,23},{8,24},{9,... | collective-permute-start | bytes 1572872 | tf_op jit(solution)/shard_map/ppermute | solution.py:251
  39.2 2.1 %collective-permute-start = (bf16[256,1024]{1,0:T(8,128)(2,1)S(1)}, bf16[256,1024]{1,0:T(8,128)(2,1)S(1)}, u32[]{:S(2)}, u32[]{:S(2)}) collective-permute-start(bf16[256,1024]{1,0:T(8,128)(2,1)S(1)} %constant_dynamic-update-slice_fusion.qg0), channel_id=1, source_target_pairs={{0,8},{1,9},{2,10},{3,11},{4,12},{5,13},{6,14},{7,15},{8,0},{9,1},... | collective-permute-start | bytes 1572872 | tf_op jit(solution)/shard_map/ppermute | solution.py:251
  41.4 1.5 collective-permute-done.6
  43.0 4.2 %collective-permute-start.7 = (bf16[2048,128]{1,0:T(8,128)(2,1)S(1)}, bf16[2048,128]{1,0:T(8,128)(2,1)S(1)}, u32[]{:S(2)}, u32[]{:S(2)}) collective-permute-start(bf16[2048,128]{1,0:T(8,128)(2,1)S(1)} %constant_dynamic-update-slice_fusion.9.low), channel_id=1, source_target_pairs={{0,1},{1,0},{2,3},{3,2},{4,5},{5,4},{6,7},{7,6},{8,9},{9,8},{10,11... | collective-permute-start | bytes 1572872 | tf_op jit(solution)/shard_map/ppermute | solution.py:251
  47.1 0.0 copy-start.4
  47.1 0.0 copy-start.3
  47.2 0.7 copy-done.4
  47.8 0.0 copy-done.3
  47.8 0.1 concatenate.17.meta
  47.9 11.6 %collective-permute-done.2.qg3 = bf16[256,1024]{1,0:T(8,128)(2,1)S(1)} collective-permute-done((bf16[256,1024]{1,0:T(8,128)(2,1)S(1)}, bf16[256,1024]{1,0:T(8,128)(2,1)S(1)}, u32[]{:S(2)}, u32[]{:S(2)}) %collective-permute-start.2) | collective-permute-done | bytes 524320 | tf_op jit(solution)/shard_map/ppermute | solution.py:251
  59.5 0.0 collective-permute-done.1.qg2
  59.5 2.8 %collective-permute-done.qg1 = bf16[256,1024]{1,0:T(8,128)(2,1)S(1)} collective-permute-done((bf16[256,1024]{1,0:T(8,128)(2,1)S(1)}, bf16[256,1024]{1,0:T(8,128)(2,1)S(1)}, u32[]{:S(2)}, u32[]{:S(2)}) %collective-permute-start) | collective-permute-done | bytes 524320 | tf_op jit(solution)/shard_map/ppermute | solution.py:251
  62.4 0.0 collective-permute-done.7.high
  62.4 9.8 %shard_map.85.st0 = f32[12,1024]{1,0:T(8,128)S(1)} custom-call(s32[1026]{0:T(1024)S(1)} %concatenate.17.meta, bf16[256,1024]{1,0:T(8,128)(2,1)S(1)} %constant_dynamic-update-slice_fusion.qg0, bf16[256,1024]{1,0:T(8,128)(2,1)S(1)} %collective-permute-done.qg1, bf16[256,1024]{1,0:T(8,128)(2,1)S(1)} %collective-permute-done.1.qg2, ...), custom_call_target="tpu_custom_call" | custom-call | flops 1342177280 | bytes 4194304 | tf_op jit(solution)/shard_map/pallas_call | solution.py:217
  72.1 5.0 %collective-permute-start.10 = (f32[12,1024]{1,0:T(8,128)S(1)}, f32[12,1024]{1,0:T(8,128)S(1)}, u32[]{:S(2)}, u32[]{:S(2)}) collective-permute-start(f32[12,1024]{1,0:T(8,128)S(1)} %shard_map.85.st0), channel_id=1, source_target_pairs={{0,24},{1,25},{2,26},{3,27},{4,28},{5,29},{6,30},{7,31},{8,16},{9,... | collective-permute-start | bytes 147464 | tf_op jit(solution)/shard_map/ppermute | solution.py:251
  77.2 7.0 %collective-permute-start.9 = (f32[12,1024]{1,0:T(8,128)S(1)}, f32[12,1024]{1,0:T(8,128)S(1)}, u32[]{:S(2)}, u32[]{:S(2)}) collective-permute-start(f32[12,1024]{1,0:T(8,128)S(1)} %shard_map.85.st0), channel_id=1, source_target_pairs={{0,16},{1,17},{2,18},{3,19},{4,20},{5,21},{6,22},{7,23},{8,24},{9,... | collective-permute-start | bytes 147464 | tf_op jit(solution)/shard_map/ppermute | solution.py:251
  84.2 1.9 %collective-permute-start.8 = (f32[12,1024]{1,0:T(8,128)S(1)}, f32[12,1024]{1,0:T(8,128)S(1)}, u32[]{:S(2)}, u32[]{:S(2)}) collective-permute-start(f32[12,1024]{1,0:T(8,128)S(1)} %shard_map.85.st0), channel_id=1, source_target_pairs={{0,8},{1,9},{2,10},{3,11},{4,12},{5,13},{6,14},{7,15},{8,0},{9,1},... | collective-permute-start | bytes 147464 | tf_op jit(solution)/shard_map/ppermute | solution.py:251
  86.1 0.0 collective-permute-done.10.st3
  86.1 0.0 collective-permute-done.9.st2
  86.1 3.1 %collective-permute-done.8.st1 = f32[12,1024]{1,0:T(8,128)S(1)} collective-permute-done((f32[12,1024]{1,0:T(8,128)S(1)}, f32[12,1024]{1,0:T(8,128)S(1)}, u32[]{:S(2)}, u32[]{:S(2)}) %collective-permute-start.8) | collective-permute-done | bytes 49184 | tf_op jit(solution)/shard_map/ppermute | solution.py:251
  89.2 13.5 %shard_map.86 = (bf16[2048,128]{1,0:T(8,128)(2,1)S(1)}, bf16[1024,128]{1,0:T(8,128)(2,1)S(1)}, bf16[256,128]{1,0:T(8,128)(2,1)S(1)}, bf16[256,128]{1,0:T(8,128)(...) custom-call(s32[1026]{0:T(1024)S(1)} %concatenate.17.meta, ...), custom_call_target="tpu_custom_call" | custom-call | flops 3355443200 | bytes 4194304 | tf_op jit(solution)/shard_map/pallas_call | solution.py:231
  102.7 1.9 %collective-permute-start.14 = (bf16[2048,128]{1,0:T(8,128)(2,1)S(1)}, bf16[2048,128]{1,0:T(8,128)(2,1)S(1)}, u32[]{:S(2)}, u32[]{:S(2)}) collective-permute-start(bf16[2048,128]{1,0:T(8,128)(2,1)S(1)} %get-tuple-element.18), channel_id=1, source_target_pairs={{0,1},{1,0},{2,3},{3,2},{4,5},{5,4},{6,7},{7,6},{8,9},{9,8},{10,11... | collective-permute-start | bytes 1572872 | tf_op jit(solution)/shard_map/ppermute | solution.py:251
  104.6 13.6 %collective-permute-done.14 = bf16[2048,128]{1,0:T(8,128)(2,1)S(1)} collective-permute-done((bf16[2048,128]{1,0:T(8,128)(2,1)S(1)}, bf16[2048,128]{1,0:T(8,128)(2,1)S(1)}, u32[]{:S(2)}, u32[]{:S(2)}) %collective-permute-start.14) | collective-permute-done | bytes 524320 | tf_op jit(solution)/shard_map/ppermute | solution.py:251
  118.2 0.1 add_convert_fusion
  118.3 1.9 %collective-permute-start.15 = (bf16[1024,128]{1,0:T(8,128)(2,1)S(1)}, bf16[1024,128]{1,0:T(8,128)(2,1)S(1)}, u32[]{:S(2)}, u32[]{:S(2)}) collective-permute-start(bf16[1024,128]{1,0:T(8,128)(2,1)S(1)} %add_convert_fusion), channel_id=1, source_target_pairs={{0,2},{1,3},{2,0},{3,1},{4,6},{5,7},{6,4},{7,5},{8,10},{9,11},{10,... | collective-permute-start | bytes 786440 | tf_op jit(solution)/shard_map/ppermute | solution.py:251
  120.2 7.5 %collective-permute-start.11 = (bf16[128,1024]{1,0:T(8,128)(2,1)S(1)}, bf16[128,1024]{1,0:T(8,128)(2,1)S(1)}, u32[]{:S(2)}, u32[]{:S(2)}) collective-permute-start(bf16[128,1024]{1,0:T(8,128)(2,1)S(1)} %get-tuple-element.14), channel_id=1, source_target_pairs={{0,8},{1,9},{2,10},{3,11},{4,12},{5,13},{6,14},{7,15},{8,0},{9,1},... | collective-permute-start | bytes 786440 | tf_op jit(solution)/shard_map/ppermute | solution.py:251
  127.7 1.9 %collective-permute-start.12 = (bf16[128,1024]{1,0:T(8,128)(2,1)S(1)}, bf16[128,1024]{1,0:T(8,128)(2,1)S(1)}, u32[]{:S(2)}, u32[]{:S(2)}) collective-permute-start(bf16[128,1024]{1,0:T(8,128)(2,1)S(1)} %get-tuple-element.15), channel_id=1, source_target_pairs={{0,16},{1,17},{2,18},{3,19},{4,20},{5,21},{6,22},{7,23},{8,24},{9,... | collective-permute-start | bytes 786440 | tf_op jit(solution)/shard_map/ppermute | solution.py:251
  129.6 4.3 %collective-permute-start.13 = (bf16[128,1024]{1,0:T(8,128)(2,1)S(1)}, bf16[128,1024]{1,0:T(8,128)(2,1)S(1)}, u32[]{:S(2)}, u32[]{:S(2)}) collective-permute-start(bf16[128,1024]{1,0:T(8,128)(2,1)S(1)} %get-tuple-element.16), channel_id=1, source_target_pairs={{0,24},{1,25},{2,26},{3,27},{4,28},{5,29},{6,30},{7,31},{8,16},{9,... | collective-permute-start | bytes 786440 | tf_op jit(solution)/shard_map/ppermute | solution.py:251
  133.9 0.0 collective-permute-done.15
  134.0 0.1 add_convert_fusion.5
  134.0 10.9 %collective-permute-start.16 = (bf16[256,128]{1,0:T(8,128)(2,1)S(1)}, bf16[256,128]{1,0:T(8,128)(2,1)S(1)}, u32[]{:S(2)}, u32[]{:S(2)}) collective-permute-start(bf16[256,128]{1,0:T(8,128)(2,1)S(1)} %get-tuple-element.23), channel_id=1, source_target_pairs={{0,4},{1,5},{2,6},{3,7},{4,0},{5,1},{6,2},{7,3},{8,12},{9,13},{10,... | collective-permute-start | bytes 196616 | tf_op jit(solution)/shard_map/ppermute | solution.py:251
  145.0 1.9 %collective-permute-start.18 = (bf16[256,128]{1,0:T(8,128)(2,1)S(1)}, bf16[256,128]{1,0:T(8,128)(2,1)S(1)}, u32[]{:S(2)}, u32[]{:S(2)}) collective-permute-start(bf16[256,128]{1,0:T(8,128)(2,1)S(1)} %get-tuple-element.24), channel_id=1, source_target_pairs={{32,3},{33,2},{34,1},{35,0},{36,7},{37,6},{38,5},{39,4},{40,11},{4... | collective-permute-start | bytes 196616 | tf_op jit(solution)/shard_map/ppermute | solution.py:262
  146.9 0.0 collective-permute-done.11
  146.9 1.9 %collective-permute-start.17 = (bf16[256,128]{1,0:T(8,128)(2,1)S(1)}, bf16[256,128]{1,0:T(8,128)(2,1)S(1)}, u32[]{:S(2)}, u32[]{:S(2)}) collective-permute-start(bf16[256,128]{1,0:T(8,128)(2,1)S(1)} %get-tuple-element.25), channel_id=1, source_target_pairs={{32,4},{33,5},{34,6},{35,7},{36,0},{37,1},{38,2},{39,3},{40,12},{4... | collective-permute-start | bytes 196616 | tf_op jit(solution)/shard_map/ppermute | solution.py:262
  148.9 0.0 collective-permute-done.12
  148.9 0.0 collective-permute-done.13
  148.9 0.9 add_convert_fusion.1
  149.8 0.0 collective-permute-done.16
  149.8 10.6 %collective-permute-done.18 = bf16[256,128]{1,0:T(8,128)(2,1)S(1)} collective-permute-done((bf16[256,128]{1,0:T(8,128)(2,1)S(1)}, bf16[256,128]{1,0:T(8,128)(2,1)S(1)}, u32[]{:S(2)}, u32[]{:S(2)}) %collective-permute-start.18) | collective-permute-done | bytes 65568 | tf_op jit(solution)/shard_map/ppermute | solution.py:262
  160.3 0.0 collective-permute-done.17
  160.3 0.1 add_convert_fusion.2
  160.4 0.6 fusion
  (7 shorter events, 0.2 us)
Async XLA Ops:
  0.6 0.8 copy-start.2
  1.5 20.0 %collective-permute-start.3 = (bf16[256,128]{1,0:T(8,128)(2,1)S(1)}, bf16[256,128]{1,0:T(8,128)(2,1)S(1)}, u32[]{:S(2)}, u32[]{:S(2)}) collective-permute-start(bf16[256,128]{1,0:T(8,128)(2,1)S(1)} %get-tuple-element.35), channel_id=1, source_target_pairs={{0,4},{1,5},{2,6},{3,7},{4,0},{5,1},{6,2},{7,3},{8,12},{9,13},{10,... | collective-permute-start | bytes 196616 | tf_op jit(solution)/shard_map/ppermute | solution.py:251
  10.3 19.9 %collective-permute-start.5 = (bf16[256,128]{1,0:T(8,128)(2,1)S(1)}, bf16[256,128]{1,0:T(8,128)(2,1)S(1)}, u32[]{:S(2)}, u32[]{:S(2)}) collective-permute-start(bf16[256,128]{1,0:T(8,128)(2,1)S(1)} %get-tuple-element.35), channel_id=1, source_target_pairs={{0,35},{1,34},{2,33},{3,32},{4,39},{5,38},{6,37},{7,36},{8,43},{9,... | collective-permute-start | bytes 196616 | tf_op jit(solution)/shard_map/ppermute | solution.py:262
  19.5 10.6 %collective-permute-start.4 = (bf16[256,128]{1,0:T(8,128)(2,1)S(1)}, bf16[256,128]{1,0:T(8,128)(2,1)S(1)}, u32[]{:S(2)}, u32[]{:S(2)}) collective-permute-start(bf16[256,128]{1,0:T(8,128)(2,1)S(1)} %get-tuple-element.35), channel_id=1, source_target_pairs={{0,36},{1,37},{2,38},{3,39},{4,32},{5,33},{6,34},{7,35},{8,44},{9,... | collective-permute-start | bytes 196616 | tf_op jit(solution)/shard_map/ppermute | solution.py:262
  21.5 10.8 %copy-start = (bf16[128,1024]{1,0:T(8,128)(2,1)S(1)}, bf16[128,1024]{1,0:T(8,128)(2,1)}, u32[]{:S(2)}) copy-start(bf16[128,1024]{1,0:T(8,128)(2,1)} %param.6) | copy-start | bytes 786436
  30.2 2.1 %copy-start.1 = (bf16[128,1024]{1,0:T(8,128)(2,1)S(1)}, bf16[128,1024]{1,0:T(8,128)(2,1)}, u32[]{:S(2)}) copy-start(bf16[128,1024]{1,0:T(8,128)(2,1)} %param.9) | copy-start | bytes 786436
  30.2 12.7 %collective-permute-start.6 = (bf16[1024,128]{1,0:T(8,128)(2,1)S(1)}, bf16[1024,128]{1,0:T(8,128)(2,1)S(1)}, u32[]{:S(2)}, u32[]{:S(2)}) collective-permute-start(bf16[1024,128]{1,0:T(8,128)(2,1)S(1)} %get-tuple-element.28), channel_id=1, source_target_pairs={{0,2},{1,3},{2,0},{3,1},{4,6},{5,7},{6,4},{7,5},{8,10},{9,11},{10,... | collective-permute-start | bytes 786440 | tf_op jit(solution)/shard_map/ppermute | solution.py:251
  32.3 27.2 %collective-permute-start.2 = (bf16[256,1024]{1,0:T(8,128)(2,1)S(1)}, bf16[256,1024]{1,0:T(8,128)(2,1)S(1)}, u32[]{:S(2)}, u32[]{:S(2)}) collective-permute-start(bf16[256,1024]{1,0:T(8,128)(2,1)S(1)} %constant_dynamic-update-slice_fusion.qg0), channel_id=1, source_target_pairs={{0,24},{1,25},{2,26},{3,27},{4,28},{5,29},{6,30},{7,31},{8,16},{9,... | collective-permute-start | bytes 1572872 | tf_op jit(solution)/shard_map/ppermute | solution.py:251
  37.0 22.6 %collective-permute-start.1 = (bf16[256,1024]{1,0:T(8,128)(2,1)S(1)}, bf16[256,1024]{1,0:T(8,128)(2,1)S(1)}, u32[]{:S(2)}, u32[]{:S(2)}) collective-permute-start(bf16[256,1024]{1,0:T(8,128)(2,1)S(1)} %constant_dynamic-update-slice_fusion.qg0), channel_id=1, source_target_pairs={{0,16},{1,17},{2,18},{3,19},{4,20},{5,21},{6,22},{7,23},{8,24},{9,... | collective-permute-start | bytes 1572872 | tf_op jit(solution)/shard_map/ppermute | solution.py:251
  39.2 23.1 %collective-permute-start = (bf16[256,1024]{1,0:T(8,128)(2,1)S(1)}, bf16[256,1024]{1,0:T(8,128)(2,1)S(1)}, u32[]{:S(2)}, u32[]{:S(2)}) collective-permute-start(bf16[256,1024]{1,0:T(8,128)(2,1)S(1)} %constant_dynamic-update-slice_fusion.qg0), channel_id=1, source_target_pairs={{0,8},{1,9},{2,10},{3,11},{4,12},{5,13},{6,14},{7,15},{8,0},{9,1},... | collective-permute-start | bytes 1572872 | tf_op jit(solution)/shard_map/ppermute | solution.py:251
  43.0 19.4 %collective-permute-start.7 = (bf16[2048,128]{1,0:T(8,128)(2,1)S(1)}, bf16[2048,128]{1,0:T(8,128)(2,1)S(1)}, u32[]{:S(2)}, u32[]{:S(2)}) collective-permute-start(bf16[2048,128]{1,0:T(8,128)(2,1)S(1)} %constant_dynamic-update-slice_fusion.9.low), channel_id=1, source_target_pairs={{0,1},{1,0},{2,3},{3,2},{4,5},{5,4},{6,7},{7,6},{8,9},{9,8},{10,11... | collective-permute-start | bytes 1572872 | tf_op jit(solution)/shard_map/ppermute | solution.py:251
  47.1 0.7 copy-start.4
  47.1 0.7 copy-start.3
  72.1 14.0 %collective-permute-start.10 = (f32[12,1024]{1,0:T(8,128)S(1)}, f32[12,1024]{1,0:T(8,128)S(1)}, u32[]{:S(2)}, u32[]{:S(2)}) collective-permute-start(f32[12,1024]{1,0:T(8,128)S(1)} %shard_map.85.st0), channel_id=1, source_target_pairs={{0,24},{1,25},{2,26},{3,27},{4,28},{5,29},{6,30},{7,31},{8,16},{9,... | collective-permute-start | bytes 147464 | tf_op jit(solution)/shard_map/ppermute | solution.py:251
  77.2 8.9 %collective-permute-start.9 = (f32[12,1024]{1,0:T(8,128)S(1)}, f32[12,1024]{1,0:T(8,128)S(1)}, u32[]{:S(2)}, u32[]{:S(2)}) collective-permute-start(f32[12,1024]{1,0:T(8,128)S(1)} %shard_map.85.st0), channel_id=1, source_target_pairs={{0,16},{1,17},{2,18},{3,19},{4,20},{5,21},{6,22},{7,23},{8,24},{9,... | collective-permute-start | bytes 147464 | tf_op jit(solution)/shard_map/ppermute | solution.py:251
  84.2 5.0 %collective-permute-start.8 = (f32[12,1024]{1,0:T(8,128)S(1)}, f32[12,1024]{1,0:T(8,128)S(1)}, u32[]{:S(2)}, u32[]{:S(2)}) collective-permute-start(f32[12,1024]{1,0:T(8,128)S(1)} %shard_map.85.st0), channel_id=1, source_target_pairs={{0,8},{1,9},{2,10},{3,11},{4,12},{5,13},{6,14},{7,15},{8,0},{9,1},... | collective-permute-start | bytes 147464 | tf_op jit(solution)/shard_map/ppermute | solution.py:251
  102.7 15.5 %collective-permute-start.14 = (bf16[2048,128]{1,0:T(8,128)(2,1)S(1)}, bf16[2048,128]{1,0:T(8,128)(2,1)S(1)}, u32[]{:S(2)}, u32[]{:S(2)}) collective-permute-start(bf16[2048,128]{1,0:T(8,128)(2,1)S(1)} %get-tuple-element.18), channel_id=1, source_target_pairs={{0,1},{1,0},{2,3},{3,2},{4,5},{5,4},{6,7},{7,6},{8,9},{9,8},{10,11... | collective-permute-start | bytes 1572872 | tf_op jit(solution)/shard_map/ppermute | solution.py:251
  118.3 15.7 %collective-permute-start.15 = (bf16[1024,128]{1,0:T(8,128)(2,1)S(1)}, bf16[1024,128]{1,0:T(8,128)(2,1)S(1)}, u32[]{:S(2)}, u32[]{:S(2)}) collective-permute-start(bf16[1024,128]{1,0:T(8,128)(2,1)S(1)} %add_convert_fusion), channel_id=1, source_target_pairs={{0,2},{1,3},{2,0},{3,1},{4,6},{5,7},{6,4},{7,5},{8,10},{9,11},{10,... | collective-permute-start | bytes 786440 | tf_op jit(solution)/shard_map/ppermute | solution.py:251
  120.2 26.7 %collective-permute-start.11 = (bf16[128,1024]{1,0:T(8,128)(2,1)S(1)}, bf16[128,1024]{1,0:T(8,128)(2,1)S(1)}, u32[]{:S(2)}, u32[]{:S(2)}) collective-permute-start(bf16[128,1024]{1,0:T(8,128)(2,1)S(1)} %get-tuple-element.14), channel_id=1, source_target_pairs={{0,8},{1,9},{2,10},{3,11},{4,12},{5,13},{6,14},{7,15},{8,0},{9,1},... | collective-permute-start | bytes 786440 | tf_op jit(solution)/shard_map/ppermute | solution.py:251
  127.7 21.2 %collective-permute-start.12 = (bf16[128,1024]{1,0:T(8,128)(2,1)S(1)}, bf16[128,1024]{1,0:T(8,128)(2,1)S(1)}, u32[]{:S(2)}, u32[]{:S(2)}) collective-permute-start(bf16[128,1024]{1,0:T(8,128)(2,1)S(1)} %get-tuple-element.15), channel_id=1, source_target_pairs={{0,16},{1,17},{2,18},{3,19},{4,20},{5,21},{6,22},{7,23},{8,24},{9,... | collective-permute-start | bytes 786440 | tf_op jit(solution)/shard_map/ppermute | solution.py:251
  129.6 19.2 %collective-permute-start.13 = (bf16[128,1024]{1,0:T(8,128)(2,1)S(1)}, bf16[128,1024]{1,0:T(8,128)(2,1)S(1)}, u32[]{:S(2)}, u32[]{:S(2)}) collective-permute-start(bf16[128,1024]{1,0:T(8,128)(2,1)S(1)} %get-tuple-element.16), channel_id=1, source_target_pairs={{0,24},{1,25},{2,26},{3,27},{4,28},{5,29},{6,30},{7,31},{8,16},{9,... | collective-permute-start | bytes 786440 | tf_op jit(solution)/shard_map/ppermute | solution.py:251
  134.0 15.7 %collective-permute-start.16 = (bf16[256,128]{1,0:T(8,128)(2,1)S(1)}, bf16[256,128]{1,0:T(8,128)(2,1)S(1)}, u32[]{:S(2)}, u32[]{:S(2)}) collective-permute-start(bf16[256,128]{1,0:T(8,128)(2,1)S(1)} %get-tuple-element.23), channel_id=1, source_target_pairs={{0,4},{1,5},{2,6},{3,7},{4,0},{5,1},{6,2},{7,3},{8,12},{9,13},{10,... | collective-permute-start | bytes 196616 | tf_op jit(solution)/shard_map/ppermute | solution.py:251
  145.0 15.3 %collective-permute-start.18 = (bf16[256,128]{1,0:T(8,128)(2,1)S(1)}, bf16[256,128]{1,0:T(8,128)(2,1)S(1)}, u32[]{:S(2)}, u32[]{:S(2)}) collective-permute-start(bf16[256,128]{1,0:T(8,128)(2,1)S(1)} %get-tuple-element.24), channel_id=1, source_target_pairs={{32,3},{33,2},{34,1},{35,0},{36,7},{37,6},{38,5},{39,4},{40,11},{4... | collective-permute-start | bytes 196616 | tf_op jit(solution)/shard_map/ppermute | solution.py:262
  146.9 13.4 %collective-permute-start.17 = (bf16[256,128]{1,0:T(8,128)(2,1)S(1)}, bf16[256,128]{1,0:T(8,128)(2,1)S(1)}, u32[]{:S(2)}, u32[]{:S(2)}) collective-permute-start(bf16[256,128]{1,0:T(8,128)(2,1)S(1)} %get-tuple-element.25), channel_id=1, source_target_pairs={{32,4},{33,5},{34,6},{35,7},{36,0},{37,1},{38,2},{39,3},{40,12},{4... | collective-permute-start | bytes 196616 | tf_op jit(solution)/shard_map/ppermute | solution.py:262

commit v3 on v2

v3 whole, which is shorter than its diff:
```python
import functools

import jax
import jax.numpy as jnp
from jax import lax
from jax.experimental import pallas as pl
from jax.experimental.pallas import tpu as pltpu
from jax.sharding import PartitionSpec as P

BLOCK = 128
HD = 128
HEADS = 8
ROWS = HEADS * BLOCK
GROUP = 32
BLOCKS = 512
FAR = 4
STATS = 16
LIST = 32
NY = 4
NZ = 8
CHUNK = 256
NEG = -1e30
SCALE = HD**-0.5
SCALE2 = SCALE * 1.4426950408889634
VMEM_LIMIT = 40 * 1024 * 1024


def dot_nt(a, b):
    return lax.dot_general(a, b, (((1,), (1,)), ((), ())), preferred_element_type=jnp.float32)


def dot_nn(a, b):
    return lax.dot_general(a, b, (((1,), (0,)), ((), ())), preferred_element_type=jnp.float32)


def dot_tn(a, b):
    return lax.dot_general(a, b, (((0,), (0,)), ((), ())), preferred_element_type=jnp.float32)


def stack_heads(refs, qs, gs):
    for r, ref in enumerate(refs):
        for h in range(HEADS):
            to = r * ROWS + h * BLOCK
            qs[to : to + BLOCK, :] = ref[0:BLOCK, h * HD : (h + 1) * HD]
            gs[to : to + BLOCK, :] = ref[BLOCK : 2 * BLOCK, h * HD : (h + 1) * HD]


def place(low, high, ks, vs):
    for half, ref in enumerate((low, high)):
        for at in range(8):
            quarter, before, odd = at // 4, (at // 2) % 2, at % 2
            lo = at * 2 * BLOCK
            to = (NZ * before + 4 * half + 2 * quarter + odd) * BLOCK
            ks[to : to + BLOCK, :] = ref[lo : lo + BLOCK, :]
            vs[to : to + BLOCK, :] = ref[lo + BLOCK : lo + 2 * BLOCK, :]


def list_pairs(meta, lists):
    outer, inner = meta[2 * BLOCKS], meta[2 * BLOCKS + 1]
    q_at = [meta[BLOCKS + outer * GROUP + (inner ^ (r * NZ))] for r in range(NY)]
    q_doc = [meta[at] for at in q_at]
    far = jnp.where(outer % 2 == 0, FAR, 0)
    k_at, k_doc = [], []
    for s in range(2 * NZ):
        flip = ((s & 1) << 2) | (s & 2) | ((s >> 2) & 1)
        if s < NZ:
            at = meta[BLOCKS + outer * GROUP + (inner ^ flip)]
            doc = meta[at]
        else:
            at = meta[BLOCKS + jnp.maximum(outer - 1, 0) * GROUP + (inner ^ flip ^ far)]
            doc = jnp.where(outer > 0, meta[at], -1)
        k_at.append(at)
        k_doc.append(doc)
    for r in range(NY):
        count = jnp.int32(0)
        for s in range(2 * NZ):
            if r == 0 and s == 0:
                continue
            sees = q_doc[r] == k_doc[s]
            if s < NZ:
                sees = sees & (k_at[s] < q_at[r])
            lists[r * LIST + count] = jnp.int32(s)
            count = count + sees.astype(jnp.int32)
        lists[r * LIST + count] = jnp.int32(0)
        lists[r * LIST + LIST - 1] = count


def diagonal_mask():
    k_at = lax.broadcasted_iota(jnp.int32, (BLOCK, CHUNK), 0)
    q_at = lax.broadcasted_iota(jnp.int32, (BLOCK, CHUNK), 1) % BLOCK
    return k_at <= q_at


def for_pairs(lists, pair):
    pair(0, (0,), 0.0, True)

    @pl.loop(0, NY)
    def _(r):
        count = lists[r * LIST + LIST - 1]

        @pl.loop(0, (count + 1) // 2)
        def _(j):
            at = r * LIST + 2 * j
            bias = jnp.where(2 * j + 1 < count, 0.0, -NEG)
            pair(r, (lists[at], lists[at + 1]), bias, False)


def rows_of(ref, slots):
    return jnp.concatenate([ref[pl.ds(s * BLOCK, BLOCK), :] for s in slots], axis=0)


def stats_kernel(meta, qg0, qg1, qg2, qg3, low, high, stats, qs, gs, ks, vs, lists):
    list_pairs(meta, lists)
    stack_heads((qg0, qg1, qg2, qg3), qs, gs)
    place(low, high, ks, vs)
    stats[0:NY, :] = jnp.full((NY, ROWS), NEG, jnp.float32)
    stats[NY:STATS, :] = jnp.zeros((STATS - NY, ROWS), jnp.float32)

    def pair(r, slots, bias, diagonal):
        key, value = rows_of(ks, slots), rows_of(vs, slots)
        for c in range(ROWS // CHUNK):
            rows = pl.ds(r * ROWS + c * CHUNK, CHUNK)
            cols = pl.ds(c * CHUNK, CHUNK)
            scores = dot_nt(key, qs[rows, :]) * SCALE2
            dprob = dot_nt(value, gs[rows, :])
            if diagonal:
                scores = jnp.where(diagonal_mask(), scores, NEG)
            biases = (0.0, bias)[: len(slots)]
            top = stats[pl.ds(r, 1), cols]
            new_top = top
            for i, less in enumerate(biases):
                part = scores[i * BLOCK : (i + 1) * BLOCK]
                new_top = jnp.maximum(new_top, jnp.max(part, axis=0, keepdims=True) - less)
            factor = jnp.exp2(top - new_top)
            total = stats[pl.ds(NY + r, 1), cols] * factor
            product = stats[pl.ds(2 * NY + r, 1), cols] * factor
            for i, less in enumerate(biases):
                half = slice(i * BLOCK, (i + 1) * BLOCK)
                weights = jnp.exp2(scores[half] - (new_top + less))
                total = total + jnp.sum(weights, axis=0, keepdims=True)
                product = product + jnp.sum(weights * dprob[half], axis=0, keepdims=True)
            stats[pl.ds(r, 1), cols] = new_top
            stats[pl.ds(NY + r, 1), cols] = total
            stats[pl.ds(2 * NY + r, 1), cols] = product

    for_pairs(lists, pair)


def grads_kernel(meta, lists, qs, gs, ks, vs, stats, *rest):
    out_high, out_mid, own_one, own_zero, before_one, before_zero = rest[:6]
    dq_outs = rest[6:10]
    lse, delta, w_low, d_low, dk, dv, dq = rest[10:]
    dk[...] = jnp.zeros_like(dk)
    dv[...] = jnp.zeros_like(dv)
    dq[...] = jnp.zeros_like(dq)
    me = meta[2 * BLOCKS + 1] // NZ
    for r in range(NY):
        tops, sums, products = [], [], []
        for y in range(NY):
            at = STATS * y + (y ^ me ^ r)
            tops.append(stats[pl.ds(at, 1), :])
            sums.append(stats[pl.ds(at + NY, 1), :])
            products.append(stats[pl.ds(at + 2 * NY, 1), :])
        top = functools.reduce(jnp.maximum, tops)
        factors = [jnp.exp2(t - top) for t in tops]
        total = sum(x * f for x, f in zip(sums, factors))
        product = sum(x * f for x, f in zip(products, factors))
        lse[r : r + 1, :] = top + jnp.log2(total)
        delta[r : r + 1, :] = product / total

    def pair(r, slots, bias, diagonal):
        key, value = rows_of(ks, slots), rows_of(vs, slots)
        count = len(slots) * BLOCK
        for c in range(ROWS // CHUNK):
            rows = pl.ds(r * ROWS + c * CHUNK, CHUNK)
            cols = pl.ds(c * CHUNK, CHUNK)
            scores = dot_nt(key, qs[rows, :]) * SCALE2
            dprob = dot_nt(value, gs[rows, :])
            for i, less in enumerate((0.0, bias)[: len(slots)]):
                half = slice(i * BLOCK, (i + 1) * BLOCK)
                probs = jnp.exp2(scores[half] - (lse[pl.ds(r, 1), cols] + less))
                if diagonal:
                    probs = jnp.where(diagonal_mask(), probs, 0.0)
                w_low[half, cols] = probs.astype(jnp.bfloat16)
                dscore = probs * (dprob[half] - delta[pl.ds(r, 1), cols])
                d_low[half, cols] = dscore.astype(jnp.bfloat16)
        rows = pl.ds(r * ROWS, ROWS)
        dk_part = dot_nn(d_low[0:count, :], qs[rows, :])
        dv_part = dot_nn(w_low[0:count, :], gs[rows, :])
        for i, s in enumerate(slots):
            half = slice(i * BLOCK, (i + 1) * BLOCK)
            dk[pl.ds(s * BLOCK, BLOCK), :] += dk_part[half]
            dv[pl.ds(s * BLOCK, BLOCK), :] += dv_part[half]
        dq[pl.ds(r * HD, HD), :] += dot_tn(key, d_low[0:count, :])

    for_pairs(lists, pair)

    def write(slots, out, at):
        for s in slots:
            rows = slice(s * BLOCK, (s + 1) * BLOCK)
            out[at : at + BLOCK, :] = (dk[rows, :] * SCALE).astype(jnp.bfloat16)
            out[at + BLOCK : at + 2 * BLOCK, :] = dv[rows, :].astype(jnp.bfloat16)
            at += 2 * BLOCK

    write((4, 5, NZ + 4, NZ + 5, 6, 7, NZ + 6, NZ + 7), out_high, 0)
    write((2, 3, NZ + 2, NZ + 3), out_mid, 0)
    write((1,), own_one, 0)
    write((0,), own_zero, 0)
    write((NZ + 1,), before_one, 0)
    write((NZ,), before_zero, 0)
    for r in range(NY):
        for h in range(HEADS):
            part = dq[r * HD : (r + 1) * HD, h * BLOCK : (h + 1) * BLOCK] * SCALE
            dq_outs[r][:, h * HD : (h + 1) * HD] = part.astype(jnp.bfloat16).T


def smem():
    return pl.BlockSpec(memory_space=pltpu.SMEM)


def vmem():
    return pl.BlockSpec(memory_space=pltpu.VMEM)


def cost(matmuls, pairs):
    return pl.CostEstimate(
        flops=matmuls * pairs * 2 * ROWS * BLOCK * HD,
        bytes_accessed=4 * 1024 * 1024,
        transcendentals=pairs * ROWS * BLOCK,
    )


def run_stats(*args):
    stacked = jax.ShapeDtypeStruct((NY * ROWS, HD), jnp.bfloat16)
    blocks = jax.ShapeDtypeStruct((2 * NZ * BLOCK, HD), jnp.bfloat16)
    return pl.pallas_call(
        stats_kernel,
        out_shape=[
            jax.ShapeDtypeStruct((STATS, ROWS), jnp.float32),
            stacked,
            stacked,
            blocks,
            blocks,
            jax.ShapeDtypeStruct((NY * LIST,), jnp.int32),
        ],
        in_specs=[smem()] + [vmem()] * (len(args) - 1),
        out_specs=[vmem()] * 5 + [smem()],
        compiler_params=pltpu.CompilerParams(vmem_limit_bytes=VMEM_LIMIT),
        cost_estimate=cost(2, 20),
    )(*args)


def run_grads(*args):
    outs = [jax.ShapeDtypeStruct((n * 2 * BLOCK, HD), jnp.bfloat16) for n in (8, 4, 1, 1, 1, 1)]
    outs += [jax.ShapeDtypeStruct((BLOCK, HEADS * HD), jnp.bfloat16)] * NY
    return pl.pallas_call(
        grads_kernel,
        out_shape=outs,
        in_specs=[smem()] * 2 + [vmem()] * (len(args) - 2),
        out_specs=[vmem()] * len(outs),
        scratch_shapes=[
            pltpu.VMEM((NY, ROWS), jnp.float32),
            pltpu.VMEM((NY, ROWS), jnp.float32),
            pltpu.VMEM((2 * BLOCK, ROWS), jnp.bfloat16),
            pltpu.VMEM((2 * BLOCK, ROWS), jnp.bfloat16),
            pltpu.VMEM((2 * NZ * BLOCK, HD), jnp.float32),
            pltpu.VMEM((2 * NZ * BLOCK, HD), jnp.float32),
            pltpu.VMEM((NY * HD, ROWS), jnp.float32),
        ],
        compiler_params=pltpu.CompilerParams(vmem_limit_bytes=VMEM_LIMIT),
        cost_estimate=cost(5, 20),
    )(*args)


def swap(array, flip):
    return lax.ppermute(array, "inner", [(i, i ^ flip) for i in range(GROUP)])


def across(array, by):
    outer = lax.axis_size("outer")
    pairs = [
        (o * GROUP + i, (o + by) * GROUP + (i ^ (0 if max(o, o + by) % 2 else FAR)))
        for o in range(outer)
        if 0 <= o + by < outer
        for i in range(GROUP)
    ]
    return lax.ppermute(array, ("outer", "inner"), pairs)


def add_low(*terms):
    total = terms[0].astype(jnp.float32)
    for term in terms[1:]:
        total = total + term.astype(jnp.float32)
    return total.astype(jnp.bfloat16)


def shards(queries, keys, values, grad_out, doc_ids, block_order):
    one = 2 * BLOCK
    ids = jnp.stack([lax.axis_index("outer"), lax.axis_index("inner")]).astype(jnp.int32)
    meta = jnp.concatenate([doc_ids, block_order, ids])
    own = jnp.concatenate([keys, values], axis=0)
    qg0 = jnp.concatenate([queries, grad_out], axis=0)

    own_pair = jnp.concatenate([own, swap(own, 4)], axis=0)
    before_pair = across(own_pair, 1)
    qg2 = swap(qg0, 2 * NZ)
    qg1 = swap(qg0, NZ)
    qg3 = swap(qg0, 3 * NZ)
    quad = jnp.concatenate([own_pair, before_pair], axis=0)
    quad, qg1, qg3 = lax.optimization_barrier((quad, qg1, qg3))
    low = jnp.concatenate([quad, swap(quad, 2)], axis=0)
    high = swap(low, 1)

    stats, qs, gs, ks, vs, lists = run_stats(meta, qg0, qg1, qg2, qg3, low, high)
    along_y = [[y * NZ + z for y in range(NY)] for z in range(NZ)]
    all_stats = lax.all_gather(stats, "inner", axis=0, tiled=True, axis_index_groups=along_y)
    d_high, d_mid, own_one, own_zero, before_one, before_zero, dq0, dq1, dq2, dq3 = run_grads(
        meta, lists, qs, gs, ks, vs, all_stats
    )

    near = swap(d_high, 1)
    e2 = swap(dq2, 2 * NZ)
    e1 = swap(dq1, NZ)
    e3 = swap(dq3, 3 * NZ)
    near, e1, e3 = lax.optimization_barrier((near, e1, e3))
    far = swap(add_low(d_mid, near[4 * one :]), 2)
    back = across(
        add_low(
            jnp.concatenate([before_zero, before_one], axis=0),
            near[2 * one : 4 * one],
            far[2 * one : 4 * one],
        ),
        -1,
    )
    own_far = swap(add_low(own_one, near[one : 2 * one], far[one : 2 * one], back[one:]), 4)
    grad_queries = add_low(dq0, e1, e2, e3)
    totals = add_low(own_zero, near[:one], far[:one], back[:one], own_far)
    return grad_queries, totals[:BLOCK], totals[BLOCK:]


def solution(mesh):
    rows = P(("outer", "inner"), None)
    return jax.shard_map(
        shards,
        mesh=mesh,
        in_specs=(rows, rows, rows, rows, P(), P()),
        out_specs=(rows, rows, rows),
        check_vma=False,
    )
```

time: 162 us -> 152 us (0.938)
  the two profiles are of different devices: /device:TPU:67 before, /device:TPU:7 now
where the time goes in v3:
time: 152 us; the launch traced here: 150 us
  starting transfers between devices  72.9 us (48%)
  waiting for transfers between devices  48.3 us (32%)
  Pallas kernels  14.9 us (10%)
  blocking collectives  9.46 us (6%)
  local copies, waits for them, and re-layouts  2.5 us (2%)
    ppermute x12, starting transfers between devices, swap(): return lax.ppermute(array, 'inner', [(i, i ^ flip) for i in range(GROUP)])  46.7 us
    ppermute x12, waiting for transfers between devices, swap(): return lax.ppermute(array, 'inner', [(i, i ^ flip) for i in range(GROUP)])  43.6 us
    ppermute x2, starting transfers between devices, across(): return lax.ppermute(array, ('outer', 'inner'), pairs)  26.2 us
    all_gather x1, blocking collectives, shards(): lax.all_gather(stats, 'inner', axis=0, tiled=True, axis_index_groups=alon...  9.46 us
    pallas_call x1, Pallas kernels, run_grads(): pl.pallas_call(grads_kernel, out_shape=outs, in_specs=[smem()] * 2 + [vme...  8.21 us
    pallas_call x1, Pallas kernels, run_stats(): pl.pallas_call(stats_kernel, out_shape=[jax.ShapeDtypeStruct((STATS, ROWS...  6.73 us
    ppermute x2, waiting for transfers between devices, across(): return lax.ppermute(array, ('outer', 'inner'), pairs)  4.7 us
  transfers between devices with their start and end apart: 14, of which 9 were waited for; matrix products, arithmetic and copies ran while one was open for 1% of the time, Pallas kernels for 0%

profile of v3, /device:TPU:7, one launch (start us, length us, event | category | flops | bytes accessed | tf_op | source)
XLA Modules:
  0.0 150.1 jit_solution(15825451751954193011)
XLA Ops:
  0.6 0.0 copy-start.2
  0.6 1.0 constant_dynamic-update-slice_fusion.1
  1.7 0.0 copy-done.2
  1.7 0.0 copy-start
  1.7 0.0 copy-start.1
  1.7 4.6 %collective-permute-start.3 = (bf16[256,1024]{1,0:T(8,128)(2,1)S(1)}, bf16[256,1024]{1,0:T(8,128)(2,1)S(1)}, u32[]{:S(2)}, u32[]{:S(2)}) collective-permute-start(bf16[256,1024]{1,0:T(8,128)(2,1)S(1)} %constant_dynamic-update-slice_fusion.qg0), channel_id=1, source_target_pairs={{0,24},{1,25},{2,26},{3,27},{4,28},{5,29},{6,30},{7,31},{8,16},{9,... | collective-permute-start | bytes 1572872 | tf_op jit(solution)/shard_map/ppermute | solution.py:276
  6.4 1.9 %collective-permute-start.2 = (bf16[256,1024]{1,0:T(8,128)(2,1)S(1)}, bf16[256,1024]{1,0:T(8,128)(2,1)S(1)}, u32[]{:S(2)}, u32[]{:S(2)}) collective-permute-start(bf16[256,1024]{1,0:T(8,128)(2,1)S(1)} %constant_dynamic-update-slice_fusion.qg0), channel_id=1, source_target_pairs={{0,8},{1,9},{2,10},{3,11},{4,12},{5,13},{6,14},{7,15},{8,0},{9,1},... | collective-permute-start | bytes 1572872 | tf_op jit(solution)/shard_map/ppermute | solution.py:276
  8.3 0.0 copy-done
  8.3 0.0 copy-done.1
  8.3 8.8 %collective-permute-start = (bf16[256,128]{1,0:T(8,128)(2,1)S(1)}, bf16[256,128]{1,0:T(8,128)(2,1)S(1)}, u32[]{:S(2)}, u32[]{:S(2)}) collective-permute-start(bf16[256,128]{1,0:T(8,128)(2,1)S(1)} %pad_maximum_fusion.2), channel_id=1, source_target_pairs={{0,4},{1,5},{2,6},{3,7},{4,0},{5,1},{6,2},{7,3},{8,12},{9,13},{10,... | collective-permute-start | bytes 196616 | tf_op jit(solution)/shard_map/ppermute | solution.py:276
  17.2 1.6 %collective-permute-done = bf16[256,128]{1,0:T(8,128)(2,1)S(1)} collective-permute-done((bf16[256,128]{1,0:T(8,128)(2,1)S(1)}, bf16[256,128]{1,0:T(8,128)(2,1)S(1)}, u32[]{:S(2)}, u32[]{:S(2)}) %collective-permute-start) | collective-permute-done | bytes 65568 | tf_op jit(solution)/shard_map/ppermute | solution.py:276
  18.8 13.6 %collective-permute-start.1 = (bf16[512,128]{1,0:T(8,128)(2,1)S(1)}, bf16[512,128]{1,0:T(8,128)(2,1)S(1)}, u32[]{:S(2)}, u32[]{:S(2)}) collective-permute-start(bf16[512,128]{1,0:T(8,128)(2,1)S(1)} %pad_maximum_fusion.1), channel_id=1, source_target_pairs={{0,32},{1,33},{2,34},{3,35},{4,36},{5,37},{6,38},{7,39},{8,40},{9,... | collective-permute-start | bytes 393224 | tf_op jit(solution)/shard_map/ppermute | solution.py:287
  32.4 4.7 %collective-permute-done.1 = bf16[512,128]{1,0:T(8,128)(2,1)S(1)} collective-permute-done((bf16[512,128]{1,0:T(8,128)(2,1)S(1)}, bf16[512,128]{1,0:T(8,128)(2,1)S(1)}, u32[]{:S(2)}, u32[]{:S(2)}) %collective-permute-start.1) | collective-permute-done | bytes 131104 | tf_op jit(solution)/shard_map/ppermute | solution.py:287
  37.1 0.0 collective-permute-done.3.qg3
  37.1 0.0 collective-permute-done.2.qg1
  37.1 1.9 %collective-permute-start.5 = (bf16[1024,128]{1,0:T(8,128)(2,1)S(1)}, bf16[1024,128]{1,0:T(8,128)(2,1)S(1)}, u32[]{:S(2)}, u32[]{:S(2)}) collective-permute-start(bf16[1024,128]{1,0:T(8,128)(2,1)S(1)} %pad_maximum_fusion), channel_id=1, source_target_pairs={{0,2},{1,3},{2,0},{3,1},{4,6},{5,7},{6,4},{7,5},{8,10},{9,11},{10,... | collective-permute-start | bytes 786440 | tf_op jit(solution)/shard_map/ppermute | solution.py:276
  39.1 3.1 %collective-permute-start.4 = (bf16[256,1024]{1,0:T(8,128)(2,1)S(1)}, bf16[256,1024]{1,0:T(8,128)(2,1)S(1)}, u32[]{:S(2)}, u32[]{:S(2)}) collective-permute-start(bf16[256,1024]{1,0:T(8,128)(2,1)S(1)} %constant_dynamic-update-slice_fusion.qg0), channel_id=1, source_target_pairs={{0,16},{1,17},{2,18},{3,19},{4,20},{5,21},{6,22},{7,23},{8,24},{9,... | collective-permute-start | bytes 1572872 | tf_op jit(solution)/shard_map/ppermute | solution.py:276
  42.2 11.0 %collective-permute-done.5 = bf16[1024,128]{1,0:T(8,128)(2,1)S(1)} collective-permute-done((bf16[1024,128]{1,0:T(8,128)(2,1)S(1)}, bf16[1024,128]{1,0:T(8,128)(2,1)S(1)}, u32[]{:S(2)}, u32[]{:S(2)}) %collective-permute-start.5) | collective-permute-done | bytes 262176 | tf_op jit(solution)/shard_map/ppermute | solution.py:276
  53.3 1.9 %collective-permute-start.6 = (bf16[2048,128]{1,0:T(8,128)(2,1)S(1)}, bf16[2048,128]{1,0:T(8,128)(2,1)S(1)}, u32[]{:S(2)}, u32[]{:S(2)}) collective-permute-start(bf16[2048,128]{1,0:T(8,128)(2,1)S(1)} %constant_dynamic-update-slice_fusion.2.low), channel_id=1, source_target_pairs={{0,1},{1,0},{2,3},{3,2},{4,5},{5,4},{6,7},{7,6},{8,9},{9,8},{10,11... | collective-permute-start | bytes 1572872 | tf_op jit(solution)/shard_map/ppermute | solution.py:276
  55.2 0.0 copy-start.4
  55.2 0.0 copy-start.3
  55.2 0.7 copy-done.4
  55.9 0.0 copy-done.3
  55.9 0.1 concatenate.23.meta
  56.0 0.0 collective-permute-done.4.qg2
  56.0 12.3 %collective-permute-done.6.high = bf16[2048,128]{1,0:T(8,128)(2,1)S(1)} collective-permute-done((bf16[2048,128]{1,0:T(8,128)(2,1)S(1)}, bf16[2048,128]{1,0:T(8,128)(2,1)S(1)}, u32[]{:S(2)}, u32[]{:S(2)}) %collective-permute-start.6) | collective-permute-done | bytes 524320 | tf_op jit(solution)/shard_map/ppermute | solution.py:276
  68.3 6.7 %shard_map.85 = (f32[16,1024]{1,0:T(8,128)S(1)}, bf16[4096,128]{1,0:T(8,128)(2,1)S(1)}, bf16[4096,128]{1,0:T(8,128)(2,1)S(1)}, bf16[2048,128]{1,0:T(8,128)(2,1)S...) custom-call(s32[1026]{0:T(1024)S(1)} %concatenate.23.meta, ...), custom_call_target="tpu_custom_call" | custom-call | flops 1342177280 | bytes 4194304 | tf_op jit(solution)/shard_map/pallas_call | solution.py:236
  75.0 9.5 %all_gather.3.stats = f32[64,1024]{1,0:T(8,128)S(1)} all-gather(f32[16,1024]{1,0:T(8,128)S(1)} %get-tuple-element.33), channel_id=1, replica_groups={{0,8,16,24},{1,9,17,25},{2,10,18,26},{3,11,19,27},{4,12,20,28},{5,13,21..., dimensions={0}, use_global_device_ids=true | all-gather | bytes 327680 | tf_op jit(solution)/shard_map/all_gather | solution.py:316
  84.5 8.2 %shard_map.86 = (bf16[2048,128]{1,0:T(8,128)(2,1)S(1)}, bf16[1024,128]{1,0:T(8,128)(2,1)S(1)}, bf16[256,128]{1,0:T(8,128)(2,1)S(1)}, bf16[256,128]{1,0:T(8,128)(...) custom-call(s32[1026]{0:T(1024)S(1)} %concatenate.23.meta, ...), custom_call_target="tpu_custom_call" | custom-call | flops 3355443200 | bytes 4194304 | tf_op jit(solution)/shard_map/pallas_call | solution.py:256
  92.7 5.4 %collective-permute-start.7 = (bf16[2048,128]{1,0:T(8,128)(2,1)S(1)}, bf16[2048,128]{1,0:T(8,128)(2,1)S(1)}, u32[]{:S(2)}, u32[]{:S(2)}) collective-permute-start(bf16[2048,128]{1,0:T(8,128)(2,1)S(1)} %get-tuple-element.35), channel_id=1, source_target_pairs={{0,1},{1,0},{2,3},{3,2},{4,5},{5,4},{6,7},{7,6},{8,9},{9,8},{10,11... | collective-permute-start | bytes 1572872 | tf_op jit(solution)/shard_map/ppermute | solution.py:276
  98.1 1.9 %collective-permute-start.8 = (bf16[128,1024]{1,0:T(8,128)(2,1)S(1)}, bf16[128,1024]{1,0:T(8,128)(2,1)S(1)}, u32[]{:S(2)}, u32[]{:S(2)}) collective-permute-start(bf16[128,1024]{1,0:T(8,128)(2,1)S(1)} %get-tuple-element.36), channel_id=1, source_target_pairs={{0,8},{1,9},{2,10},{3,11},{4,12},{5,13},{6,14},{7,15},{8,0},{9,1},... | collective-permute-start | bytes 786440 | tf_op jit(solution)/shard_map/ppermute | solution.py:276
  100.1 2.1 %collective-permute-start.9 = (bf16[128,1024]{1,0:T(8,128)(2,1)S(1)}, bf16[128,1024]{1,0:T(8,128)(2,1)S(1)}, u32[]{:S(2)}, u32[]{:S(2)}) collective-permute-start(bf16[128,1024]{1,0:T(8,128)(2,1)S(1)} %get-tuple-element.37), channel_id=1, source_target_pairs={{0,24},{1,25},{2,26},{3,27},{4,28},{5,29},{6,30},{7,31},{8,16},{9,... | collective-permute-start | bytes 786440 | tf_op jit(solution)/shard_map/ppermute | solution.py:276
  102.2 3.0 %collective-permute-done.8 = bf16[128,1024]{1,0:T(8,128)(2,1)S(1)} collective-permute-done((bf16[128,1024]{1,0:T(8,128)(2,1)S(1)}, bf16[128,1024]{1,0:T(8,128)(2,1)S(1)}, u32[]{:S(2)}, u32[]{:S(2)}) %collective-permute-start.8) | collective-permute-done | bytes 262176 | tf_op jit(solution)/shard_map/ppermute | solution.py:276
  105.3 3.1 %collective-permute-done.9 = bf16[128,1024]{1,0:T(8,128)(2,1)S(1)} collective-permute-done((bf16[128,1024]{1,0:T(8,128)(2,1)S(1)}, bf16[128,1024]{1,0:T(8,128)(2,1)S(1)}, u32[]{:S(2)}, u32[]{:S(2)}) %collective-permute-start.9) | collective-permute-done | bytes 262176 | tf_op jit(solution)/shard_map/ppermute | solution.py:276
  108.4 0.0 collective-permute-done.7
  108.4 0.1 add_convert_fusion
  108.5 7.6 %collective-permute-start.11 = (bf16[1024,128]{1,0:T(8,128)(2,1)S(1)}, bf16[1024,128]{1,0:T(8,128)(2,1)S(1)}, u32[]{:S(2)}, u32[]{:S(2)}) collective-permute-start(bf16[1024,128]{1,0:T(8,128)(2,1)S(1)} %add_convert_fusion), channel_id=1, source_target_pairs={{0,2},{1,3},{2,0},{3,1},{4,6},{5,7},{6,4},{7,5},{8,10},{9,11},{10,... | collective-permute-start | bytes 786440 | tf_op jit(solution)/shard_map/ppermute | solution.py:276
  116.0 6.3 %collective-permute-done.11 = bf16[1024,128]{1,0:T(8,128)(2,1)S(1)} collective-permute-done((bf16[1024,128]{1,0:T(8,128)(2,1)S(1)}, bf16[1024,128]{1,0:T(8,128)(2,1)S(1)}, u32[]{:S(2)}, u32[]{:S(2)}) %collective-permute-start.11) | collective-permute-done | bytes 262176 | tf_op jit(solution)/shard_map/ppermute | solution.py:276
  122.3 0.1 add_convert_fusion.2
  122.4 12.6 %collective-permute-start.12 = (bf16[512,128]{1,0:T(8,128)(2,1)S(1)}, bf16[512,128]{1,0:T(8,128)(2,1)S(1)}, u32[]{:S(2)}, u32[]{:S(2)}) collective-permute-start(bf16[512,128]{1,0:T(8,128)(2,1)S(1)} %add_convert_fusion.2), channel_id=1, source_target_pairs={{32,0},{33,1},{34,2},{35,3},{36,4},{37,5},{38,6},{39,7},{40,8},{41... | collective-permute-start | bytes 393224 | tf_op jit(solution)/shard_map/ppermute | solution.py:287
  135.0 2.5 %collective-permute-start.10 = (bf16[128,1024]{1,0:T(8,128)(2,1)S(1)}, bf16[128,1024]{1,0:T(8,128)(2,1)S(1)}, u32[]{:S(2)}, u32[]{:S(2)}) collective-permute-start(bf16[128,1024]{1,0:T(8,128)(2,1)S(1)} %get-tuple-element.39), channel_id=1, source_target_pairs={{0,16},{1,17},{2,18},{3,19},{4,20},{5,21},{6,22},{7,23},{8,24},{9,... | collective-permute-start | bytes 786440 | tf_op jit(solution)/shard_map/ppermute | solution.py:276
  137.5 0.0 collective-permute-done.12
  137.6 4.8 %collective-permute-start.13 = (bf16[256,128]{1,0:T(8,128)(2,1)S(1)}, bf16[256,128]{1,0:T(8,128)(2,1)S(1)}, u32[]{:S(2)}, u32[]{:S(2)}) collective-permute-start(bf16[256,128]{1,0:T(8,128)(2,1)S(1)} %add_convert_fusion.4), channel_id=1, source_target_pairs={{0,4},{1,5},{2,6},{3,7},{4,0},{5,1},{6,2},{7,3},{8,12},{9,13},{10,... | collective-permute-start | bytes 196616 | tf_op jit(solution)/shard_map/ppermute | solution.py:276
  142.4 4.0 %collective-permute-done.10 = bf16[128,1024]{1,0:T(8,128)(2,1)S(1)} collective-permute-done((bf16[128,1024]{1,0:T(8,128)(2,1)S(1)}, bf16[128,1024]{1,0:T(8,128)(2,1)S(1)}, u32[]{:S(2)}, u32[]{:S(2)}) %collective-permute-start.10) | collective-permute-done | bytes 262176 | tf_op jit(solution)/shard_map/ppermute | solution.py:276
  146.3 0.9 add_convert_fusion.1
  147.2 2.2 %collective-permute-done.13 = bf16[256,128]{1,0:T(8,128)(2,1)S(1)} collective-permute-done((bf16[256,128]{1,0:T(8,128)(2,1)S(1)}, bf16[256,128]{1,0:T(8,128)(2,1)S(1)}, u32[]{:S(2)}, u32[]{:S(2)}) %collective-permute-start.13) | collective-permute-done | bytes 65568 | tf_op jit(solution)/shard_map/ppermute | solution.py:276
  149.5 0.6 fusion
  (8 shorter events, 0.2 us)
Async XLA Ops:
  0.6 1.0 copy-start.2
  1.7 6.6 %copy-start = (bf16[128,128]{1,0:T(8,128)(2,1)S(1)}, bf16[128,128]{1,0:T(8,128)(2,1)}, u32[]{:S(2)}) copy-start(bf16[128,128]{1,0:T(8,128)(2,1)} %param.8) | copy-start | bytes 98308
  1.7 6.6 %copy-start.1 = (bf16[128,128]{1,0:T(8,128)(2,1)S(1)}, bf16[128,128]{1,0:T(8,128)(2,1)}, u32[]{:S(2)}) copy-start(bf16[128,128]{1,0:T(8,128)(2,1)} %param.7) | copy-start | bytes 98308
  1.7 35.4 %collective-permute-start.3 = (bf16[256,1024]{1,0:T(8,128)(2,1)S(1)}, bf16[256,1024]{1,0:T(8,128)(2,1)S(1)}, u32[]{:S(2)}, u32[]{:S(2)}) collective-permute-start(bf16[256,1024]{1,0:T(8,128)(2,1)S(1)} %constant_dynamic-update-slice_fusion.qg0), channel_id=1, source_target_pairs={{0,24},{1,25},{2,26},{3,27},{4,28},{5,29},{6,30},{7,31},{8,16},{9,... | collective-permute-start | bytes 1572872 | tf_op jit(solution)/shard_map/ppermute | solution.py:276
  6.4 30.8 %collective-permute-start.2 = (bf16[256,1024]{1,0:T(8,128)(2,1)S(1)}, bf16[256,1024]{1,0:T(8,128)(2,1)S(1)}, u32[]{:S(2)}, u32[]{:S(2)}) collective-permute-start(bf16[256,1024]{1,0:T(8,128)(2,1)S(1)} %constant_dynamic-update-slice_fusion.qg0), channel_id=1, source_target_pairs={{0,8},{1,9},{2,10},{3,11},{4,12},{5,13},{6,14},{7,15},{8,0},{9,1},... | collective-permute-start | bytes 1572872 | tf_op jit(solution)/shard_map/ppermute | solution.py:276
  8.3 10.5 %collective-permute-start = (bf16[256,128]{1,0:T(8,128)(2,1)S(1)}, bf16[256,128]{1,0:T(8,128)(2,1)S(1)}, u32[]{:S(2)}, u32[]{:S(2)}) collective-permute-start(bf16[256,128]{1,0:T(8,128)(2,1)S(1)} %pad_maximum_fusion.2), channel_id=1, source_target_pairs={{0,4},{1,5},{2,6},{3,7},{4,0},{5,1},{6,2},{7,3},{8,12},{9,13},{10,... | collective-permute-start | bytes 196616 | tf_op jit(solution)/shard_map/ppermute | solution.py:276
  18.8 18.3 %collective-permute-start.1 = (bf16[512,128]{1,0:T(8,128)(2,1)S(1)}, bf16[512,128]{1,0:T(8,128)(2,1)S(1)}, u32[]{:S(2)}, u32[]{:S(2)}) collective-permute-start(bf16[512,128]{1,0:T(8,128)(2,1)S(1)} %pad_maximum_fusion.1), channel_id=1, source_target_pairs={{0,32},{1,33},{2,34},{3,35},{4,36},{5,37},{6,38},{7,39},{8,40},{9,... | collective-permute-start | bytes 393224 | tf_op jit(solution)/shard_map/ppermute | solution.py:287
  37.1 16.1 %collective-permute-start.5 = (bf16[1024,128]{1,0:T(8,128)(2,1)S(1)}, bf16[1024,128]{1,0:T(8,128)(2,1)S(1)}, u32[]{:S(2)}, u32[]{:S(2)}) collective-permute-start(bf16[1024,128]{1,0:T(8,128)(2,1)S(1)} %pad_maximum_fusion), channel_id=1, source_target_pairs={{0,2},{1,3},{2,0},{3,1},{4,6},{5,7},{6,4},{7,5},{8,10},{9,11},{10,... | collective-permute-start | bytes 786440 | tf_op jit(solution)/shard_map/ppermute | solution.py:276
  39.1 16.9 %collective-permute-start.4 = (bf16[256,1024]{1,0:T(8,128)(2,1)S(1)}, bf16[256,1024]{1,0:T(8,128)(2,1)S(1)}, u32[]{:S(2)}, u32[]{:S(2)}) collective-permute-start(bf16[256,1024]{1,0:T(8,128)(2,1)S(1)} %constant_dynamic-update-slice_fusion.qg0), channel_id=1, source_target_pairs={{0,16},{1,17},{2,18},{3,19},{4,20},{5,21},{6,22},{7,23},{8,24},{9,... | collective-permute-start | bytes 1572872 | tf_op jit(solution)/shard_map/ppermute | solution.py:276
  53.3 15.0 %collective-permute-start.6 = (bf16[2048,128]{1,0:T(8,128)(2,1)S(1)}, bf16[2048,128]{1,0:T(8,128)(2,1)S(1)}, u32[]{:S(2)}, u32[]{:S(2)}) collective-permute-start(bf16[2048,128]{1,0:T(8,128)(2,1)S(1)} %constant_dynamic-update-slice_fusion.2.low), channel_id=1, source_target_pairs={{0,1},{1,0},{2,3},{3,2},{4,5},{5,4},{6,7},{7,6},{8,9},{9,8},{10,11... | collective-permute-start | bytes 1572872 | tf_op jit(solution)/shard_map/ppermute | solution.py:276
  55.2 0.7 copy-start.4
  55.2 0.7 copy-start.3
  92.7 15.7 %collective-permute-start.7 = (bf16[2048,128]{1,0:T(8,128)(2,1)S(1)}, bf16[2048,128]{1,0:T(8,128)(2,1)S(1)}, u32[]{:S(2)}, u32[]{:S(2)}) collective-permute-start(bf16[2048,128]{1,0:T(8,128)(2,1)S(1)} %get-tuple-element.35), channel_id=1, source_target_pairs={{0,1},{1,0},{2,3},{3,2},{4,5},{5,4},{6,7},{7,6},{8,9},{9,8},{10,11... | collective-permute-start | bytes 1572872 | tf_op jit(solution)/shard_map/ppermute | solution.py:276
  98.1 7.1 %collective-permute-start.8 = (bf16[128,1024]{1,0:T(8,128)(2,1)S(1)}, bf16[128,1024]{1,0:T(8,128)(2,1)S(1)}, u32[]{:S(2)}, u32[]{:S(2)}) collective-permute-start(bf16[128,1024]{1,0:T(8,128)(2,1)S(1)} %get-tuple-element.36), channel_id=1, source_target_pairs={{0,8},{1,9},{2,10},{3,11},{4,12},{5,13},{6,14},{7,15},{8,0},{9,1},... | collective-permute-start | bytes 786440 | tf_op jit(solution)/shard_map/ppermute | solution.py:276
  100.1 8.3 %collective-permute-start.9 = (bf16[128,1024]{1,0:T(8,128)(2,1)S(1)}, bf16[128,1024]{1,0:T(8,128)(2,1)S(1)}, u32[]{:S(2)}, u32[]{:S(2)}) collective-permute-start(bf16[128,1024]{1,0:T(8,128)(2,1)S(1)} %get-tuple-element.37), channel_id=1, source_target_pairs={{0,24},{1,25},{2,26},{3,27},{4,28},{5,29},{6,30},{7,31},{8,16},{9,... | collective-permute-start | bytes 786440 | tf_op jit(solution)/shard_map/ppermute | solution.py:276
  108.5 13.9 %collective-permute-start.11 = (bf16[1024,128]{1,0:T(8,128)(2,1)S(1)}, bf16[1024,128]{1,0:T(8,128)(2,1)S(1)}, u32[]{:S(2)}, u32[]{:S(2)}) collective-permute-start(bf16[1024,128]{1,0:T(8,128)(2,1)S(1)} %add_convert_fusion), channel_id=1, source_target_pairs={{0,2},{1,3},{2,0},{3,1},{4,6},{5,7},{6,4},{7,5},{8,10},{9,11},{10,... | collective-permute-start | bytes 786440 | tf_op jit(solution)/shard_map/ppermute | solution.py:276
  122.4 15.1 %collective-permute-start.12 = (bf16[512,128]{1,0:T(8,128)(2,1)S(1)}, bf16[512,128]{1,0:T(8,128)(2,1)S(1)}, u32[]{:S(2)}, u32[]{:S(2)}) collective-permute-start(bf16[512,128]{1,0:T(8,128)(2,1)S(1)} %add_convert_fusion.2), channel_id=1, source_target_pairs={{32,0},{33,1},{34,2},{35,3},{36,4},{37,5},{38,6},{39,7},{40,8},{41... | collective-permute-start | bytes 393224 | tf_op jit(solution)/shard_map/ppermute | solution.py:287
  135.0 11.3 %collective-permute-start.10 = (bf16[128,1024]{1,0:T(8,128)(2,1)S(1)}, bf16[128,1024]{1,0:T(8,128)(2,1)S(1)}, u32[]{:S(2)}, u32[]{:S(2)}) collective-permute-start(bf16[128,1024]{1,0:T(8,128)(2,1)S(1)} %get-tuple-element.39), channel_id=1, source_target_pairs={{0,16},{1,17},{2,18},{3,19},{4,20},{5,21},{6,22},{7,23},{8,24},{9,... | collective-permute-start | bytes 786440 | tf_op jit(solution)/shard_map/ppermute | solution.py:276
  137.6 11.9 %collective-permute-start.13 = (bf16[256,128]{1,0:T(8,128)(2,1)S(1)}, bf16[256,128]{1,0:T(8,128)(2,1)S(1)}, u32[]{:S(2)}, u32[]{:S(2)}) collective-permute-start(bf16[256,128]{1,0:T(8,128)(2,1)S(1)} %add_convert_fusion.4), channel_id=1, source_target_pairs={{0,4},{1,5},{2,6},{3,7},{4,0},{5,1},{6,2},{7,3},{8,12},{9,13},{10,... | collective-permute-start | bytes 196616 | tf_op jit(solution)/shard_map/ppermute | solution.py:276

commit v4 on v3

--- a/solution.py
+++ b/solution.py
@@ -15,7 +15,7 @@
 BLOCKS = 512
 FAR = 4
 STATS = 16
-LIST = 32
+LIST = 16
 NY = 4
 NZ = 8
 CHUNK = 256
@@ -46,38 +46,35 @@
 
 
 def place(low, high, ks, vs):
-    for half, ref in enumerate((low, high)):
-        for at in range(8):
-            quarter, before, odd = at // 4, (at // 2) % 2, at % 2
-            lo = at * 2 * BLOCK
-            to = (NZ * before + 4 * half + 2 * quarter + odd) * BLOCK
-            ks[to : to + BLOCK, :] = ref[lo : lo + BLOCK, :]
-            vs[to : to + BLOCK, :] = ref[lo + BLOCK : lo + 2 * BLOCK, :]
-
-
-def list_pairs(meta, lists):
+    for s in range(NZ):
+        ref, lo, to = (low, high)[s // 4], (s % 4) * 2 * BLOCK, s * BLOCK
+        ks[to : to + BLOCK, :] = ref[lo : lo + BLOCK, :]
+        vs[to : to + BLOCK, :] = ref[lo + BLOCK : lo + 2 * BLOCK, :]
+
+
+def list_pairs(meta, before, lists):
     outer, inner = meta[2 * BLOCKS], meta[2 * BLOCKS + 1]
     q_at = [meta[BLOCKS + outer * GROUP + (inner ^ (r * NZ))] for r in range(NY)]
     q_doc = [meta[at] for at in q_at]
-    far = jnp.where(outer % 2 == 0, FAR, 0)
     k_at, k_doc = [], []
-    for s in range(2 * NZ):
+    for s in range(NZ):
         flip = ((s & 1) << 2) | (s & 2) | ((s >> 2) & 1)
-        if s < NZ:
+        if before:
+            far = jnp.where(outer % 2 == 0, FAR, 0)
+            at = meta[BLOCKS + jnp.maximum(outer - 1, 0) * GROUP + (inner ^ flip ^ far)]
+            doc = jnp.where(outer > 0, meta[at], -1)
+        else:
             at = meta[BLOCKS + outer * GROUP + (inner ^ flip)]
             doc = meta[at]
-        else:
-            at = meta[BLOCKS + jnp.maximum(outer - 1, 0) * GROUP + (inner ^ flip ^ far)]
-            doc = jnp.where(outer > 0, meta[at], -1)
         k_at.append(at)
         k_doc.append(doc)
     for r in range(NY):
         count = jnp.int32(0)
-        for s in range(2 * NZ):
-            if r == 0 and s == 0:
+        for s in range(NZ):
+            if not before and r == 0 and s == 0:
                 continue
             sees = q_doc[r] == k_doc[s]
-            if s < NZ:
+            if not before:
                 sees = sees & (k_at[s] < q_at[r])
             lists[r * LIST + count] = jnp.int32(s)
             count = count + sees.astype(jnp.int32)
@@ -91,8 +88,9 @@
     return k_at <= q_at
 
 
-def for_pairs(lists, pair):
-    pair(0, (0,), 0.0, True)
+def for_pairs(before, lists, pair):
+    if not before:
+        pair(0, (0,), 0.0, True)
 
     @pl.loop(0, NY)
     def _(r):
@@ -109,12 +107,17 @@
     return jnp.concatenate([ref[pl.ds(s * BLOCK, BLOCK), :] for s in slots], axis=0)
 
 
-def stats_kernel(meta, qg0, qg1, qg2, qg3, low, high, stats, qs, gs, ks, vs, lists):
-    list_pairs(meta, lists)
-    stack_heads((qg0, qg1, qg2, qg3), qs, gs)
+def stats_kernel(before, *refs):
+    if before:
+        meta, low, high, qs, gs, earlier, stats, ks, vs, lists = refs
+        stats[...] = earlier[...]
+    else:
+        meta, low, high, *qg, stats, ks, vs, lists, qs, gs = refs
+        stack_heads(qg, qs, gs)
+        stats[0:NY, :] = jnp.full((NY, ROWS), NEG, jnp.float32)
+        stats[NY:STATS, :] = jnp.zeros((STATS - NY, ROWS), jnp.float32)
+    list_pairs(meta, before, lists)
     place(low, high, ks, vs)
-    stats[0:NY, :] = jnp.full((NY, ROWS), NEG, jnp.float32)
-    stats[NY:STATS, :] = jnp.zeros((STATS - NY, ROWS), jnp.float32)
 
     def pair(r, slots, bias, diagonal):
         key, value = rows_of(ks, slots), rows_of(vs, slots)
@@ -143,12 +146,11 @@
             stats[pl.ds(NY + r, 1), cols] = total
             stats[pl.ds(2 * NY + r, 1), cols] = product
 
-    for_pairs(lists, pair)
-
-
-def grads_kernel(meta, lists, qs, gs, ks, vs, stats, *rest):
-    out_high, out_mid, own_one, own_zero, before_one, before_zero = rest[:6]
-    dq_outs = rest[6:10]
+    for_pairs(before, lists, pair)
+
+
+def grads_kernel(meta, own_lists, before_lists, qs, gs, own_k, own_v, before_k, before_v, stats, *rest):
+    b_high, b_mid, b_pair, o_high, o_mid, o_one, o_zero, dq0, dq12, dq3 = rest[:10]
     lse, delta, w_low, d_low, dk, dv, dq = rest[10:]
     dk[...] = jnp.zeros_like(dk)
     dv[...] = jnp.zeros_like(dv)
@@ -168,7 +170,7 @@
         lse[r : r + 1, :] = top + jnp.log2(total)
         delta[r : r + 1, :] = product / total
 
-    def pair(r, slots, bias, diagonal):
+    def pair(ks, vs, base, r, slots, bias, diagonal):
         key, value = rows_of(ks, slots), rows_of(vs, slots)
         count = len(slots) * BLOCK
         for c in range(ROWS // CHUNK):
@@ -189,11 +191,12 @@
         dv_part = dot_nn(w_low[0:count, :], gs[rows, :])
         for i, s in enumerate(slots):
             half = slice(i * BLOCK, (i + 1) * BLOCK)
-            dk[pl.ds(s * BLOCK, BLOCK), :] += dk_part[half]
-            dv[pl.ds(s * BLOCK, BLOCK), :] += dv_part[half]
+            dk[pl.ds((base + s) * BLOCK, BLOCK), :] += dk_part[half]
+            dv[pl.ds((base + s) * BLOCK, BLOCK), :] += dv_part[half]
         dq[pl.ds(r * HD, HD), :] += dot_tn(key, d_low[0:count, :])
 
-    for_pairs(lists, pair)
+    for_pairs(False, own_lists, functools.partial(pair, own_k, own_v, 0))
+    for_pairs(True, before_lists, functools.partial(pair, before_k, before_v, NZ))
 
     def write(slots, out, at):
         for s in slots:
@@ -202,16 +205,17 @@
             out[at + BLOCK : at + 2 * BLOCK, :] = dv[rows, :].astype(jnp.bfloat16)
             at += 2 * BLOCK
 
-    write((4, 5, NZ + 4, NZ + 5, 6, 7, NZ + 6, NZ + 7), out_high, 0)
-    write((2, 3, NZ + 2, NZ + 3), out_mid, 0)
-    write((1,), own_one, 0)
-    write((0,), own_zero, 0)
-    write((NZ + 1,), before_one, 0)
-    write((NZ,), before_zero, 0)
-    for r in range(NY):
+    write((NZ + 4, NZ + 5, NZ + 6, NZ + 7), b_high, 0)
+    write((NZ + 2, NZ + 3), b_mid, 0)
+    write((NZ, NZ + 1), b_pair, 0)
+    write((4, 5, 6, 7), o_high, 0)
+    write((2, 3), o_mid, 0)
+    write((1,), o_one, 0)
+    write((0,), o_zero, 0)
+    for r, (out, at) in enumerate(((dq0, 0), (dq12, 0), (dq12, BLOCK), (dq3, 0))):
         for h in range(HEADS):
             part = dq[r * HD : (r + 1) * HD, h * BLOCK : (h + 1) * BLOCK] * SCALE
-            dq_outs[r][:, h * HD : (h + 1) * HD] = part.astype(jnp.bfloat16).T
+            out[at : at + BLOCK, h * HD : (h + 1) * HD] = part.astype(jnp.bfloat16).T
 
 
 def smem():
@@ -230,33 +234,35 @@
     )
 
 
-def run_stats(*args):
-    stacked = jax.ShapeDtypeStruct((NY * ROWS, HD), jnp.bfloat16)
-    blocks = jax.ShapeDtypeStruct((2 * NZ * BLOCK, HD), jnp.bfloat16)
+def run_stats(before, *args):
+    blocks = jax.ShapeDtypeStruct((NZ * BLOCK, HD), jnp.bfloat16)
+    outs = [
+        jax.ShapeDtypeStruct((STATS, ROWS), jnp.float32),
+        blocks,
+        blocks,
+        jax.ShapeDtypeStruct((NY * LIST,), jnp.int32),
+    ]
+    specs = [vmem()] * 3 + [smem()]
+    if not before:
+        outs += [jax.ShapeDtypeStruct((NY * ROWS, HD), jnp.bfloat16)] * 2
+        specs += [vmem()] * 2
     return pl.pallas_call(
-        stats_kernel,
-        out_shape=[
-            jax.ShapeDtypeStruct((STATS, ROWS), jnp.float32),
-            stacked,
-            stacked,
-            blocks,
-            blocks,
-            jax.ShapeDtypeStruct((NY * LIST,), jnp.int32),
-        ],
+        functools.partial(stats_kernel, before),
+        out_shape=outs,
         in_specs=[smem()] + [vmem()] * (len(args) - 1),
-        out_specs=[vmem()] * 5 + [smem()],
+        out_specs=specs,
         compiler_params=pltpu.CompilerParams(vmem_limit_bytes=VMEM_LIMIT),
-        cost_estimate=cost(2, 20),
+        cost_estimate=cost(2, 10),
     )(*args)
 
 
 def run_grads(*args):
-    outs = [jax.ShapeDtypeStruct((n * 2 * BLOCK, HD), jnp.bfloat16) for n in (8, 4, 1, 1, 1, 1)]
-    outs += [jax.ShapeDtypeStruct((BLOCK, HEADS * HD), jnp.bfloat16)] * NY
+    outs = [jax.ShapeDtypeStruct((n * 2 * BLOCK, HD), jnp.bfloat16) for n in (4, 2, 2, 4, 2, 1, 1)]
+    outs += [jax.ShapeDtypeStruct((n * BLOCK, HEADS * HD), jnp.bfloat16) for n in (1, 2, 1)]
     return pl.pallas_call(
         grads_kernel,
         out_shape=outs,
-        in_specs=[smem()] * 2 + [vmem()] * (len(args) - 2),
+        in_specs=[smem()] * 3 + [vmem()] * (len(args) - 3),
         out_specs=[vmem()] * len(outs),
         scratch_shapes=[
             pltpu.VMEM((NY, ROWS), jnp.float32),
@@ -301,40 +307,42 @@
     own = jnp.concatenate([keys, values], axis=0)
     qg0 = jnp.concatenate([queries, grad_out], axis=0)
 
-    own_pair = jnp.concatenate([own, swap(own, 4)], axis=0)
+    own4 = swap(own, 4)
+    qg_later, _ = lax.optimization_barrier((qg0, own4))
+    qg1 = swap(qg0, NZ)
+    qg3 = swap(qg_later, 3 * NZ)
+    qg2 = swap(qg_later, 2 * NZ)
+    own_pair = jnp.concatenate([own, own4], axis=0)
     before_pair = across(own_pair, 1)
-    qg2 = swap(qg0, 2 * NZ)
-    qg1 = swap(qg0, NZ)
-    qg3 = swap(qg0, 3 * NZ)
-    quad = jnp.concatenate([own_pair, before_pair], axis=0)
-    quad, qg1, qg3 = lax.optimization_barrier((quad, qg1, qg3))
-    low = jnp.concatenate([quad, swap(quad, 2)], axis=0)
-    high = swap(low, 1)
-
-    stats, qs, gs, ks, vs, lists = run_stats(meta, qg0, qg1, qg2, qg3, low, high)
+    own_low = jnp.concatenate([own_pair, swap(own_pair, 2)], axis=0)
+    own_high = swap(own_low, 1)
+    before_low = jnp.concatenate([before_pair, swap(before_pair, 2)], axis=0)
+    before_low, qg1, qg2 = lax.optimization_barrier((before_low, qg1, qg2))
+    before_high = swap(before_low, 1)
+
+    stats, own_k, own_v, own_lists, qs, gs = run_stats(
+        False, meta, own_low, own_high, qg0, qg1, qg2, qg3
+    )
+    stats, before_k, before_v, before_lists = run_stats(
+        True, meta, before_low, before_high, qs, gs, stats
+    )
     along_y = [[y * NZ + z for y in range(NY)] for z in range(NZ)]
     all_stats = lax.all_gather(stats, "inner", axis=0, tiled=True, axis_index_groups=along_y)
-    d_high, d_mid, own_one, own_zero, before_one, before_zero, dq0, dq1, dq2, dq3 = run_grads(
-        meta, lists, qs, gs, ks, vs, all_stats
-    )
-
-    near = swap(d_high, 1)
-    e2 = swap(dq2, 2 * NZ)
-    e1 = swap(dq1, NZ)
+    b_high, b_mid, b_pair, o_high, o_mid, o_one, o_zero, dq0, dq12, dq3 = run_grads(
+        meta, own_lists, before_lists, qs, gs, own_k, own_v, before_k, before_v, all_stats
+    )
+
+    b_near = swap(b_high, 1)
+    o_near = swap(o_high, 1)
+    e12 = swap(dq12, NZ)
+    b_far = swap(add_low(b_mid, b_near[2 * one :]), 2)
+    back = across(add_low(b_pair, b_near[: 2 * one], b_far), -1)
+    o_far = swap(add_low(o_mid, o_near[2 * one :]), 2)
+    dq3 = add_low(dq3, e12[BLOCK:])
     e3 = swap(dq3, 3 * NZ)
-    near, e1, e3 = lax.optimization_barrier((near, e1, e3))
-    far = swap(add_low(d_mid, near[4 * one :]), 2)
-    back = across(
-        add_low(
-            jnp.concatenate([before_zero, before_one], axis=0),
-            near[2 * one : 4 * one],
-            far[2 * one : 4 * one],
-        ),
-        -1,
-    )
-    own_far = swap(add_low(own_one, near[one : 2 * one], far[one : 2 * one], back[one:]), 4)
-    grad_queries = add_low(dq0, e1, e2, e3)
-    totals = add_low(own_zero, near[:one], far[:one], back[:one], own_far)
+    o_four = swap(add_low(o_one, o_near[one : 2 * one], o_far[one:], back[one:]), 4)
+    grad_queries = add_low(dq0, e12[:BLOCK], e3)
+    totals = add_low(o_zero, o_near[:one], o_far[:one], back[:one], o_four)
     return grad_queries, totals[:BLOCK], totals[BLOCK:]
 
 

time: 152 us -> 138 us (0.908)
  waiting for transfers between devices: 48.3 us -> 28.7 us
  Pallas kernels: 14.9 us -> 23 us
  starting transfers between devices: 72.9 us -> 69.1 us
    ppermute x12 -> x15, waiting for transfers between devices: 43.6 us -> 19 us  [swap(): return lax.ppermute(array, 'inner', [(i, i ^ flip) for i in range(GROUP)])]
    ppermute x2, starting transfers between devices: 26.2 us -> 13.4 us  [across(): return lax.ppermute(array, ('outer', 'inner'), pairs)]
    ppermute x12 -> x15, starting transfers between devices: 46.7 us -> 55.7 us  [swap(): return lax.ppermute(array, 'inner', [(i, i ^ flip) for i in range(GROUP)])]
    pallas_call x2 -> x3, Pallas kernels: 14.9 us -> 23 us  [the longest x1 12.1 us: run_grads(): pl.pallas_call(grads_kernel, out_shape=outs, in_specs=[smem()] * 3 + [vme...]
    ppermute x2, waiting for transfers between devices: 4.7 us -> 9.63 us  [across(): return lax.ppermute(array, ('outer', 'inner'), pairs)]
  transfers between devices with their start and end apart: 14 -> 17, of which waited for: 9 -> 10; matrix products, arithmetic and copies ran while one was open for 1% -> 2% of each run, Pallas kernels for 0% -> 5%
where the time goes in v4:
time: 138 us; the launch traced here: 136 us
  starting transfers between devices  69.1 us (50%)
  waiting for transfers between devices  28.7 us (21%)
  Pallas kernels  23 us (17%)
  blocking collectives  9.37 us (7%)
  local copies, waits for them, and re-layouts  2.47 us (2%)
  other arithmetic  1.92 us (1%)
    ppermute x15, starting transfers between devices, swap(): return lax.ppermute(array, 'inner', [(i, i ^ flip) for i in range(GROUP)])  55.7 us
    ppermute x15, waiting for transfers between devices, swap(): return lax.ppermute(array, 'inner', [(i, i ^ flip) for i in range(GROUP)])  19 us
    ppermute x2, starting transfers between devices, across(): return lax.ppermute(array, ('outer', 'inner'), pairs)  13.4 us
    pallas_call x1, Pallas kernels, run_grads(): pl.pallas_call(grads_kernel, out_shape=outs, in_specs=[smem()] * 3 + [vme...  12.1 us
    pallas_call x2, Pallas kernels, run_stats(): pl.pallas_call(functools.partial(stats_kernel, before), out_shape=outs, i...  10.9 us
    ppermute x2, waiting for transfers between devices, across(): return lax.ppermute(array, ('outer', 'inner'), pairs)  9.63 us
    all_gather x1, blocking collectives, shards(): lax.all_gather(stats, 'inner', axis=0, tiled=True, axis_index_groups=alon...  9.37 us
  transfers between devices with their start and end apart: 17, of which 10 were waited for; matrix products, arithmetic and copies ran while one was open for 2% of the time, Pallas kernels for 5%

profile of v4, /device:TPU:7, one launch (start us, length us, event | category | flops | bytes accessed | tf_op | source)
XLA Modules:
  0.0 135.5 jit_solution(10556032395800421243)
XLA Ops:
  0.6 0.8 pad_maximum_fusion.1
  1.4 0.0 copy-start
  1.4 8.9 %collective-permute-start = (bf16[256,128]{1,0:T(8,128)(2,1)S(1)}, bf16[256,128]{1,0:T(8,128)(2,1)S(1)}, u32[]{:S(2)}, u32[]{:S(2)}) collective-permute-start(bf16[256,128]{1,0:T(8,128)(2,1)S(1)} %pad_maximum_fusion.1), channel_id=1, source_target_pairs={{0,4},{1,5},{2,6},{3,7},{4,0},{5,1},{6,2},{7,3},{8,12},{9,13},{10,... | collective-permute-start | bytes 196616 | tf_op jit(solution)/shard_map/ppermute | solution.py:282
  10.4 1.0 constant_dynamic-update-slice_fusion.8
  11.3 0.0 copy-done
  11.3 0.0 copy-start.1
  11.4 0.0 copy-start.2
  11.4 3.2 %collective-permute-start.5 = (bf16[256,1024]{1,0:T(8,128)(2,1)S(1)}, bf16[256,1024]{1,0:T(8,128)(2,1)S(1)}, u32[]{:S(2)}, u32[]{:S(2)}) collective-permute-start(bf16[256,1024]{1,0:T(8,128)(2,1)S(1)} %constant_dynamic-update-slice_fusion.7.refs_3_), channel_id=1, source_target_pairs={{0,8},{1,9},{2,10},{3,11},{4,12},{5,13},{6,14},{7,15},{8,0},{9,1},... | collective-permute-start | bytes 1572872 | tf_op jit(solution)/shard_map/ppermute | solution.py:282
  14.6 0.0 copy-done.1
  14.6 0.0 collective-permute-done
  14.6 4.5 %collective-permute-start.6 = (bf16[256,1024]{1,0:T(8,128)(2,1)S(1)}, bf16[256,1024]{1,0:T(8,128)(2,1)S(1)}, u32[]{:S(2)}, u32[]{:S(2)}) collective-permute-start(bf16[256,1024]{1,0:T(8,128)(2,1)S(1)} %constant_dynamic-update-slice_fusion.7.refs_3_), channel_id=1, source_target_pairs={{0,16},{1,17},{2,18},{3,19},{4,20},{5,21},{6,22},{7,23},{8,24},{9,... | collective-permute-start | bytes 1572872 | tf_op jit(solution)/shard_map/ppermute | solution.py:282
  19.2 0.0 copy-done.2
  19.2 11.5 %collective-permute-start.3 = (bf16[512,128]{1,0:T(8,128)(2,1)S(1)}, bf16[512,128]{1,0:T(8,128)(2,1)S(1)}, u32[]{:S(2)}, u32[]{:S(2)}) collective-permute-start(bf16[512,128]{1,0:T(8,128)(2,1)S(1)} %get-tuple-element.53), channel_id=1, source_target_pairs={{0,32},{1,33},{2,34},{3,35},{4,36},{5,37},{6,38},{7,39},{8,40},{9,... | collective-permute-start | bytes 393224 | tf_op jit(solution)/shard_map/ppermute | solution.py:293
  30.8 4.6 %collective-permute-start.1 = (bf16[512,128]{1,0:T(8,128)(2,1)S(1)}, bf16[512,128]{1,0:T(8,128)(2,1)S(1)}, u32[]{:S(2)}, u32[]{:S(2)}) collective-permute-start(bf16[512,128]{1,0:T(8,128)(2,1)S(1)} %get-tuple-element.53), channel_id=1, source_target_pairs={{0,2},{1,3},{2,0},{3,1},{4,6},{5,7},{6,4},{7,5},{8,10},{9,11},{10,... | collective-permute-start | bytes 393224 | tf_op jit(solution)/shard_map/ppermute | solution.py:282
  35.4 2.7 %collective-permute-start.7 = (bf16[256,1024]{1,0:T(8,128)(2,1)S(1)}, bf16[256,1024]{1,0:T(8,128)(2,1)S(1)}, u32[]{:S(2)}, u32[]{:S(2)}) collective-permute-start(bf16[256,1024]{1,0:T(8,128)(2,1)S(1)} %constant_dynamic-update-slice_fusion.7.refs_3_), channel_id=1, source_target_pairs={{0,24},{1,25},{2,26},{3,27},{4,28},{5,29},{6,30},{7,31},{8,16},{9,... | collective-permute-start | bytes 1572872 | tf_op jit(solution)/shard_map/ppermute | solution.py:282
  38.1 0.0 collective-permute-done.3
  38.1 1.9 %collective-permute-start.4 = (bf16[512,128]{1,0:T(8,128)(2,1)S(1)}, bf16[512,128]{1,0:T(8,128)(2,1)S(1)}, u32[]{:S(2)}, u32[]{:S(2)}) collective-permute-start(bf16[512,128]{1,0:T(8,128)(2,1)S(1)} %collective-permute-done.3), channel_id=1, source_target_pairs={{0,2},{1,3},{2,0},{3,1},{4,6},{5,7},{6,4},{7,5},{8,10},{9,11},{10,... | collective-permute-start | bytes 393224 | tf_op jit(solution)/shard_map/ppermute | solution.py:282
  40.0 0.6 collective-permute-done.1
  40.7 3.3 %collective-permute-start.2 = (bf16[1024,128]{1,0:T(8,128)(2,1)S(1)}, bf16[1024,128]{1,0:T(8,128)(2,1)S(1)}, u32[]{:S(2)}, u32[]{:S(2)}) collective-permute-start(bf16[1024,128]{1,0:T(8,128)(2,1)S(1)} %constant_dynamic-update-slice_fusion.3.refs_1_), channel_id=1, source_target_pairs={{0,1},{1,0},{2,3},{3,2},{4,5},{5,4},{6,7},{7,6},{8,9},{9,8},{10,11... | collective-permute-start | bytes 786440 | tf_op jit(solution)/shard_map/ppermute | solution.py:282
  44.0 3.6 %collective-permute-done.4 = bf16[512,128]{1,0:T(8,128)(2,1)S(1)} collective-permute-done((bf16[512,128]{1,0:T(8,128)(2,1)S(1)}, bf16[512,128]{1,0:T(8,128)(2,1)S(1)}, u32[]{:S(2)}, u32[]{:S(2)}) %collective-permute-start.4) | collective-permute-done | bytes 131104 | tf_op jit(solution)/shard_map/ppermute | solution.py:282
  47.7 0.0 collective-permute-done.5.refs_4_
  47.7 0.0 collective-permute-done.6.refs_5_
  47.7 2.5 %collective-permute-start.8 = (bf16[1024,128]{1,0:T(8,128)(2,1)S(1)}, bf16[1024,128]{1,0:T(8,128)(2,1)S(1)}, u32[]{:S(2)}, u32[]{:S(2)}) collective-permute-start(bf16[1024,128]{1,0:T(8,128)(2,1)S(1)} %pad_maximum_fusion.refs_1_), channel_id=1, source_target_pairs={{0,1},{1,0},{2,3},{3,2},{4,5},{5,4},{6,7},{7,6},{8,9},{9,8},{10,11... | collective-permute-start | bytes 786440 | tf_op jit(solution)/shard_map/ppermute | solution.py:282
  50.2 0.0 copy-start.4
  50.2 0.0 copy-start.3
  50.2 0.7 copy-done.4
  50.9 0.0 copy-done.3
  50.9 0.1 concatenate.20.refs_0_.meta
  51.0 0.6 collective-permute-done.2.refs_2_
  51.5 0.3 collective-permute-done.7.refs_6_
  51.9 7.2 %shard_map.85 = (f32[16,1024]{1,0:T(8,128)S(1)}, bf16[1024,128]{1,0:T(8,128)(2,1)S(1)}, bf16[1024,128]{1,0:T(8,128)(2,1)S(1)}, s32[64]{0:T(128)S(1)}, bf16[4096,...) custom-call(s32[1026]{0:T(1024)S(1)} %concatenate.20.refs_0_.meta, ...), custom_call_target="tpu_custom_call" | custom-call | flops 671088640 | bytes 4194304 | tf_op jit(solution)/shard_map/pallas_call | solution.py:249
  59.1 0.0 collective-permute-done.8.refs_2_
  59.1 3.7 %shard_map.86 = (f32[16,1024]{1,0:T(8,128)S(1)}, bf16[1024,128]{1,0:T(8,128)(2,1)S(1)}, bf16[1024,128]{1,0:T(8,128)(2,1)S(1)}, s32[64]{0:T(128)S(1)}) custom-call(s32[1026]{0:T(1024)S(1)} %concatenate.20.refs_0_.meta, bf16[1024,128]{1,0:T(8,128)(2,1)S(1)} %pad_maximum_fusion.refs_1_, bf16[1024,128]{1,0:T(8,128)(2,1)S(1)} %collective-permute-done.8.refs_2_, ...), custom_call_target="tpu_custom_call" | custom-call | flops 671088640 | bytes 4194304 | tf_op jit(solution)/shard_map/pallas_call | solution.py:249
  62.8 9.4 %all_gather.3.stats = f32[64,1024]{1,0:T(8,128)S(1)} all-gather(f32[16,1024]{1,0:T(8,128)S(1)} %get-tuple-element.40), channel_id=1, replica_groups={{0,8,16,24},{1,9,17,25},{2,10,18,26},{3,11,19,27},{4,12,20,28},{5,13,21..., dimensions={0}, use_global_device_ids=true | all-gather | bytes 327680 | tf_op jit(solution)/shard_map/all_gather | solution.py:330
  72.2 12.1 %shard_map.87 = (bf16[1024,128]{1,0:T(8,128)(2,1)S(1)}, bf16[512,128]{1,0:T(8,128)(2,1)S(1)}, bf16[512,128]{1,0:T(8,128)(2,1)S(1)}, bf16[1024,128]{1,0:T(8,128)(...) custom-call(s32[1026]{0:T(1024)S(1)} %concatenate.20.refs_0_.meta, ...), custom_call_target="tpu_custom_call" | custom-call | flops 3355443200 | bytes 4194304 | tf_op jit(solution)/shard_map/pallas_call | solution.py:262
  84.3 1.9 %collective-permute-start.13 = (bf16[1024,128]{1,0:T(8,128)(2,1)S(1)}, bf16[1024,128]{1,0:T(8,128)(2,1)S(1)}, u32[]{:S(2)}, u32[]{:S(2)}) collective-permute-start(bf16[1024,128]{1,0:T(8,128)(2,1)S(1)} %get-tuple-element.48), channel_id=1, source_target_pairs={{0,1},{1,0},{2,3},{3,2},{4,5},{5,4},{6,7},{7,6},{8,9},{9,8},{10,11... | collective-permute-start | bytes 786440 | tf_op jit(solution)/shard_map/ppermute | solution.py:282
  86.2 3.4 %collective-permute-start.11 = (bf16[1024,128]{1,0:T(8,128)(2,1)S(1)}, bf16[1024,128]{1,0:T(8,128)(2,1)S(1)}, u32[]{:S(2)}, u32[]{:S(2)}) collective-permute-start(bf16[1024,128]{1,0:T(8,128)(2,1)S(1)} %get-tuple-element.45), channel_id=1, source_target_pairs={{0,1},{1,0},{2,3},{3,2},{4,5},{5,4},{6,7},{7,6},{8,9},{9,8},{10,11... | collective-permute-start | bytes 786440 | tf_op jit(solution)/shard_map/ppermute | solution.py:282
  89.6 1.9 %collective-permute-start.9 = (bf16[256,1024]{1,0:T(8,128)(2,1)S(1)}, bf16[256,1024]{1,0:T(8,128)(2,1)S(1)}, u32[]{:S(2)}, u32[]{:S(2)}) collective-permute-start(bf16[256,1024]{1,0:T(8,128)(2,1)S(1)} %get-tuple-element.42), channel_id=1, source_target_pairs={{0,8},{1,9},{2,10},{3,11},{4,12},{5,13},{6,14},{7,15},{8,0},{9,1},... | collective-permute-start | bytes 1572872 | tf_op jit(solution)/shard_map/ppermute | solution.py:282
  91.5 3.0 %collective-permute-done.13 = bf16[1024,128]{1,0:T(8,128)(2,1)S(1)} collective-permute-done((bf16[1024,128]{1,0:T(8,128)(2,1)S(1)}, bf16[1024,128]{1,0:T(8,128)(2,1)S(1)}, u32[]{:S(2)}, u32[]{:S(2)}) %collective-permute-start.13) | collective-permute-done | bytes 262176 | tf_op jit(solution)/shard_map/ppermute | solution.py:282
  94.6 5.4 %collective-permute-start.14 = (bf16[512,128]{1,0:T(8,128)(2,1)S(1)}, bf16[512,128]{1,0:T(8,128)(2,1)S(1)}, u32[]{:S(2)}, u32[]{:S(2)}) collective-permute-start(bf16[512,128]{1,0:T(8,128)(2,1)S(1)} %add_convert_fusion.3), channel_id=1, source_target_pairs={{0,2},{1,3},{2,0},{3,1},{4,6},{5,7},{6,4},{7,5},{8,10},{9,11},{10,... | collective-permute-start | bytes 393224 | tf_op jit(solution)/shard_map/ppermute | solution.py:282
  100.0 0.0 collective-permute-done.11
  100.1 3.0 %collective-permute-start.12 = (bf16[512,128]{1,0:T(8,128)(2,1)S(1)}, bf16[512,128]{1,0:T(8,128)(2,1)S(1)}, u32[]{:S(2)}, u32[]{:S(2)}) collective-permute-start(bf16[512,128]{1,0:T(8,128)(2,1)S(1)} %add_convert_fusion.4), channel_id=1, source_target_pairs={{0,2},{1,3},{2,0},{3,1},{4,6},{5,7},{6,4},{7,5},{8,10},{9,11},{10,... | collective-permute-start | bytes 393224 | tf_op jit(solution)/shard_map/ppermute | solution.py:282
  103.1 6.5 %collective-permute-done.14 = bf16[512,128]{1,0:T(8,128)(2,1)S(1)} collective-permute-done((bf16[512,128]{1,0:T(8,128)(2,1)S(1)}, bf16[512,128]{1,0:T(8,128)(2,1)S(1)}, u32[]{:S(2)}, u32[]{:S(2)}) %collective-permute-start.14) | collective-permute-done | bytes 131104 | tf_op jit(solution)/shard_map/ppermute | solution.py:282
  109.6 0.1 add_convert_fusion.2
  109.7 1.9 %collective-permute-start.15 = (bf16[512,128]{1,0:T(8,128)(2,1)S(1)}, bf16[512,128]{1,0:T(8,128)(2,1)S(1)}, u32[]{:S(2)}, u32[]{:S(2)}) collective-permute-start(bf16[512,128]{1,0:T(8,128)(2,1)S(1)} %add_convert_fusion.2), channel_id=1, source_target_pairs={{32,0},{33,1},{34,2},{35,3},{36,4},{37,5},{38,6},{39,7},{40,8},{41... | collective-permute-start | bytes 393224 | tf_op jit(solution)/shard_map/ppermute | solution.py:293
  111.6 0.1 collective-permute-done.12
  111.7 9.6 %collective-permute-done.15 = bf16[512,128]{1,0:T(8,128)(2,1)S(1)} collective-permute-done((bf16[512,128]{1,0:T(8,128)(2,1)S(1)}, bf16[512,128]{1,0:T(8,128)(2,1)S(1)}, u32[]{:S(2)}, u32[]{:S(2)}) %collective-permute-start.15) | collective-permute-done | bytes 131104 | tf_op jit(solution)/shard_map/ppermute | solution.py:293
  121.3 4.9 %collective-permute-start.16 = (bf16[256,128]{1,0:T(8,128)(2,1)S(1)}, bf16[256,128]{1,0:T(8,128)(2,1)S(1)}, u32[]{:S(2)}, u32[]{:S(2)}) collective-permute-start(bf16[256,128]{1,0:T(8,128)(2,1)S(1)} %add_convert_fusion.6), channel_id=1, source_target_pairs={{0,4},{1,5},{2,6},{3,7},{4,0},{5,1},{6,2},{7,3},{8,12},{9,13},{10,... | collective-permute-start | bytes 196616 | tf_op jit(solution)/shard_map/ppermute | solution.py:282
  126.3 0.0 collective-permute-done.9
  126.3 0.1 add_convert_fusion.1
  126.4 3.4 %collective-permute-start.10 = (bf16[128,1024]{1,0:T(8,128)(2,1)S(1)}, bf16[128,1024]{1,0:T(8,128)(2,1)S(1)}, u32[]{:S(2)}, u32[]{:S(2)}) collective-permute-start(bf16[128,1024]{1,0:T(8,128)(2,1)S(1)} %add_convert_fusion.1), channel_id=1, source_target_pairs={{0,24},{1,25},{2,26},{3,27},{4,28},{5,29},{6,30},{7,31},{8,16},{9,... | collective-permute-start | bytes 786440 | tf_op jit(solution)/shard_map/ppermute | solution.py:282
  129.7 0.5 collective-permute-done.16
  130.3 0.6 fusion
  130.9 3.8 %collective-permute-done.10 = bf16[128,1024]{1,0:T(8,128)(2,1)S(1)} collective-permute-done((bf16[128,1024]{1,0:T(8,128)(2,1)S(1)}, bf16[128,1024]{1,0:T(8,128)(2,1)S(1)}, u32[]{:S(2)}, u32[]{:S(2)}) %collective-permute-start.10) | collective-permute-done | bytes 262176 | tf_op jit(solution)/shard_map/ppermute | solution.py:282
  134.7 0.8 add_convert_fusion
  (10 shorter events, 0.3 us)
Async XLA Ops:
  1.4 9.9 %copy-start = (bf16[128,1024]{1,0:T(8,128)(2,1)S(1)}, bf16[128,1024]{1,0:T(8,128)(2,1)}, u32[]{:S(2)}) copy-start(bf16[128,1024]{1,0:T(8,128)(2,1)} %param.9) | copy-start | bytes 786436
  1.4 13.2 %collective-permute-start = (bf16[256,128]{1,0:T(8,128)(2,1)S(1)}, bf16[256,128]{1,0:T(8,128)(2,1)S(1)}, u32[]{:S(2)}, u32[]{:S(2)}) collective-permute-start(bf16[256,128]{1,0:T(8,128)(2,1)S(1)} %pad_maximum_fusion.1), channel_id=1, source_target_pairs={{0,4},{1,5},{2,6},{3,7},{4,0},{5,1},{6,2},{7,3},{8,12},{9,13},{10,... | collective-permute-start | bytes 196616 | tf_op jit(solution)/shard_map/ppermute | solution.py:282
  11.3 3.3 %copy-start.1 = (bf16[128,128]{1,0:T(8,128)(2,1)S(1)}, bf16[128,128]{1,0:T(8,128)(2,1)}, u32[]{:S(2)}) copy-start(bf16[128,128]{1,0:T(8,128)(2,1)} %param.7) | copy-start | bytes 98308
  11.4 7.8 %copy-start.2 = (bf16[128,128]{1,0:T(8,128)(2,1)S(1)}, bf16[128,128]{1,0:T(8,128)(2,1)}, u32[]{:S(2)}) copy-start(bf16[128,128]{1,0:T(8,128)(2,1)} %param.8) | copy-start | bytes 98308
  11.4 36.3 %collective-permute-start.5 = (bf16[256,1024]{1,0:T(8,128)(2,1)S(1)}, bf16[256,1024]{1,0:T(8,128)(2,1)S(1)}, u32[]{:S(2)}, u32[]{:S(2)}) collective-permute-start(bf16[256,1024]{1,0:T(8,128)(2,1)S(1)} %constant_dynamic-update-slice_fusion.7.refs_3_), channel_id=1, source_target_pairs={{0,8},{1,9},{2,10},{3,11},{4,12},{5,13},{6,14},{7,15},{8,0},{9,1},... | collective-permute-start | bytes 1572872 | tf_op jit(solution)/shard_map/ppermute | solution.py:282
  14.6 33.0 %collective-permute-start.6 = (bf16[256,1024]{1,0:T(8,128)(2,1)S(1)}, bf16[256,1024]{1,0:T(8,128)(2,1)S(1)}, u32[]{:S(2)}, u32[]{:S(2)}) collective-permute-start(bf16[256,1024]{1,0:T(8,128)(2,1)S(1)} %constant_dynamic-update-slice_fusion.7.refs_3_), channel_id=1, source_target_pairs={{0,16},{1,17},{2,18},{3,19},{4,20},{5,21},{6,22},{7,23},{8,24},{9,... | collective-permute-start | bytes 1572872 | tf_op jit(solution)/shard_map/ppermute | solution.py:282
  19.2 18.8 %collective-permute-start.3 = (bf16[512,128]{1,0:T(8,128)(2,1)S(1)}, bf16[512,128]{1,0:T(8,128)(2,1)S(1)}, u32[]{:S(2)}, u32[]{:S(2)}) collective-permute-start(bf16[512,128]{1,0:T(8,128)(2,1)S(1)} %get-tuple-element.53), channel_id=1, source_target_pairs={{0,32},{1,33},{2,34},{3,35},{4,36},{5,37},{6,38},{7,39},{8,40},{9,... | collective-permute-start | bytes 393224 | tf_op jit(solution)/shard_map/ppermute | solution.py:293
  30.8 9.9 %collective-permute-start.1 = (bf16[512,128]{1,0:T(8,128)(2,1)S(1)}, bf16[512,128]{1,0:T(8,128)(2,1)S(1)}, u32[]{:S(2)}, u32[]{:S(2)}) collective-permute-start(bf16[512,128]{1,0:T(8,128)(2,1)S(1)} %get-tuple-element.53), channel_id=1, source_target_pairs={{0,2},{1,3},{2,0},{3,1},{4,6},{5,7},{6,4},{7,5},{8,10},{9,11},{10,... | collective-permute-start | bytes 393224 | tf_op jit(solution)/shard_map/ppermute | solution.py:282
  35.4 16.5 %collective-permute-start.7 = (bf16[256,1024]{1,0:T(8,128)(2,1)S(1)}, bf16[256,1024]{1,0:T(8,128)(2,1)S(1)}, u32[]{:S(2)}, u32[]{:S(2)}) collective-permute-start(bf16[256,1024]{1,0:T(8,128)(2,1)S(1)} %constant_dynamic-update-slice_fusion.7.refs_3_), channel_id=1, source_target_pairs={{0,24},{1,25},{2,26},{3,27},{4,28},{5,29},{6,30},{7,31},{8,16},{9,... | collective-permute-start | bytes 1572872 | tf_op jit(solution)/shard_map/ppermute | solution.py:282
  38.1 9.6 %collective-permute-start.4 = (bf16[512,128]{1,0:T(8,128)(2,1)S(1)}, bf16[512,128]{1,0:T(8,128)(2,1)S(1)}, u32[]{:S(2)}, u32[]{:S(2)}) collective-permute-start(bf16[512,128]{1,0:T(8,128)(2,1)S(1)} %collective-permute-done.3), channel_id=1, source_target_pairs={{0,2},{1,3},{2,0},{3,1},{4,6},{5,7},{6,4},{7,5},{8,10},{9,11},{10,... | collective-permute-start | bytes 393224 | tf_op jit(solution)/shard_map/ppermute | solution.py:282
  40.7 10.9 %collective-permute-start.2 = (bf16[1024,128]{1,0:T(8,128)(2,1)S(1)}, bf16[1024,128]{1,0:T(8,128)(2,1)S(1)}, u32[]{:S(2)}, u32[]{:S(2)}) collective-permute-start(bf16[1024,128]{1,0:T(8,128)(2,1)S(1)} %constant_dynamic-update-slice_fusion.3.refs_1_), channel_id=1, source_target_pairs={{0,1},{1,0},{2,3},{3,2},{4,5},{5,4},{6,7},{7,6},{8,9},{9,8},{10,11... | collective-permute-start | bytes 786440 | tf_op jit(solution)/shard_map/ppermute | solution.py:282
  47.7 11.4 %collective-permute-start.8 = (bf16[1024,128]{1,0:T(8,128)(2,1)S(1)}, bf16[1024,128]{1,0:T(8,128)(2,1)S(1)}, u32[]{:S(2)}, u32[]{:S(2)}) collective-permute-start(bf16[1024,128]{1,0:T(8,128)(2,1)S(1)} %pad_maximum_fusion.refs_1_), channel_id=1, source_target_pairs={{0,1},{1,0},{2,3},{3,2},{4,5},{5,4},{6,7},{7,6},{8,9},{9,8},{10,11... | collective-permute-start | bytes 786440 | tf_op jit(solution)/shard_map/ppermute | solution.py:282
  50.2 0.7 copy-start.4
  50.2 0.7 copy-start.3
  84.3 10.2 %collective-permute-start.13 = (bf16[1024,128]{1,0:T(8,128)(2,1)S(1)}, bf16[1024,128]{1,0:T(8,128)(2,1)S(1)}, u32[]{:S(2)}, u32[]{:S(2)}) collective-permute-start(bf16[1024,128]{1,0:T(8,128)(2,1)S(1)} %get-tuple-element.48), channel_id=1, source_target_pairs={{0,1},{1,0},{2,3},{3,2},{4,5},{5,4},{6,7},{7,6},{8,9},{9,8},{10,11... | collective-permute-start | bytes 786440 | tf_op jit(solution)/shard_map/ppermute | solution.py:282
  86.2 13.8 %collective-permute-start.11 = (bf16[1024,128]{1,0:T(8,128)(2,1)S(1)}, bf16[1024,128]{1,0:T(8,128)(2,1)S(1)}, u32[]{:S(2)}, u32[]{:S(2)}) collective-permute-start(bf16[1024,128]{1,0:T(8,128)(2,1)S(1)} %get-tuple-element.45), channel_id=1, source_target_pairs={{0,1},{1,0},{2,3},{3,2},{4,5},{5,4},{6,7},{7,6},{8,9},{9,8},{10,11... | collective-permute-start | bytes 786440 | tf_op jit(solution)/shard_map/ppermute | solution.py:282
  89.6 36.7 %collective-permute-start.9 = (bf16[256,1024]{1,0:T(8,128)(2,1)S(1)}, bf16[256,1024]{1,0:T(8,128)(2,1)S(1)}, u32[]{:S(2)}, u32[]{:S(2)}) collective-permute-start(bf16[256,1024]{1,0:T(8,128)(2,1)S(1)} %get-tuple-element.42), channel_id=1, source_target_pairs={{0,8},{1,9},{2,10},{3,11},{4,12},{5,13},{6,14},{7,15},{8,0},{9,1},... | collective-permute-start | bytes 1572872 | tf_op jit(solution)/shard_map/ppermute | solution.py:282
  94.6 15.0 %collective-permute-start.14 = (bf16[512,128]{1,0:T(8,128)(2,1)S(1)}, bf16[512,128]{1,0:T(8,128)(2,1)S(1)}, u32[]{:S(2)}, u32[]{:S(2)}) collective-permute-start(bf16[512,128]{1,0:T(8,128)(2,1)S(1)} %add_convert_fusion.3), channel_id=1, source_target_pairs={{0,2},{1,3},{2,0},{3,1},{4,6},{5,7},{6,4},{7,5},{8,10},{9,11},{10,... | collective-permute-start | bytes 393224 | tf_op jit(solution)/shard_map/ppermute | solution.py:282
  100.1 11.6 %collective-permute-start.12 = (bf16[512,128]{1,0:T(8,128)(2,1)S(1)}, bf16[512,128]{1,0:T(8,128)(2,1)S(1)}, u32[]{:S(2)}, u32[]{:S(2)}) collective-permute-start(bf16[512,128]{1,0:T(8,128)(2,1)S(1)} %add_convert_fusion.4), channel_id=1, source_target_pairs={{0,2},{1,3},{2,0},{3,1},{4,6},{5,7},{6,4},{7,5},{8,10},{9,11},{10,... | collective-permute-start | bytes 393224 | tf_op jit(solution)/shard_map/ppermute | solution.py:282
  109.7 11.6 %collective-permute-start.15 = (bf16[512,128]{1,0:T(8,128)(2,1)S(1)}, bf16[512,128]{1,0:T(8,128)(2,1)S(1)}, u32[]{:S(2)}, u32[]{:S(2)}) collective-permute-start(bf16[512,128]{1,0:T(8,128)(2,1)S(1)} %add_convert_fusion.2), channel_id=1, source_target_pairs={{32,0},{33,1},{34,2},{35,3},{36,4},{37,5},{38,6},{39,7},{40,8},{41... | collective-permute-start | bytes 393224 | tf_op jit(solution)/shard_map/ppermute | solution.py:293
  121.3 8.9 %collective-permute-start.16 = (bf16[256,128]{1,0:T(8,128)(2,1)S(1)}, bf16[256,128]{1,0:T(8,128)(2,1)S(1)}, u32[]{:S(2)}, u32[]{:S(2)}) collective-permute-start(bf16[256,128]{1,0:T(8,128)(2,1)S(1)} %add_convert_fusion.6), channel_id=1, source_target_pairs={{0,4},{1,5},{2,6},{3,7},{4,0},{5,1},{6,2},{7,3},{8,12},{9,13},{10,... | collective-permute-start | bytes 196616 | tf_op jit(solution)/shard_map/ppermute | solution.py:282
  126.4 8.3 %collective-permute-start.10 = (bf16[128,1024]{1,0:T(8,128)(2,1)S(1)}, bf16[128,1024]{1,0:T(8,128)(2,1)S(1)}, u32[]{:S(2)}, u32[]{:S(2)}) collective-permute-start(bf16[128,1024]{1,0:T(8,128)(2,1)S(1)} %add_convert_fusion.1), channel_id=1, source_target_pairs={{0,24},{1,25},{2,26},{3,27},{4,28},{5,29},{6,30},{7,31},{8,16},{9,... | collective-permute-start | bytes 786440 | tf_op jit(solution)/shard_map/ppermute | solution.py:282

commit v5 on v4

--- a/solution.py
+++ b/solution.py
@@ -16,6 +16,7 @@
 FAR = 4
 STATS = 16
 LIST = 16
+EVERY = 32
 NY = 4
 NZ = 8
 CHUNK = 256
@@ -45,9 +46,9 @@
             gs[to : to + BLOCK, :] = ref[BLOCK : 2 * BLOCK, h * HD : (h + 1) * HD]
 
 
-def place(low, high, ks, vs):
+def place(low, high, ks, vs, base):
     for s in range(NZ):
-        ref, lo, to = (low, high)[s // 4], (s % 4) * 2 * BLOCK, s * BLOCK
+        ref, lo, to = (low, high)[s // 4], (s % 4) * 2 * BLOCK, (base + s) * BLOCK
         ks[to : to + BLOCK, :] = ref[lo : lo + BLOCK, :]
         vs[to : to + BLOCK, :] = ref[lo + BLOCK : lo + 2 * BLOCK, :]
 
@@ -76,10 +77,23 @@
             sees = q_doc[r] == k_doc[s]
             if not before:
                 sees = sees & (k_at[s] < q_at[r])
-            lists[r * LIST + count] = jnp.int32(s)
+            lists[r * LIST + count] = jnp.int32(s + NZ if before else s)
             count = count + sees.astype(jnp.int32)
-        lists[r * LIST + count] = jnp.int32(0)
+        for i in range(4):
+            lists[r * LIST + count + i] = jnp.int32(0)
         lists[r * LIST + LIST - 1] = count
+
+
+def join_lists(first, second, every):
+    for r in range(NY):
+        at, more = first[r * LIST + LIST - 1], second[r * LIST + LIST - 1]
+        for i in range(NZ):
+            every[r * EVERY + i] = first[r * LIST + i]
+        for i in range(NZ + 1):
+            every[r * EVERY + at + i] = jnp.where(i < more, second[r * LIST + i], 0)
+        for i in range(4):
+            every[r * EVERY + at + more + i] = jnp.int32(0)
+        every[r * EVERY + EVERY - 1] = at + more
 
 
 def diagonal_mask():
@@ -88,19 +102,27 @@
     return k_at <= q_at
 
 
-def for_pairs(before, lists, pair):
-    if not before:
-        pair(0, (0,), 0.0, True)
+def for_quads(diagonal, lists, stride, pair):
+    if diagonal:
+        pair(0, (0,), (0.0,), True)
 
     @pl.loop(0, NY)
     def _(r):
-        count = lists[r * LIST + LIST - 1]
-
-        @pl.loop(0, (count + 1) // 2)
+        count = lists[r * stride + stride - 1]
+        quads = (count + 1) // 4
+
+        def step(width, at):
+            slots = [lists[r * stride + at + i] for i in range(width)]
+            biases = [jnp.where(at + i < count, 0.0, -NEG) for i in range(width)]
+            pair(r, slots, biases, False)
+
+        @pl.loop(0, quads)
         def _(j):
-            at = r * LIST + 2 * j
-            bias = jnp.where(2 * j + 1 < count, 0.0, -NEG)
-            pair(r, (lists[at], lists[at + 1]), bias, False)
+            step(4, 4 * j)
+
+        @pl.loop(0, (count - 4 * quads + 1) // 2)
+        def _(j):
+            step(2, 4 * quads + 2 * j)
 
 
 def rows_of(ref, slots):
@@ -109,17 +131,21 @@
 
 def stats_kernel(before, *refs):
     if before:
-        meta, low, high, qs, gs, earlier, stats, ks, vs, lists = refs
+        meta, low, high, qs, gs, earlier, own_k, own_v, own_lists, stats, ks, vs, lists, every = refs
         stats[...] = earlier[...]
+        ks[0 : NZ * BLOCK, :] = own_k[...]
+        vs[0 : NZ * BLOCK, :] = own_v[...]
     else:
         meta, low, high, *qg, stats, ks, vs, lists, qs, gs = refs
         stack_heads(qg, qs, gs)
         stats[0:NY, :] = jnp.full((NY, ROWS), NEG, jnp.float32)
         stats[NY:STATS, :] = jnp.zeros((STATS - NY, ROWS), jnp.float32)
     list_pairs(meta, before, lists)
-    place(low, high, ks, vs)
-
-    def pair(r, slots, bias, diagonal):
+    if before:
+        join_lists(own_lists, lists, every)
+    place(low, high, ks, vs, NZ if before else 0)
+
+    def pair(r, slots, biases, diagonal):
         key, value = rows_of(ks, slots), rows_of(vs, slots)
         for c in range(ROWS // CHUNK):
             rows = pl.ds(r * ROWS + c * CHUNK, CHUNK)
@@ -128,7 +154,6 @@
             dprob = dot_nt(value, gs[rows, :])
             if diagonal:
                 scores = jnp.where(diagonal_mask(), scores, NEG)
-            biases = (0.0, bias)[: len(slots)]
             top = stats[pl.ds(r, 1), cols]
             new_top = top
             for i, less in enumerate(biases):
@@ -146,10 +171,10 @@
             stats[pl.ds(NY + r, 1), cols] = total
             stats[pl.ds(2 * NY + r, 1), cols] = product
 
-    for_pairs(before, lists, pair)
-
-
-def grads_kernel(meta, own_lists, before_lists, qs, gs, own_k, own_v, before_k, before_v, stats, *rest):
+    for_quads(not before, lists, LIST, pair)
+
+
+def grads_kernel(meta, every, qs, gs, ks, vs, stats, *rest):
     b_high, b_mid, b_pair, o_high, o_mid, o_one, o_zero, dq0, dq12, dq3 = rest[:10]
     lse, delta, w_low, d_low, dk, dv, dq = rest[10:]
     dk[...] = jnp.zeros_like(dk)
@@ -170,7 +195,7 @@
         lse[r : r + 1, :] = top + jnp.log2(total)
         delta[r : r + 1, :] = product / total
 
-    def pair(ks, vs, base, r, slots, bias, diagonal):
+    def pair(r, slots, biases, diagonal):
         key, value = rows_of(ks, slots), rows_of(vs, slots)
         count = len(slots) * BLOCK
         for c in range(ROWS // CHUNK):
@@ -178,7 +203,7 @@
             cols = pl.ds(c * CHUNK, CHUNK)
             scores = dot_nt(key, qs[rows, :]) * SCALE2
             dprob = dot_nt(value, gs[rows, :])
-            for i, less in enumerate((0.0, bias)[: len(slots)]):
+            for i, less in enumerate(biases):
                 half = slice(i * BLOCK, (i + 1) * BLOCK)
                 probs = jnp.exp2(scores[half] - (lse[pl.ds(r, 1), cols] + less))
                 if diagonal:
@@ -191,12 +216,11 @@
         dv_part = dot_nn(w_low[0:count, :], gs[rows, :])
         for i, s in enumerate(slots):
             half = slice(i * BLOCK, (i + 1) * BLOCK)
-            dk[pl.ds((base + s) * BLOCK, BLOCK), :] += dk_part[half]
-            dv[pl.ds((base + s) * BLOCK, BLOCK), :] += dv_part[half]
+            dk[pl.ds(s * BLOCK, BLOCK), :] += dk_part[half]
+            dv[pl.ds(s * BLOCK, BLOCK), :] += dv_part[half]
         dq[pl.ds(r * HD, HD), :] += dot_tn(key, d_low[0:count, :])
 
-    for_pairs(False, own_lists, functools.partial(pair, own_k, own_v, 0))
-    for_pairs(True, before_lists, functools.partial(pair, before_k, before_v, NZ))
+    for_quads(True, every, EVERY, pair)
 
     def write(slots, out, at):
         for s in slots:
@@ -235,21 +259,26 @@
 
 
 def run_stats(before, *args):
-    blocks = jax.ShapeDtypeStruct((NZ * BLOCK, HD), jnp.bfloat16)
+    blocks = jax.ShapeDtypeStruct(((2 if before else 1) * NZ * BLOCK, HD), jnp.bfloat16)
     outs = [
         jax.ShapeDtypeStruct((STATS, ROWS), jnp.float32),
         blocks,
         blocks,
         jax.ShapeDtypeStruct((NY * LIST,), jnp.int32),
     ]
+    in_specs = [smem()] + [vmem()] * (len(args) - 1)
     specs = [vmem()] * 3 + [smem()]
-    if not before:
+    if before:
+        outs.append(jax.ShapeDtypeStruct((NY * EVERY,), jnp.int32))
+        specs.append(smem())
+        in_specs[-1] = smem()
+    else:
         outs += [jax.ShapeDtypeStruct((NY * ROWS, HD), jnp.bfloat16)] * 2
         specs += [vmem()] * 2
     return pl.pallas_call(
         functools.partial(stats_kernel, before),
         out_shape=outs,
-        in_specs=[smem()] + [vmem()] * (len(args) - 1),
+        in_specs=in_specs,
         out_specs=specs,
         compiler_params=pltpu.CompilerParams(vmem_limit_bytes=VMEM_LIMIT),
         cost_estimate=cost(2, 10),
@@ -262,13 +291,13 @@
     return pl.pallas_call(
         grads_kernel,
         out_shape=outs,
-        in_specs=[smem()] * 3 + [vmem()] * (len(args) - 3),
+        in_specs=[smem()] * 2 + [vmem()] * (len(args) - 2),
         out_specs=[vmem()] * len(outs),
         scratch_shapes=[
             pltpu.VMEM((NY, ROWS), jnp.float32),
             pltpu.VMEM((NY, ROWS), jnp.float32),
-            pltpu.VMEM((2 * BLOCK, ROWS), jnp.bfloat16),
-            pltpu.VMEM((2 * BLOCK, ROWS), jnp.bfloat16),
+            pltpu.VMEM((4 * BLOCK, ROWS), jnp.bfloat16),
+            pltpu.VMEM((4 * BLOCK, ROWS), jnp.bfloat16),
             pltpu.VMEM((2 * NZ * BLOCK, HD), jnp.float32),
             pltpu.VMEM((2 * NZ * BLOCK, HD), jnp.float32),
             pltpu.VMEM((NY * HD, ROWS), jnp.float32),
@@ -323,13 +352,13 @@
     stats, own_k, own_v, own_lists, qs, gs = run_stats(
         False, meta, own_low, own_high, qg0, qg1, qg2, qg3
     )
-    stats, before_k, before_v, before_lists = run_stats(
-        True, meta, before_low, before_high, qs, gs, stats
+    stats, ks, vs, _, every = run_stats(
+        True, meta, before_low, before_high, qs, gs, stats, own_k, own_v, own_lists
     )
     along_y = [[y * NZ + z for y in range(NY)] for z in range(NZ)]
     all_stats = lax.all_gather(stats, "inner", axis=0, tiled=True, axis_index_groups=along_y)
     b_high, b_mid, b_pair, o_high, o_mid, o_one, o_zero, dq0, dq12, dq3 = run_grads(
-        meta, own_lists, before_lists, qs, gs, own_k, own_v, before_k, before_v, all_stats
+        meta, every, qs, gs, ks, vs, all_stats
     )
 
     b_near = swap(b_high, 1)
@@ -338,12 +367,13 @@
     b_far = swap(add_low(b_mid, b_near[2 * one :]), 2)
     back = across(add_low(b_pair, b_near[: 2 * one], b_far), -1)
     o_far = swap(add_low(o_mid, o_near[2 * one :]), 2)
-    dq3 = add_low(dq3, e12[BLOCK:])
-    e3 = swap(dq3, 3 * NZ)
+    e3 = swap(add_low(dq3, e12[BLOCK:]), 3 * NZ)
     o_four = swap(add_low(o_one, o_near[one : 2 * one], o_far[one:], back[one:]), 4)
     grad_queries = add_low(dq0, e12[:BLOCK], e3)
-    totals = add_low(o_zero, o_near[:one], o_far[:one], back[:one], o_four)
-    return grad_queries, totals[:BLOCK], totals[BLOCK:]
+    terms = (o_zero, o_near[:one], o_far[:one], back[:one], o_four)
+    grad_keys = add_low(*[term[:BLOCK] for term in terms])
+    grad_values = add_low(*[term[BLOCK:] for term in terms])
+    return grad_queries, grad_keys, grad_values
 
 
 def solution(mesh):

time: 138 us -> 137 us (level); the launches traced: 136 us -> 136 us
  Pallas kernels: 23 us -> 15.6 us
  starting transfers between devices: 69.1 us -> 74 us
  waiting for transfers between devices: 28.7 us -> 31 us
    ppermute x15, starting transfers between devices: 55.7 us -> 60.6 us  [swap(): return lax.ppermute(array, 'inner', [(i, i ^ flip) for i in range(GROUP)])]
    pallas_call x1, Pallas kernels: 12.1 us -> 7.74 us  [run_grads(): pl.pallas_call(grads_kernel, out_shape=outs, in_specs=[smem()] * 2 + [vme...]
    pallas_call x2, Pallas kernels: 10.9 us -> 7.82 us  [run_stats(): pl.pallas_call(functools.partial(stats_kernel, before), out_shape=outs, i...]
    ppermute x15, waiting for transfers between devices: 19 us -> 21.3 us  [swap(): return lax.ppermute(array, 'inner', [(i, i ^ flip) for i in range(GROUP)])]
  transfers between devices with their start and end apart: 17 -> 17, of which waited for: 10 -> 11; matrix products, arithmetic and copies ran while one was open for 2% -> 2% of each run, Pallas kernels for 5% -> 3%
where the time goes in v5:
time: 137 us; the launch traced here: 136 us
  starting transfers between devices  74 us (54%)
  waiting for transfers between devices  31 us (23%)
  Pallas kernels  15.6 us (11%)
  blocking collectives  10.3 us (8%)
  other arithmetic  2.54 us (2%)
  local copies, waits for them, and re-layouts  1.84 us (1%)
    ppermute x15, starting transfers between devices, swap(): return lax.ppermute(array, 'inner', [(i, i ^ flip) for i in range(GROUP)])  60.6 us
    ppermute x15, waiting for transfers between devices, swap(): return lax.ppermute(array, 'inner', [(i, i ^ flip) for i in range(GROUP)])  21.3 us
    ppermute x2, starting transfers between devices, across(): return lax.ppermute(array, ('outer', 'inner'), pairs)  13.4 us
    all_gather x1, blocking collectives, shards(): lax.all_gather(stats, 'inner', axis=0, tiled=True, axis_index_groups=alon...  10.3 us
    ppermute x2, waiting for transfers between devices, across(): return lax.ppermute(array, ('outer', 'inner'), pairs)  9.66 us
    pallas_call x2, Pallas kernels, run_stats(): pl.pallas_call(functools.partial(stats_kernel, before), out_shape=outs, i...  7.82 us
    pallas_call x1, Pallas kernels, run_grads(): pl.pallas_call(grads_kernel, out_shape=outs, in_specs=[smem()] * 2 + [vme...  7.74 us
  transfers between devices with their start and end apart: 17, of which 11 were waited for; matrix products, arithmetic and copies ran while one was open for 2% of the time, Pallas kernels for 3%

profile of v5, /device:TPU:7, one launch (start us, length us, event | category | flops | bytes accessed | tf_op | source)
XLA Modules:
  0.0 136.2 jit_solution(1315853650168638475)
XLA Ops:
  0.6 0.8 pad_maximum_fusion.1
  1.4 0.0 copy-start
  1.4 8.9 %collective-permute-start = (bf16[256,128]{1,0:T(8,128)(2,1)S(1)}, bf16[256,128]{1,0:T(8,128)(2,1)S(1)}, u32[]{:S(2)}, u32[]{:S(2)}) collective-permute-start(bf16[256,128]{1,0:T(8,128)(2,1)S(1)} %pad_maximum_fusion.1), channel_id=1, source_target_pairs={{0,4},{1,5},{2,6},{3,7},{4,0},{5,1},{6,2},{7,3},{8,12},{9,13},{10,... | collective-permute-start | bytes 196616 | tf_op jit(solution)/shard_map/ppermute | solution.py:311
  10.4 1.0 constant_dynamic-update-slice_fusion.4
  11.3 0.0 copy-done
  11.3 0.0 copy-start.1
  11.4 0.0 copy-start.2
  11.4 3.2 %collective-permute-start.3 = (bf16[256,1024]{1,0:T(8,128)(2,1)S(1)}, bf16[256,1024]{1,0:T(8,128)(2,1)S(1)}, u32[]{:S(2)}, u32[]{:S(2)}) collective-permute-start(bf16[256,1024]{1,0:T(8,128)(2,1)S(1)} %constant_dynamic-update-slice_fusion.3.refs_3_), channel_id=1, source_target_pairs={{0,8},{1,9},{2,10},{3,11},{4,12},{5,13},{6,14},{7,15},{8,0},{9,1},... | collective-permute-start | bytes 1572872 | tf_op jit(solution)/shard_map/ppermute | solution.py:311
  14.6 0.0 copy-done.1
  14.6 0.0 collective-permute-done
  14.6 4.5 %collective-permute-start.4 = (bf16[256,1024]{1,0:T(8,128)(2,1)S(1)}, bf16[256,1024]{1,0:T(8,128)(2,1)S(1)}, u32[]{:S(2)}, u32[]{:S(2)}) collective-permute-start(bf16[256,1024]{1,0:T(8,128)(2,1)S(1)} %constant_dynamic-update-slice_fusion.3.refs_3_), channel_id=1, source_target_pairs={{0,16},{1,17},{2,18},{3,19},{4,20},{5,21},{6,22},{7,23},{8,24},{9,... | collective-permute-start | bytes 1572872 | tf_op jit(solution)/shard_map/ppermute | solution.py:311
  19.2 0.0 copy-done.2
  19.2 11.5 %collective-permute-start.1 = (bf16[512,128]{1,0:T(8,128)(2,1)S(1)}, bf16[512,128]{1,0:T(8,128)(2,1)S(1)}, u32[]{:S(2)}, u32[]{:S(2)}) collective-permute-start(bf16[512,128]{1,0:T(8,128)(2,1)S(1)} %get-tuple-element.54), channel_id=1, source_target_pairs={{0,32},{1,33},{2,34},{3,35},{4,36},{5,37},{6,38},{7,39},{8,40},{9,... | collective-permute-start | bytes 393224 | tf_op jit(solution)/shard_map/ppermute | solution.py:322
  30.8 4.6 %collective-permute-start.6 = (bf16[512,128]{1,0:T(8,128)(2,1)S(1)}, bf16[512,128]{1,0:T(8,128)(2,1)S(1)}, u32[]{:S(2)}, u32[]{:S(2)}) collective-permute-start(bf16[512,128]{1,0:T(8,128)(2,1)S(1)} %get-tuple-element.54), channel_id=1, source_target_pairs={{0,2},{1,3},{2,0},{3,1},{4,6},{5,7},{6,4},{7,5},{8,10},{9,11},{10,... | collective-permute-start | bytes 393224 | tf_op jit(solution)/shard_map/ppermute | solution.py:311
  35.4 2.7 %collective-permute-start.8 = (bf16[256,1024]{1,0:T(8,128)(2,1)S(1)}, bf16[256,1024]{1,0:T(8,128)(2,1)S(1)}, u32[]{:S(2)}, u32[]{:S(2)}) collective-permute-start(bf16[256,1024]{1,0:T(8,128)(2,1)S(1)} %constant_dynamic-update-slice_fusion.3.refs_3_), channel_id=1, source_target_pairs={{0,24},{1,25},{2,26},{3,27},{4,28},{5,29},{6,30},{7,31},{8,16},{9,... | collective-permute-start | bytes 1572872 | tf_op jit(solution)/shard_map/ppermute | solution.py:311
  38.1 0.0 collective-permute-done.1
  38.1 1.9 %collective-permute-start.2 = (bf16[512,128]{1,0:T(8,128)(2,1)S(1)}, bf16[512,128]{1,0:T(8,128)(2,1)S(1)}, u32[]{:S(2)}, u32[]{:S(2)}) collective-permute-start(bf16[512,128]{1,0:T(8,128)(2,1)S(1)} %collective-permute-done.1), channel_id=1, source_target_pairs={{0,2},{1,3},{2,0},{3,1},{4,6},{5,7},{6,4},{7,5},{8,10},{9,11},{10,... | collective-permute-start | bytes 393224 | tf_op jit(solution)/shard_map/ppermute | solution.py:311
  40.0 0.6 collective-permute-done.6
  40.7 3.3 %collective-permute-start.7 = (bf16[1024,128]{1,0:T(8,128)(2,1)S(1)}, bf16[1024,128]{1,0:T(8,128)(2,1)S(1)}, u32[]{:S(2)}, u32[]{:S(2)}) collective-permute-start(bf16[1024,128]{1,0:T(8,128)(2,1)S(1)} %constant_dynamic-update-slice_fusion.5.refs_1_), channel_id=1, source_target_pairs={{0,1},{1,0},{2,3},{3,2},{4,5},{5,4},{6,7},{7,6},{8,9},{9,8},{10,11... | collective-permute-start | bytes 786440 | tf_op jit(solution)/shard_map/ppermute | solution.py:311
  44.0 3.6 %collective-permute-done.2 = bf16[512,128]{1,0:T(8,128)(2,1)S(1)} collective-permute-done((bf16[512,128]{1,0:T(8,128)(2,1)S(1)}, bf16[512,128]{1,0:T(8,128)(2,1)S(1)}, u32[]{:S(2)}, u32[]{:S(2)}) %collective-permute-start.2) | collective-permute-done | bytes 131104 | tf_op jit(solution)/shard_map/ppermute | solution.py:311
  47.7 0.0 collective-permute-done.3.refs_4_
  47.7 0.0 collective-permute-done.4.refs_5_
  47.7 2.5 %collective-permute-start.5 = (bf16[1024,128]{1,0:T(8,128)(2,1)S(1)}, bf16[1024,128]{1,0:T(8,128)(2,1)S(1)}, u32[]{:S(2)}, u32[]{:S(2)}) collective-permute-start(bf16[1024,128]{1,0:T(8,128)(2,1)S(1)} %pad_maximum_fusion.refs_1_), channel_id=1, source_target_pairs={{0,1},{1,0},{2,3},{3,2},{4,5},{5,4},{6,7},{7,6},{8,9},{9,8},{10,11... | collective-permute-start | bytes 786440 | tf_op jit(solution)/shard_map/ppermute | solution.py:311
  50.2 0.0 copy-start.4
  50.2 0.0 copy-start.3
  50.2 0.7 copy-done.4
  50.9 0.0 copy-done.3
  50.9 0.1 concatenate.20.refs_0_.meta
  51.0 0.6 collective-permute-done.7.refs_2_
  51.5 0.3 collective-permute-done.8.refs_6_
  51.9 4.2 %shard_map.85 = (f32[16,1024]{1,0:T(8,128)S(1)}, bf16[1024,128]{1,0:T(8,128)(2,1)S(1)}, bf16[1024,128]{1,0:T(8,128)(2,1)S(1)}, s32[64]{0:T(128)S(1)}, bf16[4096,...) custom-call(s32[1026]{0:T(1024)S(1)} %concatenate.20.refs_0_.meta, ...), custom_call_target="tpu_custom_call" | custom-call | flops 671088640 | bytes 4194304 | tf_op jit(solution)/shard_map/pallas_call | solution.py:278
  56.1 1.2 collective-permute-done.5.refs_2_
  57.3 3.6 %shard_map.86 = (f32[16,1024]{1,0:T(8,128)S(1)}, bf16[2048,128]{1,0:T(8,128)(2,1)S(1)}, bf16[2048,128]{1,0:T(8,128)(2,1)S(1)}, s32[64]{0:T(128)}, s32[128]{0:T(128)S(1)}) custom-call(s32[1026]{0:T(1024)S(1)} %concatenate.20.refs_0_.meta, bf16[1024,128]{1,0:T(8,128)(2,1)S(1)} %pad_maximum_fusion.refs_1_, ...), custom_call_target="tpu_custom_call" | custom-call | flops 671088640 | bytes 4194304 | tf_op jit(solution)/shard_map/pallas_call | solution.py:278
  60.9 10.3 %all_gather.3.stats = f32[64,1024]{1,0:T(8,128)S(1)} all-gather(f32[16,1024]{1,0:T(8,128)S(1)} %get-tuple-element.40), channel_id=1, replica_groups={{0,8,16,24},{1,9,17,25},{2,10,18,26},{3,11,19,27},{4,12,20,28},{5,13,21..., dimensions={0}, use_global_device_ids=true | all-gather | bytes 327680 | tf_op jit(solution)/shard_map/all_gather | solution.py:359
  71.3 7.7 %shard_map.87 = (bf16[1024,128]{1,0:T(8,128)(2,1)S(1)}, bf16[512,128]{1,0:T(8,128)(2,1)S(1)}, bf16[512,128]{1,0:T(8,128)(2,1)S(1)}, bf16[1024,128]{1,0:T(8,128)(...) custom-call(s32[1026]{0:T(1024)S(1)} %concatenate.20.refs_0_.meta, ...), custom_call_target="tpu_custom_call" | custom-call | flops 3355443200 | bytes 4194304 | tf_op jit(solution)/shard_map/pallas_call | solution.py:291
  79.0 6.3 %collective-permute-start.13 = (bf16[1024,128]{1,0:T(8,128)(2,1)S(1)}, bf16[1024,128]{1,0:T(8,128)(2,1)S(1)}, u32[]{:S(2)}, u32[]{:S(2)}) collective-permute-start(bf16[1024,128]{1,0:T(8,128)(2,1)S(1)} %get-tuple-element.48), channel_id=1, source_target_pairs={{0,1},{1,0},{2,3},{3,2},{4,5},{5,4},{6,7},{7,6},{8,9},{9,8},{10,11... | collective-permute-start | bytes 786440 | tf_op jit(solution)/shard_map/ppermute | solution.py:311
  85.4 1.9 %collective-permute-start.11 = (bf16[1024,128]{1,0:T(8,128)(2,1)S(1)}, bf16[1024,128]{1,0:T(8,128)(2,1)S(1)}, u32[]{:S(2)}, u32[]{:S(2)}) collective-permute-start(bf16[1024,128]{1,0:T(8,128)(2,1)S(1)} %get-tuple-element.45), channel_id=1, source_target_pairs={{0,1},{1,0},{2,3},{3,2},{4,5},{5,4},{6,7},{7,6},{8,9},{9,8},{10,11... | collective-permute-start | bytes 786440 | tf_op jit(solution)/shard_map/ppermute | solution.py:311
  87.3 1.9 %collective-permute-start.9 = (bf16[256,1024]{1,0:T(8,128)(2,1)S(1)}, bf16[256,1024]{1,0:T(8,128)(2,1)S(1)}, u32[]{:S(2)}, u32[]{:S(2)}) collective-permute-start(bf16[256,1024]{1,0:T(8,128)(2,1)S(1)} %get-tuple-element.42), channel_id=1, source_target_pairs={{0,8},{1,9},{2,10},{3,11},{4,12},{5,13},{6,14},{7,15},{8,0},{9,1},... | collective-permute-start | bytes 1572872 | tf_op jit(solution)/shard_map/ppermute | solution.py:311
  89.2 3.1 %collective-permute-done.13 = bf16[1024,128]{1,0:T(8,128)(2,1)S(1)} collective-permute-done((bf16[1024,128]{1,0:T(8,128)(2,1)S(1)}, bf16[1024,128]{1,0:T(8,128)(2,1)S(1)}, u32[]{:S(2)}, u32[]{:S(2)}) %collective-permute-start.13) | collective-permute-done | bytes 262176 | tf_op jit(solution)/shard_map/ppermute | solution.py:311
  92.3 2.7 %collective-permute-start.14 = (bf16[512,128]{1,0:T(8,128)(2,1)S(1)}, bf16[512,128]{1,0:T(8,128)(2,1)S(1)}, u32[]{:S(2)}, u32[]{:S(2)}) collective-permute-start(bf16[512,128]{1,0:T(8,128)(2,1)S(1)} %add_convert_fusion.3), channel_id=1, source_target_pairs={{0,2},{1,3},{2,0},{3,1},{4,6},{5,7},{6,4},{7,5},{8,10},{9,11},{10,... | collective-permute-start | bytes 393224 | tf_op jit(solution)/shard_map/ppermute | solution.py:311
  95.0 1.8 %collective-permute-done.11 = bf16[1024,128]{1,0:T(8,128)(2,1)S(1)} collective-permute-done((bf16[1024,128]{1,0:T(8,128)(2,1)S(1)}, bf16[1024,128]{1,0:T(8,128)(2,1)S(1)}, u32[]{:S(2)}, u32[]{:S(2)}) %collective-permute-start.11) | collective-permute-done | bytes 262176 | tf_op jit(solution)/shard_map/ppermute | solution.py:311
  96.8 2.8 %collective-permute-start.12 = (bf16[512,128]{1,0:T(8,128)(2,1)S(1)}, bf16[512,128]{1,0:T(8,128)(2,1)S(1)}, u32[]{:S(2)}, u32[]{:S(2)}) collective-permute-start(bf16[512,128]{1,0:T(8,128)(2,1)S(1)} %add_convert_fusion.4), channel_id=1, source_target_pairs={{0,2},{1,3},{2,0},{3,1},{4,6},{5,7},{6,4},{7,5},{8,10},{9,11},{10,... | collective-permute-start | bytes 393224 | tf_op jit(solution)/shard_map/ppermute | solution.py:311
  99.6 2.6 %collective-permute-done.14 = bf16[512,128]{1,0:T(8,128)(2,1)S(1)} collective-permute-done((bf16[512,128]{1,0:T(8,128)(2,1)S(1)}, bf16[512,128]{1,0:T(8,128)(2,1)S(1)}, u32[]{:S(2)}, u32[]{:S(2)}) %collective-permute-start.14) | collective-permute-done | bytes 131104 | tf_op jit(solution)/shard_map/ppermute | solution.py:311
  102.2 0.1 add_convert_fusion.2
  102.3 1.9 %collective-permute-start.15 = (bf16[512,128]{1,0:T(8,128)(2,1)S(1)}, bf16[512,128]{1,0:T(8,128)(2,1)S(1)}, u32[]{:S(2)}, u32[]{:S(2)}) collective-permute-start(bf16[512,128]{1,0:T(8,128)(2,1)S(1)} %add_convert_fusion.2), channel_id=1, source_target_pairs={{32,0},{33,1},{34,2},{35,3},{36,4},{37,5},{38,6},{39,7},{40,8},{41... | collective-permute-start | bytes 393224 | tf_op jit(solution)/shard_map/ppermute | solution.py:322
  104.2 1.7 %collective-permute-done.12 = bf16[512,128]{1,0:T(8,128)(2,1)S(1)} collective-permute-done((bf16[512,128]{1,0:T(8,128)(2,1)S(1)}, bf16[512,128]{1,0:T(8,128)(2,1)S(1)}, u32[]{:S(2)}, u32[]{:S(2)}) %collective-permute-start.12) | collective-permute-done | bytes 131104 | tf_op jit(solution)/shard_map/ppermute | solution.py:311
  106.0 9.7 %collective-permute-done.15 = bf16[512,128]{1,0:T(8,128)(2,1)S(1)} collective-permute-done((bf16[512,128]{1,0:T(8,128)(2,1)S(1)}, bf16[512,128]{1,0:T(8,128)(2,1)S(1)}, u32[]{:S(2)}, u32[]{:S(2)}) %collective-permute-start.15) | collective-permute-done | bytes 131104 | tf_op jit(solution)/shard_map/ppermute | solution.py:322
  115.7 11.3 %collective-permute-start.16 = (bf16[256,128]{1,0:T(8,128)(2,1)S(1)}, bf16[256,128]{1,0:T(8,128)(2,1)S(1)}, u32[]{:S(2)}, u32[]{:S(2)}) collective-permute-start(bf16[256,128]{1,0:T(8,128)(2,1)S(1)} %add_convert_fusion.5), channel_id=1, source_target_pairs={{0,4},{1,5},{2,6},{3,7},{4,0},{5,1},{6,2},{7,3},{8,12},{9,13},{10,... | collective-permute-start | bytes 196616 | tf_op jit(solution)/shard_map/ppermute | solution.py:311
  127.0 0.0 collective-permute-done.9
  127.0 0.1 add_convert_fusion.1
  127.1 1.9 %collective-permute-start.10 = (bf16[128,1024]{1,0:T(8,128)(2,1)S(1)}, bf16[128,1024]{1,0:T(8,128)(2,1)S(1)}, u32[]{:S(2)}, u32[]{:S(2)}) collective-permute-start(bf16[128,1024]{1,0:T(8,128)(2,1)S(1)} %add_convert_fusion.1), channel_id=1, source_target_pairs={{0,24},{1,25},{2,26},{3,27},{4,28},{5,29},{6,30},{7,31},{8,16},{9,... | collective-permute-start | bytes 786440 | tf_op jit(solution)/shard_map/ppermute | solution.py:311
  129.0 0.0 collective-permute-done.16
  129.0 0.7 add_convert_fusion.6
  129.7 5.7 %collective-permute-done.10 = bf16[128,1024]{1,0:T(8,128)(2,1)S(1)} collective-permute-done((bf16[128,1024]{1,0:T(8,128)(2,1)S(1)}, bf16[128,1024]{1,0:T(8,128)(2,1)S(1)}, u32[]{:S(2)}, u32[]{:S(2)}) %collective-permute-start.10) | collective-permute-done | bytes 262176 | tf_op jit(solution)/shard_map/ppermute | solution.py:311
  135.4 0.8 add_convert_fusion
  (9 shorter events, 0.2 us)
Async XLA Ops:
  1.4 9.9 %copy-start = (bf16[128,1024]{1,0:T(8,128)(2,1)S(1)}, bf16[128,1024]{1,0:T(8,128)(2,1)}, u32[]{:S(2)}) copy-start(bf16[128,1024]{1,0:T(8,128)(2,1)} %param.9) | copy-start | bytes 786436
  1.4 13.2 %collective-permute-start = (bf16[256,128]{1,0:T(8,128)(2,1)S(1)}, bf16[256,128]{1,0:T(8,128)(2,1)S(1)}, u32[]{:S(2)}, u32[]{:S(2)}) collective-permute-start(bf16[256,128]{1,0:T(8,128)(2,1)S(1)} %pad_maximum_fusion.1), channel_id=1, source_target_pairs={{0,4},{1,5},{2,6},{3,7},{4,0},{5,1},{6,2},{7,3},{8,12},{9,13},{10,... | collective-permute-start | bytes 196616 | tf_op jit(solution)/shard_map/ppermute | solution.py:311
  11.3 3.3 %copy-start.1 = (bf16[128,128]{1,0:T(8,128)(2,1)S(1)}, bf16[128,128]{1,0:T(8,128)(2,1)}, u32[]{:S(2)}) copy-start(bf16[128,128]{1,0:T(8,128)(2,1)} %param.7) | copy-start | bytes 98308
  11.4 7.8 %copy-start.2 = (bf16[128,128]{1,0:T(8,128)(2,1)S(1)}, bf16[128,128]{1,0:T(8,128)(2,1)}, u32[]{:S(2)}) copy-start(bf16[128,128]{1,0:T(8,128)(2,1)} %param.8) | copy-start | bytes 98308
  11.4 36.3 %collective-permute-start.3 = (bf16[256,1024]{1,0:T(8,128)(2,1)S(1)}, bf16[256,1024]{1,0:T(8,128)(2,1)S(1)}, u32[]{:S(2)}, u32[]{:S(2)}) collective-permute-start(bf16[256,1024]{1,0:T(8,128)(2,1)S(1)} %constant_dynamic-update-slice_fusion.3.refs_3_), channel_id=1, source_target_pairs={{0,8},{1,9},{2,10},{3,11},{4,12},{5,13},{6,14},{7,15},{8,0},{9,1},... | collective-permute-start | bytes 1572872 | tf_op jit(solution)/shard_map/ppermute | solution.py:311
  14.6 33.0 %collective-permute-start.4 = (bf16[256,1024]{1,0:T(8,128)(2,1)S(1)}, bf16[256,1024]{1,0:T(8,128)(2,1)S(1)}, u32[]{:S(2)}, u32[]{:S(2)}) collective-permute-start(bf16[256,1024]{1,0:T(8,128)(2,1)S(1)} %constant_dynamic-update-slice_fusion.3.refs_3_), channel_id=1, source_target_pairs={{0,16},{1,17},{2,18},{3,19},{4,20},{5,21},{6,22},{7,23},{8,24},{9,... | collective-permute-start | bytes 1572872 | tf_op jit(solution)/shard_map/ppermute | solution.py:311
  19.2 18.8 %collective-permute-start.1 = (bf16[512,128]{1,0:T(8,128)(2,1)S(1)}, bf16[512,128]{1,0:T(8,128)(2,1)S(1)}, u32[]{:S(2)}, u32[]{:S(2)}) collective-permute-start(bf16[512,128]{1,0:T(8,128)(2,1)S(1)} %get-tuple-element.54), channel_id=1, source_target_pairs={{0,32},{1,33},{2,34},{3,35},{4,36},{5,37},{6,38},{7,39},{8,40},{9,... | collective-permute-start | bytes 393224 | tf_op jit(solution)/shard_map/ppermute | solution.py:322
  30.8 9.9 %collective-permute-start.6 = (bf16[512,128]{1,0:T(8,128)(2,1)S(1)}, bf16[512,128]{1,0:T(8,128)(2,1)S(1)}, u32[]{:S(2)}, u32[]{:S(2)}) collective-permute-start(bf16[512,128]{1,0:T(8,128)(2,1)S(1)} %get-tuple-element.54), channel_id=1, source_target_pairs={{0,2},{1,3},{2,0},{3,1},{4,6},{5,7},{6,4},{7,5},{8,10},{9,11},{10,... | collective-permute-start | bytes 393224 | tf_op jit(solution)/shard_map/ppermute | solution.py:311
  35.4 16.5 %collective-permute-start.8 = (bf16[256,1024]{1,0:T(8,128)(2,1)S(1)}, bf16[256,1024]{1,0:T(8,128)(2,1)S(1)}, u32[]{:S(2)}, u32[]{:S(2)}) collective-permute-start(bf16[256,1024]{1,0:T(8,128)(2,1)S(1)} %constant_dynamic-update-slice_fusion.3.refs_3_), channel_id=1, source_target_pairs={{0,24},{1,25},{2,26},{3,27},{4,28},{5,29},{6,30},{7,31},{8,16},{9,... | collective-permute-start | bytes 1572872 | tf_op jit(solution)/shard_map/ppermute | solution.py:311
  38.1 9.6 %collective-permute-start.2 = (bf16[512,128]{1,0:T(8,128)(2,1)S(1)}, bf16[512,128]{1,0:T(8,128)(2,1)S(1)}, u32[]{:S(2)}, u32[]{:S(2)}) collective-permute-start(bf16[512,128]{1,0:T(8,128)(2,1)S(1)} %collective-permute-done.1), channel_id=1, source_target_pairs={{0,2},{1,3},{2,0},{3,1},{4,6},{5,7},{6,4},{7,5},{8,10},{9,11},{10,... | collective-permute-start | bytes 393224 | tf_op jit(solution)/shard_map/ppermute | solution.py:311
  40.7 10.9 %collective-permute-start.7 = (bf16[1024,128]{1,0:T(8,128)(2,1)S(1)}, bf16[1024,128]{1,0:T(8,128)(2,1)S(1)}, u32[]{:S(2)}, u32[]{:S(2)}) collective-permute-start(bf16[1024,128]{1,0:T(8,128)(2,1)S(1)} %constant_dynamic-update-slice_fusion.5.refs_1_), channel_id=1, source_target_pairs={{0,1},{1,0},{2,3},{3,2},{4,5},{5,4},{6,7},{7,6},{8,9},{9,8},{10,11... | collective-permute-start | bytes 786440 | tf_op jit(solution)/shard_map/ppermute | solution.py:311
  47.7 9.6 %collective-permute-start.5 = (bf16[1024,128]{1,0:T(8,128)(2,1)S(1)}, bf16[1024,128]{1,0:T(8,128)(2,1)S(1)}, u32[]{:S(2)}, u32[]{:S(2)}) collective-permute-start(bf16[1024,128]{1,0:T(8,128)(2,1)S(1)} %pad_maximum_fusion.refs_1_), channel_id=1, source_target_pairs={{0,1},{1,0},{2,3},{3,2},{4,5},{5,4},{6,7},{7,6},{8,9},{9,8},{10,11... | collective-permute-start | bytes 786440 | tf_op jit(solution)/shard_map/ppermute | solution.py:311
  50.2 0.7 copy-start.4
  50.2 0.7 copy-start.3
  79.0 13.3 %collective-permute-start.13 = (bf16[1024,128]{1,0:T(8,128)(2,1)S(1)}, bf16[1024,128]{1,0:T(8,128)(2,1)S(1)}, u32[]{:S(2)}, u32[]{:S(2)}) collective-permute-start(bf16[1024,128]{1,0:T(8,128)(2,1)S(1)} %get-tuple-element.48), channel_id=1, source_target_pairs={{0,1},{1,0},{2,3},{3,2},{4,5},{5,4},{6,7},{7,6},{8,9},{9,8},{10,11... | collective-permute-start | bytes 786440 | tf_op jit(solution)/shard_map/ppermute | solution.py:311
  85.4 11.5 %collective-permute-start.11 = (bf16[1024,128]{1,0:T(8,128)(2,1)S(1)}, bf16[1024,128]{1,0:T(8,128)(2,1)S(1)}, u32[]{:S(2)}, u32[]{:S(2)}) collective-permute-start(bf16[1024,128]{1,0:T(8,128)(2,1)S(1)} %get-tuple-element.45), channel_id=1, source_target_pairs={{0,1},{1,0},{2,3},{3,2},{4,5},{5,4},{6,7},{7,6},{8,9},{9,8},{10,11... | collective-permute-start | bytes 786440 | tf_op jit(solution)/shard_map/ppermute | solution.py:311
  87.3 39.7 %collective-permute-start.9 = (bf16[256,1024]{1,0:T(8,128)(2,1)S(1)}, bf16[256,1024]{1,0:T(8,128)(2,1)S(1)}, u32[]{:S(2)}, u32[]{:S(2)}) collective-permute-start(bf16[256,1024]{1,0:T(8,128)(2,1)S(1)} %get-tuple-element.42), channel_id=1, source_target_pairs={{0,8},{1,9},{2,10},{3,11},{4,12},{5,13},{6,14},{7,15},{8,0},{9,1},... | collective-permute-start | bytes 1572872 | tf_op jit(solution)/shard_map/ppermute | solution.py:311
  92.3 9.9 %collective-permute-start.14 = (bf16[512,128]{1,0:T(8,128)(2,1)S(1)}, bf16[512,128]{1,0:T(8,128)(2,1)S(1)}, u32[]{:S(2)}, u32[]{:S(2)}) collective-permute-start(bf16[512,128]{1,0:T(8,128)(2,1)S(1)} %add_convert_fusion.3), channel_id=1, source_target_pairs={{0,2},{1,3},{2,0},{3,1},{4,6},{5,7},{6,4},{7,5},{8,10},{9,11},{10,... | collective-permute-start | bytes 393224 | tf_op jit(solution)/shard_map/ppermute | solution.py:311
  96.8 9.1 %collective-permute-start.12 = (bf16[512,128]{1,0:T(8,128)(2,1)S(1)}, bf16[512,128]{1,0:T(8,128)(2,1)S(1)}, u32[]{:S(2)}, u32[]{:S(2)}) collective-permute-start(bf16[512,128]{1,0:T(8,128)(2,1)S(1)} %add_convert_fusion.4), channel_id=1, source_target_pairs={{0,2},{1,3},{2,0},{3,1},{4,6},{5,7},{6,4},{7,5},{8,10},{9,11},{10,... | collective-permute-start | bytes 393224 | tf_op jit(solution)/shard_map/ppermute | solution.py:311
  102.3 13.3 %collective-permute-start.15 = (bf16[512,128]{1,0:T(8,128)(2,1)S(1)}, bf16[512,128]{1,0:T(8,128)(2,1)S(1)}, u32[]{:S(2)}, u32[]{:S(2)}) collective-permute-start(bf16[512,128]{1,0:T(8,128)(2,1)S(1)} %add_convert_fusion.2), channel_id=1, source_target_pairs={{32,0},{33,1},{34,2},{35,3},{36,4},{37,5},{38,6},{39,7},{40,8},{41... | collective-permute-start | bytes 393224 | tf_op jit(solution)/shard_map/ppermute | solution.py:322
  115.7 13.4 %collective-permute-start.16 = (bf16[256,128]{1,0:T(8,128)(2,1)S(1)}, bf16[256,128]{1,0:T(8,128)(2,1)S(1)}, u32[]{:S(2)}, u32[]{:S(2)}) collective-permute-start(bf16[256,128]{1,0:T(8,128)(2,1)S(1)} %add_convert_fusion.5), channel_id=1, source_target_pairs={{0,4},{1,5},{2,6},{3,7},{4,0},{5,1},{6,2},{7,3},{8,12},{9,13},{10,... | collective-permute-start | bytes 196616 | tf_op jit(solution)/shard_map/ppermute | solution.py:311
  127.1 8.3 %collective-permute-start.10 = (bf16[128,1024]{1,0:T(8,128)(2,1)S(1)}, bf16[128,1024]{1,0:T(8,128)(2,1)S(1)}, u32[]{:S(2)}, u32[]{:S(2)}) collective-permute-start(bf16[128,1024]{1,0:T(8,128)(2,1)S(1)} %add_convert_fusion.1), channel_id=1, source_target_pairs={{0,24},{1,25},{2,26},{3,27},{4,28},{5,29},{6,30},{7,31},{8,16},{9,... | collective-permute-start | bytes 786440 | tf_op jit(solution)/shard_map/ppermute | solution.py:311

commit v6 on v5

--- a/solution.py
+++ b/solution.py
@@ -346,7 +346,7 @@
     own_low = jnp.concatenate([own_pair, swap(own_pair, 2)], axis=0)
     own_high = swap(own_low, 1)
     before_low = jnp.concatenate([before_pair, swap(before_pair, 2)], axis=0)
-    before_low, qg1, qg2 = lax.optimization_barrier((before_low, qg1, qg2))
+    before_low, qg1, qg3 = lax.optimization_barrier((before_low, qg1, qg3))
     before_high = swap(before_low, 1)
 
     stats, own_k, own_v, own_lists, qs, gs = run_stats(
@@ -369,6 +369,7 @@
     o_far = swap(add_low(o_mid, o_near[2 * one :]), 2)
     e3 = swap(add_low(dq3, e12[BLOCK:]), 3 * NZ)
     o_four = swap(add_low(o_one, o_near[one : 2 * one], o_far[one:], back[one:]), 4)
+    o_four, e3 = lax.optimization_barrier((o_four, e3))
     grad_queries = add_low(dq0, e12[:BLOCK], e3)
     terms = (o_zero, o_near[:one], o_far[:one], back[:one], o_four)
     grad_keys = add_low(*[term[:BLOCK] for term in terms])

time: 137 us -> 132 us (0.964)
  waiting for transfers between devices: 31 us -> 18.3 us
  Pallas kernels: 15.6 us -> 19.5 us
  starting transfers between devices: 74 us -> 77.8 us
    ppermute x2, waiting for transfers between devices: 9.66 us -> 0.01 us  [across(): return lax.ppermute(array, ('outer', 'inner'), pairs)]
    ppermute x2, starting transfers between devices: 13.4 us -> 22.4 us  [across(): return lax.ppermute(array, ('outer', 'inner'), pairs)]
    ppermute x15, starting transfers between devices: 60.6 us -> 55.4 us  [swap(): return lax.ppermute(array, 'inner', [(i, i ^ flip) for i in range(GROUP)])]
    ppermute x15, waiting for transfers between devices: 21.3 us -> 18.3 us  [swap(): return lax.ppermute(array, 'inner', [(i, i ^ flip) for i in range(GROUP)])]
    pallas_call x1, Pallas kernels: 7.74 us -> 9.94 us  [run_grads(): pl.pallas_call(grads_kernel, out_shape=outs, in_specs=[smem()] * 2 + [vme...]
    pallas_call x2, Pallas kernels: 7.82 us -> 9.57 us  [run_stats(): pl.pallas_call(functools.partial(stats_kernel, before), out_shape=outs, i...]
  transfers between devices with their start and end apart: 17 -> 17, of which waited for: 11 -> 8; matrix products, arithmetic and copies ran while one was open for 2% -> 1% of each run, Pallas kernels for 3% -> 2%
where the time goes in v6:
time: 132 us; the launch traced here: 131 us
  starting transfers between devices  77.8 us (59%)
  Pallas kernels  19.5 us (15%)
  waiting for transfers between devices  18.3 us (14%)
  blocking collectives  9.81 us (7%)
  other arithmetic  2.54 us (2%)
  local copies, waits for them, and re-layouts  1.84 us (1%)
    ppermute x15, starting transfers between devices, swap(): return lax.ppermute(array, 'inner', [(i, i ^ flip) for i in range(GROUP)])  55.4 us
    ppermute x2, starting transfers between devices, across(): return lax.ppermute(array, ('outer', 'inner'), pairs)  22.4 us
    ppermute x15, waiting for transfers between devices, swap(): return lax.ppermute(array, 'inner', [(i, i ^ flip) for i in range(GROUP)])  18.3 us
    pallas_call x1, Pallas kernels, run_grads(): pl.pallas_call(grads_kernel, out_shape=outs, in_specs=[smem()] * 2 + [vme...  9.94 us
    all_gather x1, blocking collectives, shards(): lax.all_gather(stats, 'inner', axis=0, tiled=True, axis_index_groups=alon...  9.81 us
    pallas_call x2, Pallas kernels, run_stats(): pl.pallas_call(functools.partial(stats_kernel, before), out_shape=outs, i...  9.57 us
  transfers between devices with their start and end apart: 17, of which 8 were waited for; matrix products, arithmetic and copies ran while one was open for 1% of the time, Pallas kernels for 2%

profile of v6, /device:TPU:7, one launch (start us, length us, event | category | flops | bytes accessed | tf_op | source)
XLA Modules:
  0.0 130.8 jit_solution(6681317191724447695)
XLA Ops:
  0.6 0.8 pad_maximum_fusion.1
  1.4 0.0 copy-start
  1.4 8.9 %collective-permute-start = (bf16[256,128]{1,0:T(8,128)(2,1)S(1)}, bf16[256,128]{1,0:T(8,128)(2,1)S(1)}, u32[]{:S(2)}, u32[]{:S(2)}) collective-permute-start(bf16[256,128]{1,0:T(8,128)(2,1)S(1)} %pad_maximum_fusion.1), channel_id=1, source_target_pairs={{0,4},{1,5},{2,6},{3,7},{4,0},{5,1},{6,2},{7,3},{8,12},{9,13},{10,... | collective-permute-start | bytes 196616 | tf_op jit(solution)/shard_map/ppermute | solution.py:311
  10.4 1.0 constant_dynamic-update-slice_fusion.4
  11.3 0.0 copy-done
  11.3 0.0 copy-start.1
  11.4 0.0 copy-start.2
  11.4 3.2 %collective-permute-start.3 = (bf16[256,1024]{1,0:T(8,128)(2,1)S(1)}, bf16[256,1024]{1,0:T(8,128)(2,1)S(1)}, u32[]{:S(2)}, u32[]{:S(2)}) collective-permute-start(bf16[256,1024]{1,0:T(8,128)(2,1)S(1)} %constant_dynamic-update-slice_fusion.3.refs_3_), channel_id=1, source_target_pairs={{0,8},{1,9},{2,10},{3,11},{4,12},{5,13},{6,14},{7,15},{8,0},{9,1},... | collective-permute-start | bytes 1572872 | tf_op jit(solution)/shard_map/ppermute | solution.py:311
  14.6 0.0 copy-done.1
  14.6 0.0 collective-permute-done
  14.6 3.8 %collective-permute-start.4 = (bf16[256,1024]{1,0:T(8,128)(2,1)S(1)}, bf16[256,1024]{1,0:T(8,128)(2,1)S(1)}, u32[]{:S(2)}, u32[]{:S(2)}) collective-permute-start(bf16[256,1024]{1,0:T(8,128)(2,1)S(1)} %constant_dynamic-update-slice_fusion.3.refs_3_), channel_id=1, source_target_pairs={{0,24},{1,25},{2,26},{3,27},{4,28},{5,29},{6,30},{7,31},{8,16},{9,... | collective-permute-start | bytes 1572872 | tf_op jit(solution)/shard_map/ppermute | solution.py:311
  18.5 0.0 copy-done.2
  18.5 12.1 %collective-permute-start.1 = (bf16[512,128]{1,0:T(8,128)(2,1)S(1)}, bf16[512,128]{1,0:T(8,128)(2,1)S(1)}, u32[]{:S(2)}, u32[]{:S(2)}) collective-permute-start(bf16[512,128]{1,0:T(8,128)(2,1)S(1)} %get-tuple-element.58), channel_id=1, source_target_pairs={{0,32},{1,33},{2,34},{3,35},{4,36},{5,37},{6,38},{7,39},{8,40},{9,... | collective-permute-start | bytes 393224 | tf_op jit(solution)/shard_map/ppermute | solution.py:322
  30.6 4.6 %collective-permute-start.6 = (bf16[512,128]{1,0:T(8,128)(2,1)S(1)}, bf16[512,128]{1,0:T(8,128)(2,1)S(1)}, u32[]{:S(2)}, u32[]{:S(2)}) collective-permute-start(bf16[512,128]{1,0:T(8,128)(2,1)S(1)} %get-tuple-element.58), channel_id=1, source_target_pairs={{0,2},{1,3},{2,0},{3,1},{4,6},{5,7},{6,4},{7,5},{8,10},{9,11},{10,... | collective-permute-start | bytes 393224 | tf_op jit(solution)/shard_map/ppermute | solution.py:311
  35.2 2.3 %collective-permute-start.8 = (bf16[256,1024]{1,0:T(8,128)(2,1)S(1)}, bf16[256,1024]{1,0:T(8,128)(2,1)S(1)}, u32[]{:S(2)}, u32[]{:S(2)}) collective-permute-start(bf16[256,1024]{1,0:T(8,128)(2,1)S(1)} %constant_dynamic-update-slice_fusion.3.refs_3_), channel_id=1, source_target_pairs={{0,16},{1,17},{2,18},{3,19},{4,20},{5,21},{6,22},{7,23},{8,24},{9,... | collective-permute-start | bytes 1572872 | tf_op jit(solution)/shard_map/ppermute | solution.py:311
  37.5 0.0 collective-permute-done.1
  37.5 1.9 %collective-permute-start.2 = (bf16[512,128]{1,0:T(8,128)(2,1)S(1)}, bf16[512,128]{1,0:T(8,128)(2,1)S(1)}, u32[]{:S(2)}, u32[]{:S(2)}) collective-permute-start(bf16[512,128]{1,0:T(8,128)(2,1)S(1)} %collective-permute-done.1), channel_id=1, source_target_pairs={{0,2},{1,3},{2,0},{3,1},{4,6},{5,7},{6,4},{7,5},{8,10},{9,11},{10,... | collective-permute-start | bytes 393224 | tf_op jit(solution)/shard_map/ppermute | solution.py:311
  39.4 0.8 collective-permute-done.6
  40.2 3.2 %collective-permute-start.7 = (bf16[1024,128]{1,0:T(8,128)(2,1)S(1)}, bf16[1024,128]{1,0:T(8,128)(2,1)S(1)}, u32[]{:S(2)}, u32[]{:S(2)}) collective-permute-start(bf16[1024,128]{1,0:T(8,128)(2,1)S(1)} %constant_dynamic-update-slice_fusion.5.refs_1_), channel_id=1, source_target_pairs={{0,1},{1,0},{2,3},{3,2},{4,5},{5,4},{6,7},{7,6},{8,9},{9,8},{10,11... | collective-permute-start | bytes 786440 | tf_op jit(solution)/shard_map/ppermute | solution.py:311
  43.4 3.5 %collective-permute-done.2 = bf16[512,128]{1,0:T(8,128)(2,1)S(1)} collective-permute-done((bf16[512,128]{1,0:T(8,128)(2,1)S(1)}, bf16[512,128]{1,0:T(8,128)(2,1)S(1)}, u32[]{:S(2)}, u32[]{:S(2)}) %collective-permute-start.2) | collective-permute-done | bytes 131104 | tf_op jit(solution)/shard_map/ppermute | solution.py:311
  46.9 0.0 collective-permute-done.3.refs_4_
  46.9 0.0 collective-permute-done.4.refs_6_
  46.9 2.2 %collective-permute-start.5 = (bf16[1024,128]{1,0:T(8,128)(2,1)S(1)}, bf16[1024,128]{1,0:T(8,128)(2,1)S(1)}, u32[]{:S(2)}, u32[]{:S(2)}) collective-permute-start(bf16[1024,128]{1,0:T(8,128)(2,1)S(1)} %pad_maximum_fusion.refs_1_), channel_id=1, source_target_pairs={{0,1},{1,0},{2,3},{3,2},{4,5},{5,4},{6,7},{7,6},{8,9},{9,8},{10,11... | collective-permute-start | bytes 786440 | tf_op jit(solution)/shard_map/ppermute | solution.py:311
  49.1 0.0 copy-start.4
  49.1 0.0 copy-start.3
  49.2 0.7 copy-done.4
  49.8 0.0 copy-done.3
  49.8 0.1 concatenate.20.refs_0_.meta
  49.9 0.5 collective-permute-done.7.refs_2_
  50.4 0.0 collective-permute-done.8.refs_5_
  50.4 3.2 %shard_map.85 = (f32[16,1024]{1,0:T(8,128)S(1)}, bf16[1024,128]{1,0:T(8,128)(2,1)S(1)}, bf16[1024,128]{1,0:T(8,128)(2,1)S(1)}, s32[64]{0:T(128)S(1)}, bf16[4096,...) custom-call(s32[1026]{0:T(1024)S(1)} %concatenate.20.refs_0_.meta, ...), custom_call_target="tpu_custom_call" | custom-call | flops 671088640 | bytes 4194304 | tf_op jit(solution)/shard_map/pallas_call | solution.py:278
  53.6 3.0 %collective-permute-done.5.refs_2_ = bf16[1024,128]{1,0:T(8,128)(2,1)S(1)} collective-permute-done((bf16[1024,128]{1,0:T(8,128)(2,1)S(1)}, bf16[1024,128]{1,0:T(8,128)(2,1)S(1)}, u32[]{:S(2)}, u32[]{:S(2)}) %collective-permute-start.5) | collective-permute-done | bytes 262176 | tf_op jit(solution)/shard_map/ppermute | solution.py:311
  56.6 6.4 %shard_map.86 = (f32[16,1024]{1,0:T(8,128)S(1)}, bf16[2048,128]{1,0:T(8,128)(2,1)S(1)}, bf16[2048,128]{1,0:T(8,128)(2,1)S(1)}, s32[64]{0:T(128)}, s32[128]{0:T(128)S(1)}) custom-call(s32[1026]{0:T(1024)S(1)} %concatenate.20.refs_0_.meta, bf16[1024,128]{1,0:T(8,128)(2,1)S(1)} %pad_maximum_fusion.refs_1_, ...), custom_call_target="tpu_custom_call" | custom-call | flops 671088640 | bytes 4194304 | tf_op jit(solution)/shard_map/pallas_call | solution.py:278
  63.0 9.8 %all_gather.3.stats = f32[64,1024]{1,0:T(8,128)S(1)} all-gather(f32[16,1024]{1,0:T(8,128)S(1)} %get-tuple-element.42), channel_id=1, replica_groups={{0,8,16,24},{1,9,17,25},{2,10,18,26},{3,11,19,27},{4,12,20,28},{5,13,21..., dimensions={0}, use_global_device_ids=true | all-gather | bytes 327680 | tf_op jit(solution)/shard_map/all_gather | solution.py:359
  72.8 9.9 %shard_map.87 = (bf16[1024,128]{1,0:T(8,128)(2,1)S(1)}, bf16[512,128]{1,0:T(8,128)(2,1)S(1)}, bf16[512,128]{1,0:T(8,128)(2,1)S(1)}, bf16[1024,128]{1,0:T(8,128)(...) custom-call(s32[1026]{0:T(1024)S(1)} %concatenate.20.refs_0_.meta, ...), custom_call_target="tpu_custom_call" | custom-call | flops 3355443200 | bytes 4194304 | tf_op jit(solution)/shard_map/pallas_call | solution.py:291
  82.8 1.9 %collective-permute-start.12 = (bf16[1024,128]{1,0:T(8,128)(2,1)S(1)}, bf16[1024,128]{1,0:T(8,128)(2,1)S(1)}, u32[]{:S(2)}, u32[]{:S(2)}) collective-permute-start(bf16[1024,128]{1,0:T(8,128)(2,1)S(1)} %get-tuple-element.49), channel_id=1, source_target_pairs={{0,1},{1,0},{2,3},{3,2},{4,5},{5,4},{6,7},{7,6},{8,9},{9,8},{10,11... | collective-permute-start | bytes 786440 | tf_op jit(solution)/shard_map/ppermute | solution.py:311
  84.7 3.4 %collective-permute-start.10 = (bf16[1024,128]{1,0:T(8,128)(2,1)S(1)}, bf16[1024,128]{1,0:T(8,128)(2,1)S(1)}, u32[]{:S(2)}, u32[]{:S(2)}) collective-permute-start(bf16[1024,128]{1,0:T(8,128)(2,1)S(1)} %get-tuple-element.46), channel_id=1, source_target_pairs={{0,1},{1,0},{2,3},{3,2},{4,5},{5,4},{6,7},{7,6},{8,9},{9,8},{10,11... | collective-permute-start | bytes 786440 | tf_op jit(solution)/shard_map/ppermute | solution.py:311
  88.1 1.9 %collective-permute-start.9 = (bf16[256,1024]{1,0:T(8,128)(2,1)S(1)}, bf16[256,1024]{1,0:T(8,128)(2,1)S(1)}, u32[]{:S(2)}, u32[]{:S(2)}) collective-permute-start(bf16[256,1024]{1,0:T(8,128)(2,1)S(1)} %get-tuple-element.44), channel_id=1, source_target_pairs={{0,8},{1,9},{2,10},{3,11},{4,12},{5,13},{6,14},{7,15},{8,0},{9,1},... | collective-permute-start | bytes 1572872 | tf_op jit(solution)/shard_map/ppermute | solution.py:311
  90.0 2.9 %collective-permute-done.12 = bf16[1024,128]{1,0:T(8,128)(2,1)S(1)} collective-permute-done((bf16[1024,128]{1,0:T(8,128)(2,1)S(1)}, bf16[1024,128]{1,0:T(8,128)(2,1)S(1)}, u32[]{:S(2)}, u32[]{:S(2)}) %collective-permute-start.12) | collective-permute-done | bytes 262176 | tf_op jit(solution)/shard_map/ppermute | solution.py:311
  92.9 1.9 %collective-permute-start.13 = (bf16[512,128]{1,0:T(8,128)(2,1)S(1)}, bf16[512,128]{1,0:T(8,128)(2,1)S(1)}, u32[]{:S(2)}, u32[]{:S(2)}) collective-permute-start(bf16[512,128]{1,0:T(8,128)(2,1)S(1)} %add_convert_fusion.3), channel_id=1, source_target_pairs={{0,2},{1,3},{2,0},{3,1},{4,6},{5,7},{6,4},{7,5},{8,10},{9,11},{10,... | collective-permute-start | bytes 393224 | tf_op jit(solution)/shard_map/ppermute | solution.py:311
  94.8 3.4 %collective-permute-done.10 = bf16[1024,128]{1,0:T(8,128)(2,1)S(1)} collective-permute-done((bf16[1024,128]{1,0:T(8,128)(2,1)S(1)}, bf16[1024,128]{1,0:T(8,128)(2,1)S(1)}, u32[]{:S(2)}, u32[]{:S(2)}) %collective-permute-start.10) | collective-permute-done | bytes 262176 | tf_op jit(solution)/shard_map/ppermute | solution.py:311
  98.3 1.9 %collective-permute-start.11 = (bf16[512,128]{1,0:T(8,128)(2,1)S(1)}, bf16[512,128]{1,0:T(8,128)(2,1)S(1)}, u32[]{:S(2)}, u32[]{:S(2)}) collective-permute-start(bf16[512,128]{1,0:T(8,128)(2,1)S(1)} %add_convert_fusion.4), channel_id=1, source_target_pairs={{0,2},{1,3},{2,0},{3,1},{4,6},{5,7},{6,4},{7,5},{8,10},{9,11},{10,... | collective-permute-start | bytes 393224 | tf_op jit(solution)/shard_map/ppermute | solution.py:311
  100.2 0.4 collective-permute-done.13
  100.6 0.1 add_convert_fusion.2
  100.6 10.4 %collective-permute-start.14 = (bf16[512,128]{1,0:T(8,128)(2,1)S(1)}, bf16[512,128]{1,0:T(8,128)(2,1)S(1)}, u32[]{:S(2)}, u32[]{:S(2)}) collective-permute-start(bf16[512,128]{1,0:T(8,128)(2,1)S(1)} %add_convert_fusion.2), channel_id=1, source_target_pairs={{32,0},{33,1},{34,2},{35,3},{36,4},{37,5},{38,6},{39,7},{40,8},{41... | collective-permute-start | bytes 393224 | tf_op jit(solution)/shard_map/ppermute | solution.py:322
  111.1 0.0 collective-permute-done.9
  111.1 0.1 add_convert_fusion.1
  111.1 1.9 %collective-permute-start.16 = (bf16[128,1024]{1,0:T(8,128)(2,1)S(1)}, bf16[128,1024]{1,0:T(8,128)(2,1)S(1)}, u32[]{:S(2)}, u32[]{:S(2)}) collective-permute-start(bf16[128,1024]{1,0:T(8,128)(2,1)S(1)} %add_convert_fusion.1), channel_id=1, source_target_pairs={{0,24},{1,25},{2,26},{3,27},{4,28},{5,29},{6,30},{7,31},{8,16},{9,... | collective-permute-start | bytes 786440 | tf_op jit(solution)/shard_map/ppermute | solution.py:311
  113.1 0.0 collective-permute-done.11
  113.1 0.0 collective-permute-done.14
  113.1 12.3 %collective-permute-start.15 = (bf16[256,128]{1,0:T(8,128)(2,1)S(1)}, bf16[256,128]{1,0:T(8,128)(2,1)S(1)}, u32[]{:S(2)}, u32[]{:S(2)}) collective-permute-start(bf16[256,128]{1,0:T(8,128)(2,1)S(1)} %add_convert_fusion.5), channel_id=1, source_target_pairs={{0,4},{1,5},{2,6},{3,7},{4,0},{5,1},{6,2},{7,3},{8,12},{9,13},{10,... | collective-permute-start | bytes 196616 | tf_op jit(solution)/shard_map/ppermute | solution.py:311
  125.4 3.9 %collective-permute-done.15 = bf16[256,128]{1,0:T(8,128)(2,1)S(1)} collective-permute-done((bf16[256,128]{1,0:T(8,128)(2,1)S(1)}, bf16[256,128]{1,0:T(8,128)(2,1)S(1)}, u32[]{:S(2)}, u32[]{:S(2)}) %collective-permute-start.15) | collective-permute-done | bytes 65568 | tf_op jit(solution)/shard_map/ppermute | solution.py:311
  129.3 0.0 collective-permute-done.16
  129.3 0.7 add_convert_fusion.6
  130.0 0.8 add_convert_fusion
  (9 shorter events, 0.2 us)
Async XLA Ops:
  1.4 9.9 %copy-start = (bf16[128,1024]{1,0:T(8,128)(2,1)S(1)}, bf16[128,1024]{1,0:T(8,128)(2,1)}, u32[]{:S(2)}) copy-start(bf16[128,1024]{1,0:T(8,128)(2,1)} %param.9) | copy-start | bytes 786436
  1.4 13.2 %collective-permute-start = (bf16[256,128]{1,0:T(8,128)(2,1)S(1)}, bf16[256,128]{1,0:T(8,128)(2,1)S(1)}, u32[]{:S(2)}, u32[]{:S(2)}) collective-permute-start(bf16[256,128]{1,0:T(8,128)(2,1)S(1)} %pad_maximum_fusion.1), channel_id=1, source_target_pairs={{0,4},{1,5},{2,6},{3,7},{4,0},{5,1},{6,2},{7,3},{8,12},{9,13},{10,... | collective-permute-start | bytes 196616 | tf_op jit(solution)/shard_map/ppermute | solution.py:311
  11.3 3.3 %copy-start.1 = (bf16[128,128]{1,0:T(8,128)(2,1)S(1)}, bf16[128,128]{1,0:T(8,128)(2,1)}, u32[]{:S(2)}) copy-start(bf16[128,128]{1,0:T(8,128)(2,1)} %param.7) | copy-start | bytes 98308
  11.4 7.1 %copy-start.2 = (bf16[128,128]{1,0:T(8,128)(2,1)S(1)}, bf16[128,128]{1,0:T(8,128)(2,1)}, u32[]{:S(2)}) copy-start(bf16[128,128]{1,0:T(8,128)(2,1)} %param.8) | copy-start | bytes 98308
  11.4 35.5 %collective-permute-start.3 = (bf16[256,1024]{1,0:T(8,128)(2,1)S(1)}, bf16[256,1024]{1,0:T(8,128)(2,1)S(1)}, u32[]{:S(2)}, u32[]{:S(2)}) collective-permute-start(bf16[256,1024]{1,0:T(8,128)(2,1)S(1)} %constant_dynamic-update-slice_fusion.3.refs_3_), channel_id=1, source_target_pairs={{0,8},{1,9},{2,10},{3,11},{4,12},{5,13},{6,14},{7,15},{8,0},{9,1},... | collective-permute-start | bytes 1572872 | tf_op jit(solution)/shard_map/ppermute | solution.py:311
  14.6 32.3 %collective-permute-start.4 = (bf16[256,1024]{1,0:T(8,128)(2,1)S(1)}, bf16[256,1024]{1,0:T(8,128)(2,1)S(1)}, u32[]{:S(2)}, u32[]{:S(2)}) collective-permute-start(bf16[256,1024]{1,0:T(8,128)(2,1)S(1)} %constant_dynamic-update-slice_fusion.3.refs_3_), channel_id=1, source_target_pairs={{0,24},{1,25},{2,26},{3,27},{4,28},{5,29},{6,30},{7,31},{8,16},{9,... | collective-permute-start | bytes 1572872 | tf_op jit(solution)/shard_map/ppermute | solution.py:311
  18.5 18.9 %collective-permute-start.1 = (bf16[512,128]{1,0:T(8,128)(2,1)S(1)}, bf16[512,128]{1,0:T(8,128)(2,1)S(1)}, u32[]{:S(2)}, u32[]{:S(2)}) collective-permute-start(bf16[512,128]{1,0:T(8,128)(2,1)S(1)} %get-tuple-element.58), channel_id=1, source_target_pairs={{0,32},{1,33},{2,34},{3,35},{4,36},{5,37},{6,38},{7,39},{8,40},{9,... | collective-permute-start | bytes 393224 | tf_op jit(solution)/shard_map/ppermute | solution.py:322
  30.6 9.6 %collective-permute-start.6 = (bf16[512,128]{1,0:T(8,128)(2,1)S(1)}, bf16[512,128]{1,0:T(8,128)(2,1)S(1)}, u32[]{:S(2)}, u32[]{:S(2)}) collective-permute-start(bf16[512,128]{1,0:T(8,128)(2,1)S(1)} %get-tuple-element.58), channel_id=1, source_target_pairs={{0,2},{1,3},{2,0},{3,1},{4,6},{5,7},{6,4},{7,5},{8,10},{9,11},{10,... | collective-permute-start | bytes 393224 | tf_op jit(solution)/shard_map/ppermute | solution.py:311
  35.2 15.2 %collective-permute-start.8 = (bf16[256,1024]{1,0:T(8,128)(2,1)S(1)}, bf16[256,1024]{1,0:T(8,128)(2,1)S(1)}, u32[]{:S(2)}, u32[]{:S(2)}) collective-permute-start(bf16[256,1024]{1,0:T(8,128)(2,1)S(1)} %constant_dynamic-update-slice_fusion.3.refs_3_), channel_id=1, source_target_pairs={{0,16},{1,17},{2,18},{3,19},{4,20},{5,21},{6,22},{7,23},{8,24},{9,... | collective-permute-start | bytes 1572872 | tf_op jit(solution)/shard_map/ppermute | solution.py:311
  37.5 9.4 %collective-permute-start.2 = (bf16[512,128]{1,0:T(8,128)(2,1)S(1)}, bf16[512,128]{1,0:T(8,128)(2,1)S(1)}, u32[]{:S(2)}, u32[]{:S(2)}) collective-permute-start(bf16[512,128]{1,0:T(8,128)(2,1)S(1)} %collective-permute-done.1), channel_id=1, source_target_pairs={{0,2},{1,3},{2,0},{3,1},{4,6},{5,7},{6,4},{7,5},{8,10},{9,11},{10,... | collective-permute-start | bytes 393224 | tf_op jit(solution)/shard_map/ppermute | solution.py:311
  40.2 10.2 %collective-permute-start.7 = (bf16[1024,128]{1,0:T(8,128)(2,1)S(1)}, bf16[1024,128]{1,0:T(8,128)(2,1)S(1)}, u32[]{:S(2)}, u32[]{:S(2)}) collective-permute-start(bf16[1024,128]{1,0:T(8,128)(2,1)S(1)} %constant_dynamic-update-slice_fusion.5.refs_1_), channel_id=1, source_target_pairs={{0,1},{1,0},{2,3},{3,2},{4,5},{5,4},{6,7},{7,6},{8,9},{9,8},{10,11... | collective-permute-start | bytes 786440 | tf_op jit(solution)/shard_map/ppermute | solution.py:311
  46.9 9.7 %collective-permute-start.5 = (bf16[1024,128]{1,0:T(8,128)(2,1)S(1)}, bf16[1024,128]{1,0:T(8,128)(2,1)S(1)}, u32[]{:S(2)}, u32[]{:S(2)}) collective-permute-start(bf16[1024,128]{1,0:T(8,128)(2,1)S(1)} %pad_maximum_fusion.refs_1_), channel_id=1, source_target_pairs={{0,1},{1,0},{2,3},{3,2},{4,5},{5,4},{6,7},{7,6},{8,9},{9,8},{10,11... | collective-permute-start | bytes 786440 | tf_op jit(solution)/shard_map/ppermute | solution.py:311
  49.1 0.7 copy-start.4
  49.1 0.7 copy-start.3
  82.8 10.1 %collective-permute-start.12 = (bf16[1024,128]{1,0:T(8,128)(2,1)S(1)}, bf16[1024,128]{1,0:T(8,128)(2,1)S(1)}, u32[]{:S(2)}, u32[]{:S(2)}) collective-permute-start(bf16[1024,128]{1,0:T(8,128)(2,1)S(1)} %get-tuple-element.49), channel_id=1, source_target_pairs={{0,1},{1,0},{2,3},{3,2},{4,5},{5,4},{6,7},{7,6},{8,9},{9,8},{10,11... | collective-permute-start | bytes 786440 | tf_op jit(solution)/shard_map/ppermute | solution.py:311
  84.7 13.6 %collective-permute-start.10 = (bf16[1024,128]{1,0:T(8,128)(2,1)S(1)}, bf16[1024,128]{1,0:T(8,128)(2,1)S(1)}, u32[]{:S(2)}, u32[]{:S(2)}) collective-permute-start(bf16[1024,128]{1,0:T(8,128)(2,1)S(1)} %get-tuple-element.46), channel_id=1, source_target_pairs={{0,1},{1,0},{2,3},{3,2},{4,5},{5,4},{6,7},{7,6},{8,9},{9,8},{10,11... | collective-permute-start | bytes 786440 | tf_op jit(solution)/shard_map/ppermute | solution.py:311
  88.1 23.0 %collective-permute-start.9 = (bf16[256,1024]{1,0:T(8,128)(2,1)S(1)}, bf16[256,1024]{1,0:T(8,128)(2,1)S(1)}, u32[]{:S(2)}, u32[]{:S(2)}) collective-permute-start(bf16[256,1024]{1,0:T(8,128)(2,1)S(1)} %get-tuple-element.44), channel_id=1, source_target_pairs={{0,8},{1,9},{2,10},{3,11},{4,12},{5,13},{6,14},{7,15},{8,0},{9,1},... | collective-permute-start | bytes 1572872 | tf_op jit(solution)/shard_map/ppermute | solution.py:311
  92.9 7.7 %collective-permute-start.13 = (bf16[512,128]{1,0:T(8,128)(2,1)S(1)}, bf16[512,128]{1,0:T(8,128)(2,1)S(1)}, u32[]{:S(2)}, u32[]{:S(2)}) collective-permute-start(bf16[512,128]{1,0:T(8,128)(2,1)S(1)} %add_convert_fusion.3), channel_id=1, source_target_pairs={{0,2},{1,3},{2,0},{3,1},{4,6},{5,7},{6,4},{7,5},{8,10},{9,11},{10,... | collective-permute-start | bytes 393224 | tf_op jit(solution)/shard_map/ppermute | solution.py:311
  98.3 14.8 %collective-permute-start.11 = (bf16[512,128]{1,0:T(8,128)(2,1)S(1)}, bf16[512,128]{1,0:T(8,128)(2,1)S(1)}, u32[]{:S(2)}, u32[]{:S(2)}) collective-permute-start(bf16[512,128]{1,0:T(8,128)(2,1)S(1)} %add_convert_fusion.4), channel_id=1, source_target_pairs={{0,2},{1,3},{2,0},{3,1},{4,6},{5,7},{6,4},{7,5},{8,10},{9,11},{10,... | collective-permute-start | bytes 393224 | tf_op jit(solution)/shard_map/ppermute | solution.py:311
  100.6 12.4 %collective-permute-start.14 = (bf16[512,128]{1,0:T(8,128)(2,1)S(1)}, bf16[512,128]{1,0:T(8,128)(2,1)S(1)}, u32[]{:S(2)}, u32[]{:S(2)}) collective-permute-start(bf16[512,128]{1,0:T(8,128)(2,1)S(1)} %add_convert_fusion.2), channel_id=1, source_target_pairs={{32,0},{33,1},{34,2},{35,3},{36,4},{37,5},{38,6},{39,7},{40,8},{41... | collective-permute-start | bytes 393224 | tf_op jit(solution)/shard_map/ppermute | solution.py:322
  111.1 18.2 %collective-permute-start.16 = (bf16[128,1024]{1,0:T(8,128)(2,1)S(1)}, bf16[128,1024]{1,0:T(8,128)(2,1)S(1)}, u32[]{:S(2)}, u32[]{:S(2)}) collective-permute-start(bf16[128,1024]{1,0:T(8,128)(2,1)S(1)} %add_convert_fusion.1), channel_id=1, source_target_pairs={{0,24},{1,25},{2,26},{3,27},{4,28},{5,29},{6,30},{7,31},{8,16},{9,... | collective-permute-start | bytes 786440 | tf_op jit(solution)/shard_map/ppermute | solution.py:311
  113.1 16.2 %collective-permute-start.15 = (bf16[256,128]{1,0:T(8,128)(2,1)S(1)}, bf16[256,128]{1,0:T(8,128)(2,1)S(1)}, u32[]{:S(2)}, u32[]{:S(2)}) collective-permute-start(bf16[256,128]{1,0:T(8,128)(2,1)S(1)} %add_convert_fusion.5), channel_id=1, source_target_pairs={{0,4},{1,5},{2,6},{3,7},{4,0},{5,1},{6,2},{7,3},{8,12},{9,13},{10,... | collective-permute-start | bytes 196616 | tf_op jit(solution)/shard_map/ppermute | solution.py:311

commit v7 on v6

--- a/solution.py
+++ b/solution.py
@@ -369,8 +369,8 @@
     o_far = swap(add_low(o_mid, o_near[2 * one :]), 2)
     e3 = swap(add_low(dq3, e12[BLOCK:]), 3 * NZ)
     o_four = swap(add_low(o_one, o_near[one : 2 * one], o_far[one:], back[one:]), 4)
-    o_four, e3 = lax.optimization_barrier((o_four, e3))
     grad_queries = add_low(dq0, e12[:BLOCK], e3)
+    o_four, grad_queries = lax.optimization_barrier((o_four, grad_queries))
     terms = (o_zero, o_near[:one], o_far[:one], back[:one], o_four)
     grad_keys = add_low(*[term[:BLOCK] for term in terms])
     grad_values = add_low(*[term[BLOCK:] for term in terms])

time: 132 us -> 129 us (0.977)
  the two profiles are of different devices: /device:TPU:7 before, /device:TPU:9 now
where the time goes in v7:
time: 129 us; the launch traced here: 130 us
  starting transfers between devices  74.9 us (58%)
  waiting for transfers between devices  26.1 us (20%)
  Pallas kernels  12.9 us (10%)
  blocking collectives  10.4 us (8%)
  other arithmetic  2.54 us (2%)
  local copies, waits for them, and re-layouts  1.84 us (1%)
    ppermute x15, starting transfers between devices, swap(): return lax.ppermute(array, 'inner', [(i, i ^ flip) for i in range(GROUP)])  60.6 us
    ppermute x2, waiting for transfers between devices, across(): return lax.ppermute(array, ('outer', 'inner'), pairs)  14.4 us
    ppermute x2, starting transfers between devices, across(): return lax.ppermute(array, ('outer', 'inner'), pairs)  14.2 us
    ppermute x15, waiting for transfers between devices, swap(): return lax.ppermute(array, 'inner', [(i, i ^ flip) for i in range(GROUP)])  11.7 us
    all_gather x1, blocking collectives, shards(): lax.all_gather(stats, 'inner', axis=0, tiled=True, axis_index_groups=alon...  10.4 us
    pallas_call x2, Pallas kernels, run_stats(): pl.pallas_call(functools.partial(stats_kernel, before), out_shape=outs, i...  6.67 us
    pallas_call x1, Pallas kernels, run_grads(): pl.pallas_call(grads_kernel, out_shape=outs, in_specs=[smem()] * 2 + [vme...  6.18 us
  transfers between devices with their start and end apart: 17, of which 6 were waited for; matrix products, arithmetic and copies ran while one was open for 2% of the time, Pallas kernels for 4%

profile of v7, /device:TPU:9, one launch (start us, length us, event | category | flops | bytes accessed | tf_op | source)
XLA Modules:
  0.0 129.6 jit_solution(17602592385291447143)
XLA Ops:
  0.6 0.8 pad_maximum_fusion.1
  1.4 0.0 copy-start
  1.4 8.9 %collective-permute-start = (bf16[256,128]{1,0:T(8,128)(2,1)S(1)}, bf16[256,128]{1,0:T(8,128)(2,1)S(1)}, u32[]{:S(2)}, u32[]{:S(2)}) collective-permute-start(bf16[256,128]{1,0:T(8,128)(2,1)S(1)} %pad_maximum_fusion.1), channel_id=1, source_target_pairs={{0,4},{1,5},{2,6},{3,7},{4,0},{5,1},{6,2},{7,3},{8,12},{9,13},{10,... | collective-permute-start | bytes 196616 | tf_op jit(solution)/shard_map/ppermute | solution.py:311
  10.4 1.0 constant_dynamic-update-slice_fusion.4
  11.3 0.0 copy-done
  11.3 0.0 copy-start.1
  11.4 0.0 copy-start.2
  11.4 2.1 %collective-permute-start.3 = (bf16[256,1024]{1,0:T(8,128)(2,1)S(1)}, bf16[256,1024]{1,0:T(8,128)(2,1)S(1)}, u32[]{:S(2)}, u32[]{:S(2)}) collective-permute-start(bf16[256,1024]{1,0:T(8,128)(2,1)S(1)} %constant_dynamic-update-slice_fusion.3.refs_3_), channel_id=1, source_target_pairs={{0,8},{1,9},{2,10},{3,11},{4,12},{5,13},{6,14},{7,15},{8,0},{9,1},... | collective-permute-start | bytes 1572872 | tf_op jit(solution)/shard_map/ppermute | solution.py:311
  13.5 0.0 copy-done.1
  13.5 0.0 collective-permute-done
  13.5 4.0 %collective-permute-start.4 = (bf16[256,1024]{1,0:T(8,128)(2,1)S(1)}, bf16[256,1024]{1,0:T(8,128)(2,1)S(1)}, u32[]{:S(2)}, u32[]{:S(2)}) collective-permute-start(bf16[256,1024]{1,0:T(8,128)(2,1)S(1)} %constant_dynamic-update-slice_fusion.3.refs_3_), channel_id=1, source_target_pairs={{0,24},{1,25},{2,26},{3,27},{4,28},{5,29},{6,30},{7,31},{8,16},{9,... | collective-permute-start | bytes 1572872 | tf_op jit(solution)/shard_map/ppermute | solution.py:311
  17.6 0.0 copy-done.2
  17.6 11.5 %collective-permute-start.1 = (bf16[512,128]{1,0:T(8,128)(2,1)S(1)}, bf16[512,128]{1,0:T(8,128)(2,1)S(1)}, u32[]{:S(2)}, u32[]{:S(2)}) collective-permute-start(bf16[512,128]{1,0:T(8,128)(2,1)S(1)} %get-tuple-element.58), channel_id=1, source_target_pairs={{0,32},{1,33},{2,34},{3,35},{4,36},{5,37},{6,38},{7,39},{8,40},{9,... | collective-permute-start | bytes 393224 | tf_op jit(solution)/shard_map/ppermute | solution.py:322
  29.1 4.6 %collective-permute-start.6 = (bf16[512,128]{1,0:T(8,128)(2,1)S(1)}, bf16[512,128]{1,0:T(8,128)(2,1)S(1)}, u32[]{:S(2)}, u32[]{:S(2)}) collective-permute-start(bf16[512,128]{1,0:T(8,128)(2,1)S(1)} %get-tuple-element.58), channel_id=1, source_target_pairs={{0,2},{1,3},{2,0},{3,1},{4,6},{5,7},{6,4},{7,5},{8,10},{9,11},{10,... | collective-permute-start | bytes 393224 | tf_op jit(solution)/shard_map/ppermute | solution.py:311
  33.7 2.6 %collective-permute-start.8 = (bf16[256,1024]{1,0:T(8,128)(2,1)S(1)}, bf16[256,1024]{1,0:T(8,128)(2,1)S(1)}, u32[]{:S(2)}, u32[]{:S(2)}) collective-permute-start(bf16[256,1024]{1,0:T(8,128)(2,1)S(1)} %constant_dynamic-update-slice_fusion.3.refs_3_), channel_id=1, source_target_pairs={{0,16},{1,17},{2,18},{3,19},{4,20},{5,21},{6,22},{7,23},{8,24},{9,... | collective-permute-start | bytes 1572872 | tf_op jit(solution)/shard_map/ppermute | solution.py:311
  36.3 0.0 collective-permute-done.1
  36.3 1.9 %collective-permute-start.2 = (bf16[512,128]{1,0:T(8,128)(2,1)S(1)}, bf16[512,128]{1,0:T(8,128)(2,1)S(1)}, u32[]{:S(2)}, u32[]{:S(2)}) collective-permute-start(bf16[512,128]{1,0:T(8,128)(2,1)S(1)} %collective-permute-done.1), channel_id=1, source_target_pairs={{0,2},{1,3},{2,0},{3,1},{4,6},{5,7},{6,4},{7,5},{8,10},{9,11},{10,... | collective-permute-start | bytes 393224 | tf_op jit(solution)/shard_map/ppermute | solution.py:311
  38.3 3.4 %collective-permute-done.6 = bf16[512,128]{1,0:T(8,128)(2,1)S(1)} collective-permute-done((bf16[512,128]{1,0:T(8,128)(2,1)S(1)}, bf16[512,128]{1,0:T(8,128)(2,1)S(1)}, u32[]{:S(2)}, u32[]{:S(2)}) %collective-permute-start.6) | collective-permute-done | bytes 131104 | tf_op jit(solution)/shard_map/ppermute | solution.py:311
  41.7 2.3 %collective-permute-start.7 = (bf16[1024,128]{1,0:T(8,128)(2,1)S(1)}, bf16[1024,128]{1,0:T(8,128)(2,1)S(1)}, u32[]{:S(2)}, u32[]{:S(2)}) collective-permute-start(bf16[1024,128]{1,0:T(8,128)(2,1)S(1)} %constant_dynamic-update-slice_fusion.5.refs_1_), channel_id=1, source_target_pairs={{0,1},{1,0},{2,3},{3,2},{4,5},{5,4},{6,7},{7,6},{8,9},{9,8},{10,11... | collective-permute-start | bytes 786440 | tf_op jit(solution)/shard_map/ppermute | solution.py:311
  44.0 0.0 collective-permute-done.2
  44.1 0.0 collective-permute-done.3.refs_4_
  44.1 0.0 collective-permute-done.4.refs_6_
  44.1 2.9 %collective-permute-start.5 = (bf16[1024,128]{1,0:T(8,128)(2,1)S(1)}, bf16[1024,128]{1,0:T(8,128)(2,1)S(1)}, u32[]{:S(2)}, u32[]{:S(2)}) collective-permute-start(bf16[1024,128]{1,0:T(8,128)(2,1)S(1)} %pad_maximum_fusion.refs_1_), channel_id=1, source_target_pairs={{0,1},{1,0},{2,3},{3,2},{4,5},{5,4},{6,7},{7,6},{8,9},{9,8},{10,11... | collective-permute-start | bytes 786440 | tf_op jit(solution)/shard_map/ppermute | solution.py:311
  47.0 0.0 copy-start.4
  47.1 0.0 copy-start.3
  47.1 0.7 copy-done.4
  47.7 0.0 copy-done.3
  47.7 0.1 concatenate.20.refs_0_.meta
  47.8 3.2 %collective-permute-done.7.refs_2_ = bf16[1024,128]{1,0:T(8,128)(2,1)S(1)} collective-permute-done((bf16[1024,128]{1,0:T(8,128)(2,1)S(1)}, bf16[1024,128]{1,0:T(8,128)(2,1)S(1)}, u32[]{:S(2)}, u32[]{:S(2)}) %collective-permute-start.7) | collective-permute-done | bytes 262176 | tf_op jit(solution)/shard_map/ppermute | solution.py:311
  51.0 0.0 collective-permute-done.8.refs_5_
  51.0 5.1 %shard_map.85 = (f32[16,1024]{1,0:T(8,128)S(1)}, bf16[1024,128]{1,0:T(8,128)(2,1)S(1)}, bf16[1024,128]{1,0:T(8,128)(2,1)S(1)}, s32[64]{0:T(128)S(1)}, bf16[4096,...) custom-call(s32[1026]{0:T(1024)S(1)} %concatenate.20.refs_0_.meta, ...), custom_call_target="tpu_custom_call" | custom-call | flops 671088640 | bytes 4194304 | tf_op jit(solution)/shard_map/pallas_call | solution.py:278
  56.1 0.0 collective-permute-done.5.refs_2_
  56.1 1.5 %shard_map.86 = (f32[16,1024]{1,0:T(8,128)S(1)}, bf16[2048,128]{1,0:T(8,128)(2,1)S(1)}, bf16[2048,128]{1,0:T(8,128)(2,1)S(1)}, s32[64]{0:T(128)}, s32[128]{0:T(128)S(1)}) custom-call(s32[1026]{0:T(1024)S(1)} %concatenate.20.refs_0_.meta, bf16[1024,128]{1,0:T(8,128)(2,1)S(1)} %pad_maximum_fusion.refs_1_, ...), custom_call_target="tpu_custom_call" | custom-call | flops 671088640 | bytes 4194304 | tf_op jit(solution)/shard_map/pallas_call | solution.py:278
  57.7 10.4 %all_gather.3.stats = f32[64,1024]{1,0:T(8,128)S(1)} all-gather(f32[16,1024]{1,0:T(8,128)S(1)} %get-tuple-element.42), channel_id=1, replica_groups={{0,8,16,24},{1,9,17,25},{2,10,18,26},{3,11,19,27},{4,12,20,28},{5,13,21..., dimensions={0}, use_global_device_ids=true | all-gather | bytes 327680 | tf_op jit(solution)/shard_map/all_gather | solution.py:359
  68.1 6.2 %shard_map.87 = (bf16[1024,128]{1,0:T(8,128)(2,1)S(1)}, bf16[512,128]{1,0:T(8,128)(2,1)S(1)}, bf16[512,128]{1,0:T(8,128)(2,1)S(1)}, bf16[1024,128]{1,0:T(8,128)(...) custom-call(s32[1026]{0:T(1024)S(1)} %concatenate.20.refs_0_.meta, ...), custom_call_target="tpu_custom_call" | custom-call | flops 3355443200 | bytes 4194304 | tf_op jit(solution)/shard_map/pallas_call | solution.py:291
  74.2 1.9 %collective-permute-start.11 = (bf16[1024,128]{1,0:T(8,128)(2,1)S(1)}, bf16[1024,128]{1,0:T(8,128)(2,1)S(1)}, u32[]{:S(2)}, u32[]{:S(2)}) collective-permute-start(bf16[1024,128]{1,0:T(8,128)(2,1)S(1)} %get-tuple-element.47), channel_id=1, source_target_pairs={{0,1},{1,0},{2,3},{3,2},{4,5},{5,4},{6,7},{7,6},{8,9},{9,8},{10,11... | collective-permute-start | bytes 786440 | tf_op jit(solution)/shard_map/ppermute | solution.py:311
  76.2 3.4 %collective-permute-start.9 = (bf16[1024,128]{1,0:T(8,128)(2,1)S(1)}, bf16[1024,128]{1,0:T(8,128)(2,1)S(1)}, u32[]{:S(2)}, u32[]{:S(2)}) collective-permute-start(bf16[1024,128]{1,0:T(8,128)(2,1)S(1)} %get-tuple-element.44), channel_id=1, source_target_pairs={{0,1},{1,0},{2,3},{3,2},{4,5},{5,4},{6,7},{7,6},{8,9},{9,8},{10,11... | collective-permute-start | bytes 786440 | tf_op jit(solution)/shard_map/ppermute | solution.py:311
  79.5 3.2 %collective-permute-start.15 = (bf16[256,1024]{1,0:T(8,128)(2,1)S(1)}, bf16[256,1024]{1,0:T(8,128)(2,1)S(1)}, u32[]{:S(2)}, u32[]{:S(2)}) collective-permute-start(bf16[256,1024]{1,0:T(8,128)(2,1)S(1)} %get-tuple-element.50), channel_id=1, source_target_pairs={{0,8},{1,9},{2,10},{3,11},{4,12},{5,13},{6,14},{7,15},{8,0},{9,1},... | collective-permute-start | bytes 1572872 | tf_op jit(solution)/shard_map/ppermute | solution.py:311
  82.8 0.7 collective-permute-done.11
  83.5 6.9 %collective-permute-start.12 = (bf16[512,128]{1,0:T(8,128)(2,1)S(1)}, bf16[512,128]{1,0:T(8,128)(2,1)S(1)}, u32[]{:S(2)}, u32[]{:S(2)}) collective-permute-start(bf16[512,128]{1,0:T(8,128)(2,1)S(1)} %add_convert_fusion.3), channel_id=1, source_target_pairs={{0,2},{1,3},{2,0},{3,1},{4,6},{5,7},{6,4},{7,5},{8,10},{9,11},{10,... | collective-permute-start | bytes 393224 | tf_op jit(solution)/shard_map/ppermute | solution.py:311
  90.4 0.0 collective-permute-done.9
  90.4 5.3 %collective-permute-start.10 = (bf16[512,128]{1,0:T(8,128)(2,1)S(1)}, bf16[512,128]{1,0:T(8,128)(2,1)S(1)}, u32[]{:S(2)}, u32[]{:S(2)}) collective-permute-start(bf16[512,128]{1,0:T(8,128)(2,1)S(1)} %add_convert_fusion.4), channel_id=1, source_target_pairs={{0,2},{1,3},{2,0},{3,1},{4,6},{5,7},{6,4},{7,5},{8,10},{9,11},{10,... | collective-permute-start | bytes 393224 | tf_op jit(solution)/shard_map/ppermute | solution.py:311
  95.8 1.2 collective-permute-done.12
  97.0 0.1 add_convert_fusion.2
  97.0 2.7 %collective-permute-start.13 = (bf16[512,128]{1,0:T(8,128)(2,1)S(1)}, bf16[512,128]{1,0:T(8,128)(2,1)S(1)}, u32[]{:S(2)}, u32[]{:S(2)}) collective-permute-start(bf16[512,128]{1,0:T(8,128)(2,1)S(1)} %add_convert_fusion.2), channel_id=1, source_target_pairs={{32,0},{33,1},{34,2},{35,3},{36,4},{37,5},{38,6},{39,7},{40,8},{41... | collective-permute-start | bytes 393224 | tf_op jit(solution)/shard_map/ppermute | solution.py:322
  99.8 0.0 collective-permute-done.15
  99.8 0.1 add_convert_fusion.1
  99.8 5.0 %collective-permute-start.16 = (bf16[128,1024]{1,0:T(8,128)(2,1)S(1)}, bf16[128,1024]{1,0:T(8,128)(2,1)S(1)}, u32[]{:S(2)}, u32[]{:S(2)}) collective-permute-start(bf16[128,1024]{1,0:T(8,128)(2,1)S(1)} %add_convert_fusion.1), channel_id=1, source_target_pairs={{0,24},{1,25},{2,26},{3,27},{4,28},{5,29},{6,30},{7,31},{8,16},{9,... | collective-permute-start | bytes 786440 | tf_op jit(solution)/shard_map/ppermute | solution.py:311
  104.9 0.0 collective-permute-done.10
  104.9 14.4 %collective-permute-done.13 = bf16[512,128]{1,0:T(8,128)(2,1)S(1)} collective-permute-done((bf16[512,128]{1,0:T(8,128)(2,1)S(1)}, bf16[512,128]{1,0:T(8,128)(2,1)S(1)}, u32[]{:S(2)}, u32[]{:S(2)}) %collective-permute-start.13) | collective-permute-done | bytes 131104 | tf_op jit(solution)/shard_map/ppermute | solution.py:322
  119.3 5.5 %collective-permute-start.14 = (bf16[256,128]{1,0:T(8,128)(2,1)S(1)}, bf16[256,128]{1,0:T(8,128)(2,1)S(1)}, u32[]{:S(2)}, u32[]{:S(2)}) collective-permute-start(bf16[256,128]{1,0:T(8,128)(2,1)S(1)} %add_convert_fusion.5), channel_id=1, source_target_pairs={{0,4},{1,5},{2,6},{3,7},{4,0},{5,1},{6,2},{7,3},{8,12},{9,13},{10,... | collective-permute-start | bytes 196616 | tf_op jit(solution)/shard_map/ppermute | solution.py:311
  124.8 0.0 collective-permute-done.16
  124.8 0.8 add_convert_fusion
  125.7 3.3 %collective-permute-done.14 = bf16[256,128]{1,0:T(8,128)(2,1)S(1)} collective-permute-done((bf16[256,128]{1,0:T(8,128)(2,1)S(1)}, bf16[256,128]{1,0:T(8,128)(2,1)S(1)}, u32[]{:S(2)}, u32[]{:S(2)}) %collective-permute-start.14) | collective-permute-done | bytes 65568 | tf_op jit(solution)/shard_map/ppermute | solution.py:311
  128.9 0.7 add_convert_fusion.6
  (9 shorter events, 0.2 us)
Async XLA Ops:
  1.4 9.9 %copy-start = (bf16[128,1024]{1,0:T(8,128)(2,1)S(1)}, bf16[128,1024]{1,0:T(8,128)(2,1)}, u32[]{:S(2)}) copy-start(bf16[128,1024]{1,0:T(8,128)(2,1)} %param.9) | copy-start | bytes 786436
  1.4 12.1 %collective-permute-start = (bf16[256,128]{1,0:T(8,128)(2,1)S(1)}, bf16[256,128]{1,0:T(8,128)(2,1)S(1)}, u32[]{:S(2)}, u32[]{:S(2)}) collective-permute-start(bf16[256,128]{1,0:T(8,128)(2,1)S(1)} %pad_maximum_fusion.1), channel_id=1, source_target_pairs={{0,4},{1,5},{2,6},{3,7},{4,0},{5,1},{6,2},{7,3},{8,12},{9,13},{10,... | collective-permute-start | bytes 196616 | tf_op jit(solution)/shard_map/ppermute | solution.py:311
  11.3 2.1 %copy-start.1 = (bf16[128,128]{1,0:T(8,128)(2,1)S(1)}, bf16[128,128]{1,0:T(8,128)(2,1)}, u32[]{:S(2)}) copy-start(bf16[128,128]{1,0:T(8,128)(2,1)} %param.7) | copy-start | bytes 98308
  11.4 6.2 %copy-start.2 = (bf16[128,128]{1,0:T(8,128)(2,1)S(1)}, bf16[128,128]{1,0:T(8,128)(2,1)}, u32[]{:S(2)}) copy-start(bf16[128,128]{1,0:T(8,128)(2,1)} %param.8) | copy-start | bytes 98308
  11.4 32.7 %collective-permute-start.3 = (bf16[256,1024]{1,0:T(8,128)(2,1)S(1)}, bf16[256,1024]{1,0:T(8,128)(2,1)S(1)}, u32[]{:S(2)}, u32[]{:S(2)}) collective-permute-start(bf16[256,1024]{1,0:T(8,128)(2,1)S(1)} %constant_dynamic-update-slice_fusion.3.refs_3_), channel_id=1, source_target_pairs={{0,8},{1,9},{2,10},{3,11},{4,12},{5,13},{6,14},{7,15},{8,0},{9,1},... | collective-permute-start | bytes 1572872 | tf_op jit(solution)/shard_map/ppermute | solution.py:311
  13.5 30.6 %collective-permute-start.4 = (bf16[256,1024]{1,0:T(8,128)(2,1)S(1)}, bf16[256,1024]{1,0:T(8,128)(2,1)S(1)}, u32[]{:S(2)}, u32[]{:S(2)}) collective-permute-start(bf16[256,1024]{1,0:T(8,128)(2,1)S(1)} %constant_dynamic-update-slice_fusion.3.refs_3_), channel_id=1, source_target_pairs={{0,24},{1,25},{2,26},{3,27},{4,28},{5,29},{6,30},{7,31},{8,16},{9,... | collective-permute-start | bytes 1572872 | tf_op jit(solution)/shard_map/ppermute | solution.py:311
  17.6 18.7 %collective-permute-start.1 = (bf16[512,128]{1,0:T(8,128)(2,1)S(1)}, bf16[512,128]{1,0:T(8,128)(2,1)S(1)}, u32[]{:S(2)}, u32[]{:S(2)}) collective-permute-start(bf16[512,128]{1,0:T(8,128)(2,1)S(1)} %get-tuple-element.58), channel_id=1, source_target_pairs={{0,32},{1,33},{2,34},{3,35},{4,36},{5,37},{6,38},{7,39},{8,40},{9,... | collective-permute-start | bytes 393224 | tf_op jit(solution)/shard_map/ppermute | solution.py:322
  29.1 12.5 %collective-permute-start.6 = (bf16[512,128]{1,0:T(8,128)(2,1)S(1)}, bf16[512,128]{1,0:T(8,128)(2,1)S(1)}, u32[]{:S(2)}, u32[]{:S(2)}) collective-permute-start(bf16[512,128]{1,0:T(8,128)(2,1)S(1)} %get-tuple-element.58), channel_id=1, source_target_pairs={{0,2},{1,3},{2,0},{3,1},{4,6},{5,7},{6,4},{7,5},{8,10},{9,11},{10,... | collective-permute-start | bytes 393224 | tf_op jit(solution)/shard_map/ppermute | solution.py:311
  33.7 17.2 %collective-permute-start.8 = (bf16[256,1024]{1,0:T(8,128)(2,1)S(1)}, bf16[256,1024]{1,0:T(8,128)(2,1)S(1)}, u32[]{:S(2)}, u32[]{:S(2)}) collective-permute-start(bf16[256,1024]{1,0:T(8,128)(2,1)S(1)} %constant_dynamic-update-slice_fusion.3.refs_3_), channel_id=1, source_target_pairs={{0,16},{1,17},{2,18},{3,19},{4,20},{5,21},{6,22},{7,23},{8,24},{9,... | collective-permute-start | bytes 1572872 | tf_op jit(solution)/shard_map/ppermute | solution.py:311
  36.3 7.7 %collective-permute-start.2 = (bf16[512,128]{1,0:T(8,128)(2,1)S(1)}, bf16[512,128]{1,0:T(8,128)(2,1)S(1)}, u32[]{:S(2)}, u32[]{:S(2)}) collective-permute-start(bf16[512,128]{1,0:T(8,128)(2,1)S(1)} %collective-permute-done.1), channel_id=1, source_target_pairs={{0,2},{1,3},{2,0},{3,1},{4,6},{5,7},{6,4},{7,5},{8,10},{9,11},{10,... | collective-permute-start | bytes 393224 | tf_op jit(solution)/shard_map/ppermute | solution.py:311
  41.7 9.3 %collective-permute-start.7 = (bf16[1024,128]{1,0:T(8,128)(2,1)S(1)}, bf16[1024,128]{1,0:T(8,128)(2,1)S(1)}, u32[]{:S(2)}, u32[]{:S(2)}) collective-permute-start(bf16[1024,128]{1,0:T(8,128)(2,1)S(1)} %constant_dynamic-update-slice_fusion.5.refs_1_), channel_id=1, source_target_pairs={{0,1},{1,0},{2,3},{3,2},{4,5},{5,4},{6,7},{7,6},{8,9},{9,8},{10,11... | collective-permute-start | bytes 786440 | tf_op jit(solution)/shard_map/ppermute | solution.py:311
  44.1 12.0 %collective-permute-start.5 = (bf16[1024,128]{1,0:T(8,128)(2,1)S(1)}, bf16[1024,128]{1,0:T(8,128)(2,1)S(1)}, u32[]{:S(2)}, u32[]{:S(2)}) collective-permute-start(bf16[1024,128]{1,0:T(8,128)(2,1)S(1)} %pad_maximum_fusion.refs_1_), channel_id=1, source_target_pairs={{0,1},{1,0},{2,3},{3,2},{4,5},{5,4},{6,7},{7,6},{8,9},{9,8},{10,11... | collective-permute-start | bytes 786440 | tf_op jit(solution)/shard_map/ppermute | solution.py:311
  47.0 0.7 copy-start.4
  47.1 0.7 copy-start.3
  74.2 9.2 %collective-permute-start.11 = (bf16[1024,128]{1,0:T(8,128)(2,1)S(1)}, bf16[1024,128]{1,0:T(8,128)(2,1)S(1)}, u32[]{:S(2)}, u32[]{:S(2)}) collective-permute-start(bf16[1024,128]{1,0:T(8,128)(2,1)S(1)} %get-tuple-element.47), channel_id=1, source_target_pairs={{0,1},{1,0},{2,3},{3,2},{4,5},{5,4},{6,7},{7,6},{8,9},{9,8},{10,11... | collective-permute-start | bytes 786440 | tf_op jit(solution)/shard_map/ppermute | solution.py:311
  76.2 14.2 %collective-permute-start.9 = (bf16[1024,128]{1,0:T(8,128)(2,1)S(1)}, bf16[1024,128]{1,0:T(8,128)(2,1)S(1)}, u32[]{:S(2)}, u32[]{:S(2)}) collective-permute-start(bf16[1024,128]{1,0:T(8,128)(2,1)S(1)} %get-tuple-element.44), channel_id=1, source_target_pairs={{0,1},{1,0},{2,3},{3,2},{4,5},{5,4},{6,7},{7,6},{8,9},{9,8},{10,11... | collective-permute-start | bytes 786440 | tf_op jit(solution)/shard_map/ppermute | solution.py:311
  79.5 20.2 %collective-permute-start.15 = (bf16[256,1024]{1,0:T(8,128)(2,1)S(1)}, bf16[256,1024]{1,0:T(8,128)(2,1)S(1)}, u32[]{:S(2)}, u32[]{:S(2)}) collective-permute-start(bf16[256,1024]{1,0:T(8,128)(2,1)S(1)} %get-tuple-element.50), channel_id=1, source_target_pairs={{0,8},{1,9},{2,10},{3,11},{4,12},{5,13},{6,14},{7,15},{8,0},{9,1},... | collective-permute-start | bytes 1572872 | tf_op jit(solution)/shard_map/ppermute | solution.py:311
  83.5 13.5 %collective-permute-start.12 = (bf16[512,128]{1,0:T(8,128)(2,1)S(1)}, bf16[512,128]{1,0:T(8,128)(2,1)S(1)}, u32[]{:S(2)}, u32[]{:S(2)}) collective-permute-start(bf16[512,128]{1,0:T(8,128)(2,1)S(1)} %add_convert_fusion.3), channel_id=1, source_target_pairs={{0,2},{1,3},{2,0},{3,1},{4,6},{5,7},{6,4},{7,5},{8,10},{9,11},{10,... | collective-permute-start | bytes 393224 | tf_op jit(solution)/shard_map/ppermute | solution.py:311
  90.4 14.4 %collective-permute-start.10 = (bf16[512,128]{1,0:T(8,128)(2,1)S(1)}, bf16[512,128]{1,0:T(8,128)(2,1)S(1)}, u32[]{:S(2)}, u32[]{:S(2)}) collective-permute-start(bf16[512,128]{1,0:T(8,128)(2,1)S(1)} %add_convert_fusion.4), channel_id=1, source_target_pairs={{0,2},{1,3},{2,0},{3,1},{4,6},{5,7},{6,4},{7,5},{8,10},{9,11},{10,... | collective-permute-start | bytes 393224 | tf_op jit(solution)/shard_map/ppermute | solution.py:311
  97.0 22.2 %collective-permute-start.13 = (bf16[512,128]{1,0:T(8,128)(2,1)S(1)}, bf16[512,128]{1,0:T(8,128)(2,1)S(1)}, u32[]{:S(2)}, u32[]{:S(2)}) collective-permute-start(bf16[512,128]{1,0:T(8,128)(2,1)S(1)} %add_convert_fusion.2), channel_id=1, source_target_pairs={{32,0},{33,1},{34,2},{35,3},{36,4},{37,5},{38,6},{39,7},{40,8},{41... | collective-permute-start | bytes 393224 | tf_op jit(solution)/shard_map/ppermute | solution.py:322
  99.8 25.0 %collective-permute-start.16 = (bf16[128,1024]{1,0:T(8,128)(2,1)S(1)}, bf16[128,1024]{1,0:T(8,128)(2,1)S(1)}, u32[]{:S(2)}, u32[]{:S(2)}) collective-permute-start(bf16[128,1024]{1,0:T(8,128)(2,1)S(1)} %add_convert_fusion.1), channel_id=1, source_target_pairs={{0,24},{1,25},{2,26},{3,27},{4,28},{5,29},{6,30},{7,31},{8,16},{9,... | collective-permute-start | bytes 786440 | tf_op jit(solution)/shard_map/ppermute | solution.py:311
  119.3 9.6 %collective-permute-start.14 = (bf16[256,128]{1,0:T(8,128)(2,1)S(1)}, bf16[256,128]{1,0:T(8,128)(2,1)S(1)}, u32[]{:S(2)}, u32[]{:S(2)}) collective-permute-start(bf16[256,128]{1,0:T(8,128)(2,1)S(1)} %add_convert_fusion.5), channel_id=1, source_target_pairs={{0,4},{1,5},{2,6},{3,7},{4,0},{5,1},{6,2},{7,3},{8,12},{9,13},{10,... | collective-permute-start | bytes 196616 | tf_op jit(solution)/shard_map/ppermute | solution.py:311
